TPU v7x, 256 devices: a whole 4x4x8 slice. The times are simulated.
256 devices in a mesh: gx: 32 (over x, z), gy: 8 (over y, core).
Axes of the slice: x: 4, y: 4, z: 8, core: 2. Of those that a mesh axis runs over, the one named last changes fastest.
Arguments:
- classes: int32 [8192, 16384], P('gy', 'gx'), may hold values from 0 to 7
- exponents: int32 [64, 128], P('gy', 'gx'), may hold values from -1 to 1
- gain_field: bfloat16 [8192, 16384], P('gy', 'gx'), may hold values from 0.5 to 2
- level_table: float32 [8], replicated, may hold values from 0.3 to 1.2
- level_weights: float32 [3], replicated, may hold values from 0.2 to 0.8
Outputs:
- new_dose: float32 [8192, 16384], P('gy', 'gx')
All inputs are finite; a program needn't handle non-finite values.
Results may differ from a plain program's by a relative error of at most 0.0003.
The roundings to bfloat16 on the way count: a program that leaves them out, or rounds other values in their place, can miss the bound.
Values may be sent and summed in bfloat16 or wider, within the bound.
No kernel may reach another device: no remote copies, remote signals or barrier semaphores. Data moves between devices by JAX's collectives and lax.ppermute only.
A program may use at most 64 MiB of HBM per device.

v0:
```python
import functools

import jax
import jax.numpy as jnp
import ml_dtypes
import numpy as np
from jax import lax
from jax.experimental import pallas as pl
from jax.experimental.pallas import tpu as pltpu
from jax.sharding import PartitionSpec as P

HW = 4
CLASSES = 8
SB = 128
ITERS = 4
NX, NY = 32, 8
TR, TC = 1024, 512
HALO = HW * ITERS
ER = TR + 2 * HALO
EC = TC + 128
BLK = 176
NB = ER // BLK
QC, QR = 36, 68
F32, BF16 = jnp.float32, jnp.bfloat16
EXACT = lax.Precision.HIGHEST


def gauss_taps():
    offsets = np.arange(-HW, HW + 1).astype(np.float32)
    weights = np.exp(-(offsets * offsets) / np.float32(HW * HW)).astype(np.float32)
    return weights / weights.sum(dtype=np.float32)


def blur_operator(n):
    taps = gauss_taps().astype(np.float64)
    out = np.zeros((n, n))
    for k in range(-HW, HW + 1):
        out += taps[k + HW] * np.eye(n, k=k)
    return out


def up_operator(n, factor):
    target = np.arange(n * factor)
    lower = (target - factor // 2) // factor
    t = (target - factor // 2 - factor * lower + 0.5) / factor
    out = np.zeros((n * factor, n))
    np.add.at(out, (target, np.clip(lower, 0, n - 1)), 1 - t)
    np.add.at(out, (target, np.clip(lower + 1, 0, n - 1)), t)
    return out


def level_operators(n_second):
    third, fourth = n_second // 4, n_second // 16
    return (
        blur_operator(n_second),
        up_operator(third, 4) @ blur_operator(third),
        up_operator(third, 4) @ up_operator(fourth, 4) @ blur_operator(fourth),
    )


@functools.cache
def column_matrices():
    second, third, fourth = level_operators(NX * 32)
    got = np.zeros((NX, 128, 256), np.float32)
    own = np.zeros((NX, 128, 32), np.float32)
    for px in range(NX):
        for q in range(QC):
            g = min(max(32 * px + q - 2, 0), NX * 32 - 1)
            for s in np.nonzero(second[g])[0]:
                p, j = divmod(int(s), 32)
                if p == px:
                    own[px, q, j] = second[g, s]
                else:
                    assert j >= 24 if p < px else j < 8
                    got[px, q, p * 8 + j % 8] = second[g, s]
            got[px, 40 + q] = third[g]
            for j in range(2):
                got[px, 80 + q, j::8] = fourth[g, j::2]
        got[px, 120, 0::8] = 1
        got[px, 120, 1::8] = 1
    return got, own


def row_matrices(groups, first, step, length):
    second, third, fourth = level_operators(NY * 64)
    m = 16 * groups
    out = np.zeros((NY, 3 * m + 8, 192), np.float32)
    for py in range(NY):
        for b in range(groups):
            for k in range(length):
                row, q = b * 16 + k, first + step * b + k
                g = min(max(64 * py + q - 2, 0), NY * 64 - 1)
                for s in np.nonzero(second[g])[0]:
                    p, j = divmod(int(s), 64)
                    assert p == py or (j >= 56 if p < py else j < 8)
                    out[py, row, 64 + j if p == py else p * 8 + j % 8] = second[g, s]
                for s in np.nonzero(third[g])[0]:
                    p, j = divmod(int(s), 16)
                    assert p == py or (j >= 8 if p < py else j < 8)
                    out[py, m + row, 128 + j if p == py else p * 8 + j % 8] = third[g, s]
                for s in np.nonzero(fourth[g])[0]:
                    p, j = divmod(int(s), 4)
                    out[py, 2 * m + row, p * 8 + j] = fourth[g, s]
        out[py, 3 * m, 4:64:8] = 1
    return out


@functools.cache
def column_spread():
    out = np.zeros((128, EC), np.float32)
    for lane in range(EC):
        cell = lane if lane < TC + HALO else lane - EC
        if cell < -HALO:
            continue
        lower = (cell - 8) // 16
        t = (cell - 8 - 16 * lower + 0.5) / 16
        for level in range(3):
            out[40 * level + lower + 2, lane] += 1 - t
            out[40 * level + lower + 3, lane] += t
        out[120, lane] = 1
    return out


@functools.cache
def column_pool(lanes):
    out = np.zeros((lanes, 128), np.float32)
    cell = np.arange(TC)
    out[cell, cell // 16] = 1
    out[cell, 32 + cell // 64] = 1
    out[cell, 40 + cell // 256] = 1
    return out.astype(ml_dtypes.bfloat16)


@functools.cache
def row_pool(groups, stride, real, first):
    out = np.zeros((128, groups * stride), np.float32)
    for b in range(groups):
        for k in range(real):
            s = b * real + k - first
            if 0 <= s < TR // 16:
                at = b * stride + k
                out[s, at] = 2.0**-8
                out[64 + s // 4, at] = 2.0**-12
                out[80 + s // 16, at] = 2.0**-16
                out[84, at] = 1.0 / (TR * NY * TC * NX)
    return out


def fine_taps():
    return gauss_taps().astype(ml_dtypes.bfloat16)


@functools.cache
def fine_columns():
    out = np.zeros((EC, EC), ml_dtypes.bfloat16)
    taps, lane = fine_taps(), np.arange(EC)
    for k in range(-HW, HW + 1):
        out[(lane + k) % EC, lane] = taps[k + HW]
    return out


@functools.cache
def fine_rows():
    out = np.zeros((3, BLK, BLK + 32), ml_dtypes.bfloat16)
    taps = fine_taps()
    for which in range(3):
        for r in range(BLK):
            for k in range(-HW, HW + 1):
                c = r + 16 * which + k
                if 0 <= c < BLK + 32:
                    out[which, r, c] = taps[k + HW]
    return out


def params(mib=24):
    return pltpu.CompilerParams(vmem_limit_bytes=mib * 2**20)


def dot(a, b, **kw):
    return jnp.dot(a, b, preferred_element_type=F32, **kw)


def pooled_out(sums, row_pool_ref, px, send_ref, own_ref):
    pooled = dot(row_pool_ref[...], sums, precision=EXACT).T
    own_ref[...] = pooled
    lane = lax.broadcasted_iota(jnp.int32, (8, 128), 1)
    coarse = jnp.where(lane < 80, pooled[32:40], pooled[40:48])
    left = jnp.where(lane < 64, pooled[0:8], coarse)
    right = jnp.where(lane < 64, pooled[24:32], coarse)
    for p in range(NX):
        send_ref[p] = jnp.where(p < px, left, right)


def start_kernel(place, table, exps, classes, gain, cpool, rpool, dose, lo, hi, send, own, sums):
    i = pl.program_id(0)
    for n in range(TC // SB):
        e = exps[i, n]
        scale = jnp.where(e > 0, 2.0, jnp.where(e < 0, 0.5, 1.0)).astype(F32)
        at = slice(n * SB, (n + 1) * SB)
        c = classes[:, at]
        level = jnp.zeros((SB, SB), F32)
        for k in range(1, CLASSES):
            level = jnp.where(c == k, table[k] * scale, level)
        value = (level * gain[:, at].astype(F32)).astype(BF16)
        dose[:, at] = value
        if n == 0:
            lo[...] = value.astype(F32).T[:HALO].astype(BF16)
        if n == TC // SB - 1:
            hi[...] = value.astype(F32).T[SB - HALO :].astype(BF16)
    across = dot(dose[...], cpool[...])
    sums[i] = jnp.sum(across.reshape(8, 16, 128), axis=1)

    @pl.when(i == TR // SB - 1)
    def _():
        pooled_out(sums[...].reshape(64, 128), rpool, place[0], send, own)


def start(place, table, exps, classes, gain):
    steps = TR // SB
    whole = lambda *shape: pl.BlockSpec(shape, lambda i, s: (0,) * len(shape))
    strip = pl.BlockSpec((HALO, SB), lambda i, s: (0, i))
    return pl.pallas_call(
        start_kernel,
        grid_spec=pltpu.PrefetchScalarGridSpec(
            num_scalar_prefetch=1,
            grid=(steps,),
            in_specs=[
                pl.BlockSpec(memory_space=pltpu.SMEM),
                pl.BlockSpec(memory_space=pltpu.SMEM),
                pl.BlockSpec((SB, TC), lambda i, s: (i, 0)),
                pl.BlockSpec((SB, TC), lambda i, s: (i, 0)),
                whole(TC, 128),
                whole(128, 64),
            ],
            out_specs=[
                pl.BlockSpec((SB, TC), lambda i, s: (i, 0)),
                strip,
                strip,
                whole(NX, 8, 128),
                whole(128, 128),
            ],
            scratch_shapes=[pltpu.VMEM((steps, 8, 128), F32)],
        ),
        out_shape=[
            jax.ShapeDtypeStruct((TR, TC), BF16),
            jax.ShapeDtypeStruct((HALO, TR), BF16),
            jax.ShapeDtypeStruct((HALO, TR), BF16),
            jax.ShapeDtypeStruct((NX, 8, 128), F32),
            jax.ShapeDtypeStruct((128, 128), F32),
        ],
        compiler_params=params(),
        name="start",
    )(place, table, exps, classes, gain, column_pool(TC), row_pool(8, 8, 8, 0))


def across_kernel(place, got, own, mgot, mown, send, part):
    z = dot(mgot[0], got[...], precision=EXACT) + dot(mown[0], own[:32], precision=EXACT)
    z = z.T
    part[...] = z
    lane = lax.broadcasted_iota(jnp.int32, (8, 128), 1)
    coarse = z[80:88]
    up = jnp.where(lane < 40, z[0:8], jnp.where(lane < 80, z[64:72], coarse))
    down = jnp.where(lane < 40, z[56:64], jnp.where(lane < 80, z[72:80], coarse))
    for p in range(NY):
        send[p] = jnp.where(p < place[1], up, down)


def across(place, got, own):
    mgot, mown = column_matrices()
    whole = lambda *shape: pl.BlockSpec(shape, lambda i, s: (0,) * len(shape))
    mine = lambda *shape: pl.BlockSpec((1, *shape), lambda i, s: (s[0],) + (0,) * len(shape))
    return pl.pallas_call(
        across_kernel,
        grid_spec=pltpu.PrefetchScalarGridSpec(
            num_scalar_prefetch=1,
            grid=(1,),
            in_specs=[whole(256, 128), whole(128, 128), mine(128, 256), mine(128, 32)],
            out_specs=[whole(NY, 8, 128), whole(128, 128)],
        ),
        out_shape=[
            jax.ShapeDtypeStruct((NY, 8, 128), F32),
            jax.ShapeDtypeStruct((128, 128), F32),
        ],
        compiler_params=params(),
        name="across",
    )(place, got.reshape(NX * 8, 128), own, mgot, mown)


def side(strip_lo, strip_hi):
    rows = strip_lo.shape[1]
    empty = jnp.zeros((rows, 128 - 2 * HALO), F32)
    return jnp.concatenate([strip_hi.astype(F32).T, empty, strip_lo.astype(F32).T], axis=1).astype(BF16)


def edges_kernel(dose_top, dose_bottom, lo_top, hi_top, lo_bottom, hi_bottom, top, bottom):
    top[:, :TC] = dose_top[...]
    top[:, TC:] = side(lo_top[...], hi_top[...])[:HALO]
    bottom[:, :TC] = dose_bottom[...]
    bottom[:, TC:] = side(lo_bottom[...], hi_bottom[...])[128 - HALO :]


def edges(dose, lo, hi):
    first, last = TR // HALO - 1, TR // 128 - 1
    return pl.pallas_call(
        edges_kernel,
        grid=(1,),
        in_specs=[
            pl.BlockSpec((HALO, TC), lambda i: (0, 0)),
            pl.BlockSpec((HALO, TC), lambda i: (first, 0)),
            pl.BlockSpec((HALO, 128), lambda i: (0, 0)),
            pl.BlockSpec((HALO, 128), lambda i: (0, 0)),
            pl.BlockSpec((HALO, 128), lambda i: (0, last)),
            pl.BlockSpec((HALO, 128), lambda i: (0, last)),
        ],
        out_specs=[pl.BlockSpec((HALO, EC), lambda i: (0, 0))] * 2,
        out_shape=[jax.ShapeDtypeStruct((HALO, EC), BF16)] * 2,
        compiler_params=params(),
        name="edges",
    )(dose, dose, lo, hi, lo, hi)


def assemble_kernel(dose, lo, hi, above, below, out):
    out[:HALO] = above[...]
    out[HALO + TR :] = below[...]
    out[HALO : HALO + TR, :TC] = dose[...]
    for n in range(TR // 128):
        at = slice(n * 128, (n + 1) * 128)
        out[HALO + n * 128 : HALO + (n + 1) * 128, TC:] = side(lo[:, at], hi[:, at])


def assemble(dose, lo, hi, above, below):
    return pl.pallas_call(
        assemble_kernel,
        out_shape=jax.ShapeDtypeStruct((ER, EC), BF16),
        compiler_params=params(),
        name="assemble",
    )(dose, lo, hi, above, below)


def fine_kernel(last, dose, cols, rows, *refs):
    out, half = refs[0], refs[-1]
    for b in range(NB):
        at = slice(b * BLK, (b + 1) * BLK)
        half[at] = dot(dose[at], cols[...]).astype(BF16)
    for b in range(NB):
        first = min(max(b * BLK - 16, 0), ER - BLK - 32)
        which = (b * BLK - first) // 16
        values = half[first : first + BLK + 32]
        if last:
            got = dot(rows[which], values[:, :TC])
            begin, end = max(b * BLK, HALO), min((b + 1) * BLK, HALO + TR)
            out[begin - HALO : end - HALO] = got[begin - b * BLK : end - b * BLK]
        else:
            out[b * BLK : (b + 1) * BLK] = dot(rows[which], values)
    if last:
        refs[1][...] = dose[HALO : HALO + TR, :TC]


def fine(dose, last):
    if last:
        shapes = [jax.ShapeDtypeStruct((TR, TC), F32), jax.ShapeDtypeStruct((TR, TC), BF16)]
    else:
        shapes = [jax.ShapeDtypeStruct((ER, EC), F32)]
    return pl.pallas_call(
        functools.partial(fine_kernel, last),
        out_shape=shapes,
        scratch_shapes=[pltpu.VMEM((ER, EC), BF16)],
        compiler_params=params(),
        cost_estimate=pl.CostEstimate(flops=2 * ER * EC * (EC + 208), bytes_accessed=6 * ER * EC, transcendentals=0),
        name="fine",
    )(dose, fine_columns(), fine_rows())


def spread(weights, got, part, matrix, cols, grid, groups):
    m = 16 * groups
    stacked = jnp.concatenate([got[...], part[...]], axis=0)
    y = dot(matrix[0], stacked, precision=EXACT)
    lane = lax.broadcasted_iota(jnp.int32, (m, 128), 1)
    fourth = jnp.where(lane < 120, y[2 * m : 3 * m], jnp.where(lane == 120, y[3 * m : 3 * m + 1], 0.0))
    terms = jnp.where(
        lane < 40,
        weights[0] * y[:m],
        jnp.where(lane < 80, weights[1] * y[m : 2 * m], weights[2] * fourth),
    )
    grid[...] = dot(terms, cols[...], precision=EXACT).reshape(grid.shape)


def update(b, rows, dose, short, grid, out):
    lanes = dose.shape[1]
    t = (lax.broadcasted_iota(jnp.int32, (8, lanes), 0).astype(F32) + 0.5) / 16.0
    for n in range(rows // 16):
        at = slice(16 * n, 16 * n + 16)
        a, m, c = (grid[b, n + k : n + k + 1] for k in range(3))
        back = jnp.concatenate([a + (t + 0.5) * (m - a), m + t * (c - m)], axis=0)
        out[at] = (dose[at].astype(F32) * 2.0 / (1.0 + (short[at] + back))).astype(out.dtype)


def step_kernel(place, weights, got, part, matrix, cols, dose, short, cpool, rpool, out, send, own, grid, sums):
    b = pl.program_id(0)

    @pl.when(b == 0)
    def _():
        spread(weights, got, part, matrix, cols, grid, NB)

    update(b, BLK, dose, short, grid, out)
    pooled = dot(out[...], cpool[...])
    pooled = jnp.sum(pooled.reshape(BLK // 16, 16, 128), axis=1)
    sums[b] = jnp.concatenate([pooled, jnp.zeros((16 - BLK // 16, 128), F32)], axis=0)

    @pl.when(b == NB - 1)
    def _():
        pooled_out(sums[...].reshape(NB * 16, 128), rpool, place[0], send, own)


def step(place, weights, got, part, dose, short):
    whole = lambda *shape: pl.BlockSpec(shape, lambda i, s: (0,) * len(shape))
    block = pl.BlockSpec((BLK, EC), lambda i, s: (i, 0))
    m = 3 * 16 * NB + 8
    return pl.pallas_call(
        step_kernel,
        grid_spec=pltpu.PrefetchScalarGridSpec(
            num_scalar_prefetch=1,
            grid=(NB,),
            in_specs=[
                pl.BlockSpec(memory_space=pltpu.SMEM),
                whole(NY * 8, 128),
                whole(128, 128),
                pl.BlockSpec((1, m, 192), lambda i, s: (s[1], 0, 0)),
                whole(128, EC),
                block,
                block,
                whole(EC, 128),
                whole(128, NB * 16),
            ],
            out_specs=[block, whole(NX, 8, 128), whole(128, 128)],
            scratch_shapes=[pltpu.VMEM((NB, 16, EC), F32), pltpu.VMEM((NB, 16, 128), F32)],
        ),
        out_shape=[
            jax.ShapeDtypeStruct((ER, EC), BF16),
            jax.ShapeDtypeStruct((NX, 8, 128), F32),
            jax.ShapeDtypeStruct((128, 128), F32),
        ],
        compiler_params=params(),
        name="step",
    )(
        place, weights, got.reshape(NY * 8, 128), part, row_matrices(NB, 0, BLK // 16, BLK // 16 + 2),
        column_spread(), dose, short, column_pool(EC), row_pool(NB, 16, BLK // 16, 1),
    )


def finish_kernel(place, weights, got, part, matrix, cols, dose, short, out, grid):
    b = pl.program_id(0)

    @pl.when(b == 0)
    def _():
        spread(weights, got, part, matrix, cols, grid, TR // SB)

    update(b, SB, dose, short, grid, out)


def finish(place, weights, got, part, dose, short):
    whole = lambda *shape: pl.BlockSpec(shape, lambda i, s: (0,) * len(shape))
    block = pl.BlockSpec((SB, TC), lambda i, s: (i, 0))
    groups = TR // SB
    return pl.pallas_call(
        finish_kernel,
        grid_spec=pltpu.PrefetchScalarGridSpec(
            num_scalar_prefetch=1,
            grid=(groups,),
            in_specs=[
                pl.BlockSpec(memory_space=pltpu.SMEM),
                whole(NY * 8, 128),
                whole(128, 128),
                pl.BlockSpec((1, 3 * 16 * groups + 8, 192), lambda i, s: (s[1], 0, 0)),
                whole(128, TC),
                block,
                block,
            ],
            out_specs=block,
            scratch_shapes=[pltpu.VMEM((groups, 16, TC), F32)],
        ),
        out_shape=jax.ShapeDtypeStruct((TR, TC), F32),
        compiler_params=params(),
        name="finish",
    )(
        place, weights, got.reshape(NY * 8, 128), part, row_matrices(groups, 1, SB // 16, SB // 16 + 2),
        column_spread()[:, :TC], dose, short,
    )


def shifted(x, axis, by):
    n = lax.axis_size(axis)
    return lax.ppermute(x, axis, [(i, i + by) for i in range(n) if 0 <= i + by < n])


def exchanged(x, axis):
    return lax.all_to_all(x, axis, 0, 0, tiled=True)


def local(classes, exponents, gain_field, level_table, level_weights):
    place = jnp.stack([lax.axis_index("gx"), lax.axis_index("gy")]).astype(jnp.int32)
    tile, lo, hi, send, own = start(place, level_table, exponents, classes, gain_field)
    left, right = shifted(hi, "gx", 1), shifted(lo, "gx", -1)
    got = exchanged(send, "gx")
    top, bottom = edges(tile, left, right)
    above, below = shifted(bottom, "gy", 1), shifted(top, "gy", -1)
    send, part = across(place, got, own)
    got = exchanged(send, "gy")
    dose = assemble(tile, left, right, above, below)
    (short,) = fine(dose, False)
    for sweep in range(1, ITERS):
        dose, send, own = step(place, level_weights, got, part, dose, short)
        got = exchanged(send, "gx")
        last = sweep == ITERS - 1
        blurred = fine(dose, last)
        short = blurred[0]
        if last:
            dose = blurred[1]
        send, part = across(place, got, own)
        got = exchanged(send, "gy")
    return finish(place, level_weights, got, part, dose, short)


def solution(mesh):
    in_specs = (P("gy", "gx"), P("gy", "gx"), P("gy", "gx"), P(), P())
    return jax.shard_map(local, mesh=mesh, in_specs=in_specs, out_specs=P("gy", "gx"), check_vma=False)
```

profile of v0, /device:TPU:1, one launch (start us, length us, event | category | flops | bytes accessed | tf_op | source)
XLA Modules:
  0.0 184.9 jit_solution(1879845467818908228)
XLA Ops:
  6.0 4.8 %start.1 = (bf16[1024,512]{1,0:T(8,128)(2,1)S(1)}, bf16[16,1024]{1,0:T(8,128)(2,1)S(1)}, bf16[16,1024]{1,0:T(8,128)(2,1)S(1)}, f32[32,8,128]{2,1,0:T(8,128)}, f32[128,128]{1,0:T(8,128)S(1)}) custom-call(s32[2]{0:T(128)S(1)} %pad_add_fusion.place, f32[8]{0:T(128)S(1)} %copy-done.53, s32[8,4]{1,0:T(8,128)S(1)} %copy.20.exps, s32[1024,512]{1,0:T(8,128)S(1)} %copy-done.29, ...), custom_call_target="tpu_custom_call" | custom-call | tf_op jit(solution)/shard_map/start/pallas_call | solution.py:222
  10.9 12.0 %all-to-all-start = ((f32[32,8,128]{2,1,0:T(8,128)}), f32[32,8,128]{2,1,0:T(8,128)}, u32[]{:S(2)}, u32[]{:S(2)}) async-start(f32[32,8,128]{2,1,0:T(8,128)} %get-tuple-element.31), calls=%async_computation | async-start | bytes 262144 | tf_op jit(solution)/shard_map/all_to_all | solution.py:497
  22.9 3.1 %collective-permute-start = (bf16[16,1024]{1,0:T(8,128)(2,1)S(1)}, bf16[16,1024]{1,0:T(8,128)(2,1)S(1)}, u32[]{:S(2)}, u32[]{:S(2)}) collective-permute-start(bf16[16,1024]{1,0:T(8,128)(2,1)S(1)} %get-tuple-element.36), channel_id=1, source_target_pairs={{0,8},{8,16},{16,24},{24,32},{32,40},{40,48},{48,56},{56,64},{64,7... | collective-permute-start | bytes 98312 | tf_op jit(solution)/shard_map/ppermute | solution.py:493
  27.3 3.7 %collective-permute-done.1.hi_top.hi_bottom.hi = bf16[16,1024]{1,0:T(8,128)(2,1)S(1)} collective-permute-done((bf16[16,1024]{1,0:T(8,128)(2,1)S(1)}, bf16[16,1024]{1,0:T(8,128)(2,1)S(1)}, u32[]{:S(2)}, u32[]{:S(2)}) %collective-permute-start.1) | collective-permute-done | bytes 32800 | tf_op jit(solution)/shard_map/ppermute | solution.py:493
  31.2 5.5 %collective-permute-start.2 = (bf16[16,640]{1,0:T(8,128)(2,1)S(1)}, bf16[16,640]{1,0:T(8,128)(2,1)S(1)}, u32[]{:S(2)}, u32[]{:S(2)}) collective-permute-start(bf16[16,640]{1,0:T(8,128)(2,1)S(1)} %get-tuple-element.38), channel_id=1, source_target_pairs={{0,1},{1,2},{2,3},{3,4},{4,5},{5,6},{6,7},{8,9},{9,10},{10,11},{11... | collective-permute-start | bytes 61448 | tf_op jit(solution)/shard_map/ppermute | solution.py:493
  36.7 1.9 %collective-permute-start.3 = (bf16[16,640]{1,0:T(8,128)(2,1)S(1)}, bf16[16,640]{1,0:T(8,128)(2,1)S(1)}, u32[]{:S(2)}, u32[]{:S(2)}) collective-permute-start(bf16[16,640]{1,0:T(8,128)(2,1)S(1)} %get-tuple-element.39), channel_id=1, source_target_pairs={{1,0},{2,1},{3,2},{4,3},{5,4},{6,5},{7,6},{9,8},{10,9},{11,10},{12... | collective-permute-start | bytes 61448 | tf_op jit(solution)/shard_map/ppermute | solution.py:493
  38.6 3.2 %collective-permute-done.3.below = bf16[16,640]{1,0:T(8,128)(2,1)S(1)} collective-permute-done((bf16[16,640]{1,0:T(8,128)(2,1)S(1)}, bf16[16,640]{1,0:T(8,128)(2,1)S(1)}, u32[]{:S(2)}, u32[]{:S(2)}) %collective-permute-start.3) | collective-permute-done | bytes 20512 | tf_op jit(solution)/shard_map/ppermute | solution.py:493
  43.4 2.2 %copy-done = f32[32,128,256]{2,1,0:T(8,128)S(1)} copy-done((f32[32,128,256]{2,1,0:T(8,128)S(1)}, f32[32,128,256]{2,1,0:T(8,128)}, u32[]{:S(2)}) %copy-start) | copy-done | bytes 4194328
  45.6 1.8 across.4
  48.6 4.3 %all-to-all-start.1 = ((f32[8,8,128]{2,1,0:T(8,128)}), f32[8,8,128]{2,1,0:T(8,128)S(1)}, u32[]{:S(2)}, u32[]{:S(2)}) async-start(f32[8,8,128]{2,1,0:T(8,128)} %copy-done.51), calls=%async_computation.1 | async-start | bytes 65536 | tf_op jit(solution)/shard_map/all_to_all | solution.py:497
  55.0 1.9 %fine.4.short = f32[1056,640]{1,0:T(8,128)S(1)} custom-call(bf16[1056,640]{1,0:T(8,128)(2,1)S(1)} %assemble.1.dose, bf16[640,640]{1,0:T(8,128)(2,1)S(1)} %copy-done.16, bf16[3,176,208]{2,1,0:T(8,128)(2,1)S(1)} %copy-done.27), custom_call_target="tpu_custom_call" | custom-call | flops 1146224640 | bytes 4055040 | tf_op jit(solution)/shard_map/fine/pallas_call | solution.py:364
  64.6 4.6 %step.3 = (bf16[1056,640]{1,0:T(8,128)(2,1)S(1)}, f32[32,8,128]{2,1,0:T(8,128)S(1)}, f32[128,128]{1,0:T(8,128)S(1)}) custom-call(s32[2]{0:T(128)S(1)} %pad_add_fusion.place, f32[3]{0:T(128)S(1)} %copy-done.52, f32[64,128]{1,0:T(8,128)S(1)} %bitcast.16, f32[128,128]{1,0:T(8,128)S(1)} %copy-done.48, f32[8,296,192]{2,1,0:T(8,128)S(1)} %copy-done.5, ...), custom_call_target="tpu_custom_call" | custom-call | tf_op jit(solution)/shard_map/step/pallas_call | solution.py:419
  69.1 18.4 %all_to_all.40 = f32[32,8,128]{2,1,0:T(8,128)S(1)} all-to-all(f32[32,8,128]{2,1,0:T(8,128)S(1)} %get-tuple-element.40), channel_id=1, replica_groups=mesh['gx'=32,'gy'=8] {'gx'}, dimensions={0} | all-to-all | bytes 262144 | tf_op jit(solution)/shard_map/all_to_all | solution.py:497
  89.1 6.5 %all-to-all-start.3 = ((f32[8,8,128]{2,1,0:T(8,128)}), f32[8,8,128]{2,1,0:T(8,128)S(1)}, u32[]{:S(2)}, u32[]{:S(2)}) async-start(f32[8,8,128]{2,1,0:T(8,128)} %get-tuple-element.42), calls=%async_computation.3 | async-start | bytes 65536 | tf_op jit(solution)/shard_map/all_to_all | solution.py:497
  97.0 1.9 %fine.5.short = f32[1056,640]{1,0:T(8,128)S(1)} custom-call(bf16[1056,640]{1,0:T(8,128)(2,1)S(1)} %copy-done.22, bf16[640,640]{1,0:T(8,128)(2,1)S(1)} %copy-done.17, bf16[3,176,208]{2,1,0:T(8,128)(2,1)S(1)} %copy-done.28), custom_call_target="tpu_custom_call" | custom-call | flops 1146224640 | bytes 4055040 | tf_op jit(solution)/shard_map/fine/pallas_call | solution.py:364
  107.8 4.5 %step.4 = (bf16[1056,640]{1,0:T(8,128)(2,1)S(1)}, f32[32,8,128]{2,1,0:T(8,128)S(1)}, f32[128,128]{1,0:T(8,128)S(1)}) custom-call(s32[2]{0:T(128)S(1)} %pad_add_fusion.place, f32[3]{0:T(128)S(1)} %copy-done.52, f32[64,128]{1,0:T(8,128)S(1)} %bitcast.15, f32[128,128]{1,0:T(8,128)S(1)} %copy-done.46, f32[8,296,192]{2,1,0:T(8,128)S(1)} %copy-done.6, ...), custom_call_target="tpu_custom_call" | custom-call | tf_op jit(solution)/shard_map/step/pallas_call | solution.py:419
  112.3 12.4 %all_to_all.41 = f32[32,8,128]{2,1,0:T(8,128)S(1)} all-to-all(f32[32,8,128]{2,1,0:T(8,128)S(1)} %get-tuple-element.45), channel_id=1, replica_groups=mesh['gx'=32,'gy'=8] {'gx'}, dimensions={0} | all-to-all | bytes 262144 | tf_op jit(solution)/shard_map/all_to_all | solution.py:497
  126.9 6.5 %all-to-all-start.5 = ((f32[8,8,128]{2,1,0:T(8,128)}), f32[8,8,128]{2,1,0:T(8,128)S(1)}, u32[]{:S(2)}, u32[]{:S(2)}) async-start(f32[8,8,128]{2,1,0:T(8,128)} %copy-done.50), calls=%async_computation.5 | async-start | bytes 65536 | tf_op jit(solution)/shard_map/all_to_all | solution.py:497
  134.8 1.9 %fine.6.short = f32[1056,640]{1,0:T(8,128)S(1)} custom-call(bf16[1056,640]{1,0:T(8,128)(2,1)S(1)} %copy-done.19, bf16[640,640]{1,0:T(8,128)(2,1)S(1)} %copy-done.17, bf16[3,176,208]{2,1,0:T(8,128)(2,1)S(1)} %copy-done.28), custom_call_target="tpu_custom_call" | custom-call | flops 1146224640 | bytes 4055040 | tf_op jit(solution)/shard_map/fine/pallas_call | solution.py:364
  145.6 4.5 %step.5 = (bf16[1056,640]{1,0:T(8,128)(2,1)S(1)}, f32[32,8,128]{2,1,0:T(8,128)S(1)}, f32[128,128]{1,0:T(8,128)S(1)}) custom-call(s32[2]{0:T(128)S(1)} %pad_add_fusion.place, f32[3]{0:T(128)S(1)} %copy-done.52, f32[64,128]{1,0:T(8,128)S(1)} %bitcast.14, f32[128,128]{1,0:T(8,128)S(1)} %copy-done.44, f32[8,296,192]{2,1,0:T(8,128)S(1)} %copy-done.7, ...), custom_call_target="tpu_custom_call" | custom-call | tf_op jit(solution)/shard_map/step/pallas_call | solution.py:419
  150.1 12.4 %all_to_all.42 = f32[32,8,128]{2,1,0:T(8,128)S(1)} all-to-all(f32[32,8,128]{2,1,0:T(8,128)S(1)} %get-tuple-element.50), channel_id=1, replica_groups=mesh['gx'=32,'gy'=8] {'gx'}, dimensions={0} | all-to-all | bytes 262144 | tf_op jit(solution)/shard_map/all_to_all | solution.py:497
  164.1 6.5 %all-to-all-start.7 = ((f32[8,8,128]{2,1,0:T(8,128)}), f32[8,8,128]{2,1,0:T(8,128)S(1)}, u32[]{:S(2)}, u32[]{:S(2)}) async-start(f32[8,8,128]{2,1,0:T(8,128)} %get-tuple-element.52), calls=%async_computation.7 | async-start | bytes 65536 | tf_op jit(solution)/shard_map/all_to_all | solution.py:497
  175.3 1.9 %copy-done.24 = f32[8,392,192]{2,1,0:T(8,128)S(1)} copy-done((f32[8,392,192]{2,1,0:T(8,128)S(1)}, f32[8,392,192]{2,1,0:T(8,128)}, u32[]{:S(2)}) %copy-start.24) | copy-done | bytes 2408472
  179.3 5.6 %finish.1 = f32[1024,512]{1,0:T(8,128)} custom-call(s32[2]{0:T(128)S(1)} %pad_add_fusion.place, f32[3]{0:T(128)S(1)} %copy-done.52, f32[64,128]{1,0:T(8,128)S(1)} %bitcast.13, f32[128,128]{1,0:T(8,128)S(1)} %copy-done.42, f32[8,392,192]{2,1,0:T(8,128)S(1)} %copy-done.24, f32[128,512]{1,0:T(8,128)S(1)} %copy-done.39, bf16[1024,512]{1,0:T(8,128)(2,1)S(1)} %copy-done.35, ...), custom_call_target="tpu_custom_call" | custom-call | tf_op jit(solution)/shard_map/finish/pallas_call | solution.py:465
  (126 shorter events, 52.4 us)
Async XLA Ops:
  10.9 27.7 %copy-start.14 = (bf16[1024,512]{1,0:T(8,128)(2,1)}, bf16[1024,512]{1,0:T(8,128)(2,1)S(1)}, u32[]{:S(2)}) copy-start(bf16[1024,512]{1,0:T(8,128)(2,1)S(1)} %get-tuple-element.35.dose_top.dose_bottom.dose) | copy-start | bytes 3145732
  10.9 32.5 %all-to-all-start = ((f32[32,8,128]{2,1,0:T(8,128)}), f32[32,8,128]{2,1,0:T(8,128)}, u32[]{:S(2)}, u32[]{:S(2)}) async-start(f32[32,8,128]{2,1,0:T(8,128)} %get-tuple-element.31), calls=%async_computation | async-start | bytes 262144 | tf_op jit(solution)/shard_map/all_to_all | solution.py:497
  22.9 4.4 %collective-permute-start = (bf16[16,1024]{1,0:T(8,128)(2,1)S(1)}, bf16[16,1024]{1,0:T(8,128)(2,1)S(1)}, u32[]{:S(2)}, u32[]{:S(2)}) collective-permute-start(bf16[16,1024]{1,0:T(8,128)(2,1)S(1)} %get-tuple-element.36), channel_id=1, source_target_pairs={{0,8},{8,16},{16,24},{24,32},{32,40},{40,48},{48,56},{56,64},{64,7... | collective-permute-start | bytes 98312 | tf_op jit(solution)/shard_map/ppermute | solution.py:493
  26.0 5.1 %collective-permute-start.1 = (bf16[16,1024]{1,0:T(8,128)(2,1)S(1)}, bf16[16,1024]{1,0:T(8,128)(2,1)S(1)}, u32[]{:S(2)}, u32[]{:S(2)}) collective-permute-start(bf16[16,1024]{1,0:T(8,128)(2,1)S(1)} %get-tuple-element.37), channel_id=1, source_target_pairs={{8,0},{16,8},{24,16},{32,24},{40,32},{48,40},{56,48},{64,56},{72,6... | collective-permute-start | bytes 98312 | tf_op jit(solution)/shard_map/ppermute | solution.py:493
  31.0 12.3 %copy-start.4 = (f32[32,128,32]{2,1,0:T(8,128)S(1)}, f32[32,128,32]{2,1,0:T(8,128)}, u32[]{:S(2)}) copy-start(f32[32,128,32]{2,1,0:T(8,128)} %constant.36.clone.mown) | copy-start | bytes 1572868
  31.2 7.4 %collective-permute-start.2 = (bf16[16,640]{1,0:T(8,128)(2,1)S(1)}, bf16[16,640]{1,0:T(8,128)(2,1)S(1)}, u32[]{:S(2)}, u32[]{:S(2)}) collective-permute-start(bf16[16,640]{1,0:T(8,128)(2,1)S(1)} %get-tuple-element.38), channel_id=1, source_target_pairs={{0,1},{1,2},{2,3},{3,4},{4,5},{5,6},{6,7},{8,9},{9,10},{10,11},{11... | collective-permute-start | bytes 61448 | tf_op jit(solution)/shard_map/ppermute | solution.py:493
  36.7 5.1 %collective-permute-start.3 = (bf16[16,640]{1,0:T(8,128)(2,1)S(1)}, bf16[16,640]{1,0:T(8,128)(2,1)S(1)}, u32[]{:S(2)}, u32[]{:S(2)}) collective-permute-start(bf16[16,640]{1,0:T(8,128)(2,1)S(1)} %get-tuple-element.39), channel_id=1, source_target_pairs={{1,0},{2,1},{3,2},{4,3},{5,4},{6,5},{7,6},{9,8},{10,9},{11,10},{12... | collective-permute-start | bytes 61448 | tf_op jit(solution)/shard_map/ppermute | solution.py:493
  48.6 9.7 %all-to-all-start.1 = ((f32[8,8,128]{2,1,0:T(8,128)}), f32[8,8,128]{2,1,0:T(8,128)S(1)}, u32[]{:S(2)}, u32[]{:S(2)}) async-start(f32[8,8,128]{2,1,0:T(8,128)} %copy-done.51), calls=%async_computation.1 | async-start | bytes 65536 | tf_op jit(solution)/shard_map/all_to_all | solution.py:497
  55.0 3.4 %copy-start.52 = (f32[3]{0:T(128)S(1)}, f32[3]{0:T(128)}, u32[]{:S(2)}) copy-start(f32[3]{0:T(128)} %weights.7) | copy-start | bytes 40
  64.6 23.0 %copy-start.1 = (f32[32,128,256]{2,1,0:T(8,128)S(1)}, f32[32,128,256]{2,1,0:T(8,128)}, u32[]{:S(2)}) copy-start(f32[32,128,256]{2,1,0:T(8,128)} %constant.35.clone.mgot) | copy-start | bytes 12582916
  69.1 20.0 %copy-start.21 = (bf16[1056,640]{1,0:T(8,128)(2,1)}, bf16[1056,640]{1,0:T(8,128)(2,1)S(1)}, u32[]{:S(2)}) copy-start(bf16[1056,640]{1,0:T(8,128)(2,1)S(1)} %get-tuple-element.44.dose) | copy-start | bytes 4055044
  87.6 8.1 %copy-start.17 = (bf16[640,640]{1,0:T(8,128)(2,1)S(1)}, bf16[640,640]{1,0:T(8,128)(2,1)}, u32[]{:S(2)}) copy-start(bf16[640,640]{1,0:T(8,128)(2,1)} %constant.37.clone.cols) | copy-start | bytes 2457604
  87.6 8.1 %copy-start.28 = (bf16[3,176,208]{2,1,0:T(8,128)(2,1)S(1)}, bf16[3,176,208]{2,1,0:T(8,128)(2,1)}, u32[]{:S(2)}) copy-start(bf16[3,176,208]{2,1,0:T(8,128)(2,1)} %constant.38.clone.rows) | copy-start | bytes 658948
  89.1 6.6 %copy-start.45 = (f32[128,128]{1,0:T(8,128)}, f32[128,128]{1,0:T(8,128)S(1)}, u32[]{:S(2)}) copy-start(f32[128,128]{1,0:T(8,128)S(1)} %get-tuple-element.43.part) | copy-start | bytes 196612
  89.1 11.3 %all-to-all-start.3 = ((f32[8,8,128]{2,1,0:T(8,128)}), f32[8,8,128]{2,1,0:T(8,128)S(1)}, u32[]{:S(2)}, u32[]{:S(2)}) async-start(f32[8,8,128]{2,1,0:T(8,128)} %get-tuple-element.42), calls=%async_computation.3 | async-start | bytes 65536 | tf_op jit(solution)/shard_map/all_to_all | solution.py:497
  97.0 3.4 %copy-start.26 = (f32[128,640]{1,0:T(8,128)S(1)}, f32[128,640]{1,0:T(8,128)}, u32[]{:S(2)}) copy-start(f32[128,640]{1,0:T(8,128)} %constant.40.clone.cols) | copy-start | bytes 983044
  107.8 17.0 %copy-start.2 = (f32[32,128,256]{2,1,0:T(8,128)S(1)}, f32[32,128,256]{2,1,0:T(8,128)}, u32[]{:S(2)}) copy-start(f32[32,128,256]{2,1,0:T(8,128)} %constant.35.clone.mgot) | copy-start | bytes 12582916
  112.3 13.3 %copy-start.18 = (bf16[1056,640]{1,0:T(8,128)(2,1)}, bf16[1056,640]{1,0:T(8,128)(2,1)S(1)}, u32[]{:S(2)}) copy-start(bf16[1056,640]{1,0:T(8,128)(2,1)S(1)} %get-tuple-element.49.dose) | copy-start | bytes 4055044
  126.9 11.3 %all-to-all-start.5 = ((f32[8,8,128]{2,1,0:T(8,128)}), f32[8,8,128]{2,1,0:T(8,128)S(1)}, u32[]{:S(2)}, u32[]{:S(2)}) async-start(f32[8,8,128]{2,1,0:T(8,128)} %copy-done.50), calls=%async_computation.5 | async-start | bytes 65536 | tf_op jit(solution)/shard_map/all_to_all | solution.py:497
  145.6 17.0 %copy-start.3 = (f32[32,128,256]{2,1,0:T(8,128)S(1)}, f32[32,128,256]{2,1,0:T(8,128)}, u32[]{:S(2)}) copy-start(f32[32,128,256]{2,1,0:T(8,128)} %constant.35.clone.mgot) | copy-start | bytes 12582916
  150.1 13.9 %copy-start.54 = (bf16[1056,640]{1,0:T(8,128)(2,1)}, bf16[1056,640]{1,0:T(8,128)(2,1)S(1)}, u32[]{:S(2)}) copy-start(bf16[1056,640]{1,0:T(8,128)(2,1)S(1)} %get-tuple-element.54.dose) | copy-start | bytes 4055044
  164.1 6.5 %copy-start.41 = (f32[128,128]{1,0:T(8,128)}, f32[128,128]{1,0:T(8,128)S(1)}, u32[]{:S(2)}) copy-start(f32[128,128]{1,0:T(8,128)S(1)} %get-tuple-element.53.part) | copy-start | bytes 196612
  164.1 11.3 %all-to-all-start.7 = ((f32[8,8,128]{2,1,0:T(8,128)}), f32[8,8,128]{2,1,0:T(8,128)S(1)}, u32[]{:S(2)}, u32[]{:S(2)}) async-start(f32[8,8,128]{2,1,0:T(8,128)} %get-tuple-element.52), calls=%async_computation.7 | async-start | bytes 65536 | tf_op jit(solution)/shard_map/all_to_all | solution.py:497
  171.9 3.4 %copy-start.39 = (f32[128,512]{1,0:T(8,128)S(1)}, f32[128,512]{1,0:T(8,128)}, u32[]{:S(2)}) copy-start(f32[128,512]{1,0:T(8,128)} %constant.44.clone.cols) | copy-start | bytes 786436
  (41 other events, 50.9 us)
where the time goes:
time: 187 us; the launch traced here: 185 us
  local copies, waits for them, and re-layouts  48.3 us (26%)
  starting transfers between devices  47.7 us (26%)
  blocking collectives  43.3 us (23%)
  Pallas kernels  37.7 us (20%)
  waiting for transfers between devices  7.59 us (4%)
    unnamed x113, local copies, waits for them, and re-layouts  48.3 us
    all_to_all x3, blocking collectives, exchanged(): return lax.all_to_all(x, axis, 0, 0, tiled=True)  43.3 us
    all_to_all x5, starting transfers between devices, exchanged(): return lax.all_to_all(x, axis, 0, 0, tiled=True)  35.9 us
    pallas_call x3, Pallas kernels, step(): pl.pallas_call(step_kernel, grid_spec=pltpu.PrefetchScalarGridSpec(num_sc...  13.6 us
    ppermute x4, starting transfers between devices, shifted(): lax.ppermute(x, axis, [(i, i + by) for i in range(n) if 0 <= i + by < n])  11.8 us
    pallas_call x4, Pallas kernels, fine(): pl.pallas_call(functools.partial(fine_kernel, last), out_shape=shapes, sc...  7.38 us
    ppermute x4, waiting for transfers between devices, shifted(): lax.ppermute(x, axis, [(i, i + by) for i in range(n) if 0 <= i + by < n])  6.91 us
    pallas_call x4, Pallas kernels, across(): pl.pallas_call(across_kernel, grid_spec=pltpu.PrefetchScalarGridSpec(num_...  5.76 us
  transfers between devices with their start and end apart: 9, of which 3 were waited for; matrix products, arithmetic and copies ran while one was open for 0% of the time, Pallas kernels for 4%

commit v1 on v0

v1 whole, which is shorter than its diff:
```python
import functools

import jax
import jax.numpy as jnp
import ml_dtypes
import numpy as np
from jax import lax
from jax.experimental import pallas as pl
from jax.experimental.pallas import tpu as pltpu
from jax.sharding import PartitionSpec as P

HW = 4
CLASSES = 8
SB = 128
ITERS = 4
NX, NY = 32, 8
TR, TC = 1024, 512
HALO = HW * ITERS
ER = TR + 2 * HALO
EC = TC + 128
BLK = 176
NB = ER // BLK
QC, QR = 36, 68
F32, BF16 = jnp.float32, jnp.bfloat16
EXACT = lax.Precision.HIGHEST


def gauss_taps():
    offsets = np.arange(-HW, HW + 1).astype(np.float32)
    weights = np.exp(-(offsets * offsets) / np.float32(HW * HW)).astype(np.float32)
    return weights / weights.sum(dtype=np.float32)


def blur_operator(n):
    taps = gauss_taps().astype(np.float64)
    out = np.zeros((n, n))
    for k in range(-HW, HW + 1):
        out += taps[k + HW] * np.eye(n, k=k)
    return out


def up_operator(n, factor):
    target = np.arange(n * factor)
    lower = (target - factor // 2) // factor
    t = (target - factor // 2 - factor * lower + 0.5) / factor
    out = np.zeros((n * factor, n))
    np.add.at(out, (target, np.clip(lower, 0, n - 1)), 1 - t)
    np.add.at(out, (target, np.clip(lower + 1, 0, n - 1)), t)
    return out


def level_operators(n_second):
    third, fourth = n_second // 4, n_second // 16
    return (
        blur_operator(n_second),
        up_operator(third, 4) @ blur_operator(third),
        up_operator(third, 4) @ up_operator(fourth, 4) @ blur_operator(fourth),
    )


@functools.cache
def column_matrices():
    second, third, fourth = level_operators(NX * 32)
    got = np.zeros((NX, 128, 256), np.float32)
    own = np.zeros((NX, 128, 32), np.float32)
    for px in range(NX):
        for q in range(QC):
            g = min(max(32 * px + q - 2, 0), NX * 32 - 1)
            for s in np.nonzero(second[g])[0]:
                p, j = divmod(int(s), 32)
                if p == px:
                    own[px, q, j] = second[g, s]
                else:
                    assert j >= 24 if p < px else j < 8
                    got[px, q, p * 8 + j % 8] = second[g, s]
            got[px, 40 + q] = third[g]
            for j in range(2):
                got[px, 80 + q, j::8] = fourth[g, j::2]
        got[px, 120, 0::8] = 1
        got[px, 120, 1::8] = 1
    return got, own


def row_matrices(groups, first, step, length):
    second, third, fourth = level_operators(NY * 64)
    m = 16 * groups
    out = np.zeros((NY, 3 * m + 8, 192), np.float32)
    for py in range(NY):
        for b in range(groups):
            for k in range(length):
                row, q = b * 16 + k, first + step * b + k
                g = min(max(64 * py + q - 2, 0), NY * 64 - 1)
                for s in np.nonzero(second[g])[0]:
                    p, j = divmod(int(s), 64)
                    assert p == py or (j >= 56 if p < py else j < 8)
                    out[py, row, 64 + j if p == py else p * 8 + j % 8] = second[g, s]
                for s in np.nonzero(third[g])[0]:
                    p, j = divmod(int(s), 16)
                    assert p == py or (j >= 8 if p < py else j < 8)
                    out[py, m + row, 128 + j if p == py else p * 8 + j % 8] = third[g, s]
                for s in np.nonzero(fourth[g])[0]:
                    p, j = divmod(int(s), 4)
                    out[py, 2 * m + row, p * 8 + j] = fourth[g, s]
        out[py, 3 * m, 4:64:8] = 1
    return out


@functools.cache
def column_spread():
    out = np.zeros((128, EC), np.float32)
    for lane in range(EC):
        cell = lane if lane < TC + HALO else lane - EC
        if cell < -HALO:
            continue
        lower = (cell - 8) // 16
        t = (cell - 8 - 16 * lower + 0.5) / 16
        for level in range(3):
            out[40 * level + lower + 2, lane] += 1 - t
            out[40 * level + lower + 3, lane] += t
        out[120, lane] = 1
    return out.astype(ml_dtypes.bfloat16)


@functools.cache
def column_pool(lanes):
    out = np.zeros((lanes, 128), np.float32)
    cell = np.arange(TC)
    out[cell, cell // 16] = 1
    out[cell, 32 + cell // 64] = 1
    out[cell, 40 + cell // 256] = 1
    return out.astype(ml_dtypes.bfloat16)


@functools.cache
def row_pool(groups, stride, real, first):
    out = np.zeros((128, groups * stride), np.float32)
    for b in range(groups):
        for k in range(real):
            s = b * real + k - first
            if 0 <= s < TR // 16:
                at = b * stride + k
                out[s, at] = 2.0**-8
                out[64 + s // 4, at] = 2.0**-12
                out[80 + s // 16, at] = 2.0**-16
                out[84, at] = 1.0 / (TR * NY * TC * NX)
    return out.astype(ml_dtypes.bfloat16)


def fine_taps():
    return gauss_taps().astype(ml_dtypes.bfloat16)


@functools.cache
def fine_columns():
    out = np.zeros((512, 256), ml_dtypes.bfloat16)
    taps, lane = fine_taps(), np.arange(256)
    for k in range(-HW, HW + 1):
        out[lane + 128 + k, lane] = taps[k + HW]
    return out


@functools.cache
def fine_rows():
    out = np.zeros((3, BLK, BLK + 32), ml_dtypes.bfloat16)
    taps = fine_taps()
    for which in range(3):
        for r in range(BLK):
            for k in range(-HW, HW + 1):
                c = r + 16 * which + k
                if 0 <= c < BLK + 32:
                    out[which, r, c] = taps[k + HW]
    return out


VMEM = pl.BlockSpec(memory_space=pltpu.VMEM)
SMEM = pl.BlockSpec(memory_space=pltpu.SMEM)
HBM = pl.BlockSpec(memory_space=pl.ANY)
DMA = pltpu.SemaphoreType.DMA


def params(mib=24):
    return pltpu.CompilerParams(vmem_limit_bytes=mib * 2**20)


def near(x):
    return pltpu.with_memory_space_constraint(x, pltpu.VMEM)


def far(x):
    return pltpu.with_memory_space_constraint(x, pltpu.HBM)


def dot(a, b, **kw):
    return jnp.dot(a, b, preferred_element_type=F32, **kw)


def pieces(x):
    first = x.astype(BF16)
    rest = x - first.astype(F32)
    second = rest.astype(BF16)
    return first, second, (rest - second.astype(F32)).astype(BF16)


def pooled_out(sums, row_pool_ref, px, send_ref, own_ref):
    a, b, c = pieces(sums)
    rows = row_pool_ref[...]
    pooled = (dot(rows, a) + dot(rows, b) + dot(rows, c)).T
    own_ref[...] = pooled
    lane = lax.broadcasted_iota(jnp.int32, (8, 128), 1)
    coarse = jnp.where(lane < 80, pooled[32:40], pooled[40:48])
    left = jnp.where(lane < 64, pooled[0:8], coarse)
    right = jnp.where(lane < 64, pooled[24:32], coarse)
    for p in range(NX):
        send_ref[p] = jnp.where(p < px, left, right)


def operators():
    mgot, mown = column_matrices()
    return [
        (row_matrices(NB, 0, BLK // 16, BLK // 16 + 2), 1),
        (row_matrices(TR // SB, 1, SB // 16, SB // 16 + 2), 1),
        (mgot, 0),
        (mown, 0),
        (column_spread(), None),
        (column_pool(EC), None),
        (row_pool(NB, 16, BLK // 16, 1), None),
        (fine_columns(), None),
        (fine_rows(), None),
    ]


def start_kernel(picks, weights, table, exps, classes, gain, cpool, rpool, *refs):
    n, steps = len(picks), TR // SB
    tables, outs = refs[:n], refs[n + 7 : 2 * n + 7]
    dose, top, bottom, lo, hi, send, own = refs[n : n + 7]
    cbuf, gbuf, made, sums, csem, gsem, tsem, dsem = refs[2 * n + 7 :]
    place = lax.axis_index("gx"), lax.axis_index("gy")
    loads = []
    for i in range(steps):
        rows = pl.ds(i * SB, SB)
        loads.append(
            (
                pltpu.make_async_copy(classes.at[rows], cbuf.at[rows], csem.at[i]),
                pltpu.make_async_copy(gain.at[rows], gbuf.at[rows], gsem.at[i]),
            )
        )
        for copy in loads[-1]:
            copy.start()
    copies = []
    for i, pick in enumerate(picks):
        source = tables[i] if pick is None else tables[i].at[place[pick]]
        copies.append(pltpu.make_async_copy(source, outs[i], tsem.at[i]))
        copies[-1].start()
    stores = []
    for i in range(steps):
        for copy in loads[i]:
            copy.wait()
        rows = slice(i * SB, (i + 1) * SB)
        for k in range(TC // SB):
            e = exps[i, k]
            scale = jnp.where(e > 0, 2.0, jnp.where(e < 0, 0.5, 1.0)).astype(F32)
            at = slice(k * SB, (k + 1) * SB)
            c = cbuf[rows, at]
            level = jnp.zeros((SB, SB), F32)
            for j in range(1, CLASSES):
                level = jnp.where(c == j, table[j] * scale, level)
            value = (level * gbuf[rows, at].astype(F32)).astype(BF16)
            made[rows, at] = value
            if k == 0:
                lo[:, rows] = value.astype(F32).T[:HALO].astype(BF16)
            if k == TC // SB - 1:
                hi[:, rows] = value.astype(F32).T[SB - HALO :].astype(BF16)
        stores.append(pltpu.make_async_copy(made.at[rows], dose.at[rows], dsem.at[i]))
        stores[-1].start()
        across = dot(made[rows], cpool[...])
        sums[8 * i : 8 * i + 8] = jnp.sum(across.reshape(8, 16, 128), axis=1)
    top[...] = made[:HALO]
    bottom[...] = made[TR - HALO :]
    pooled_out(sums[...], rpool, place[0], send, own)
    for copy in copies:
        copy.wait()
    for ref, m in ((outs[0], 16 * NB), (outs[1], TR // SB * 16)):
        for level in range(3):
            at = slice(m * level, m * (level + 1))
            ref[at] = ref[at] * weights[level]
        ref[3 * m :] = ref[3 * m :] * weights[2]
    for copy in stores:
        copy.wait()


def start(weights, table, exps, classes, gain):
    made = operators()
    picks = [pick for _, pick in made]
    outs = [pltpu.VMEM(t.shape if pick is None else t.shape[1:], t.dtype) for t, pick in made]
    steps = TR // SB
    got = pl.pallas_call(
        functools.partial(start_kernel, picks),
        in_specs=[SMEM, SMEM, SMEM, HBM, HBM, VMEM, VMEM] + [HBM] * len(made),
        out_specs=[HBM] + [VMEM] * (6 + len(made)),
        out_shape=[
            pltpu.HBM((TR, TC), BF16),
            pltpu.VMEM((HALO, TC), BF16),
            pltpu.VMEM((HALO, TC), BF16),
            pltpu.VMEM((HALO, TR), BF16),
            pltpu.VMEM((HALO, TR), BF16),
            pltpu.VMEM((NX, 8, 128), F32),
            pltpu.VMEM((128, 128), F32),
            *outs,
        ],
        scratch_shapes=[
            pltpu.VMEM((TR, TC), jnp.int32),
            pltpu.VMEM((TR, TC), BF16),
            pltpu.VMEM((TR, TC), BF16),
            pltpu.VMEM((TR // 16, 128), F32),
            DMA((steps,)),
            DMA((steps,)),
            DMA((len(made),)),
            DMA((steps,)),
        ],
        compiler_params=params(),
        name="start",
    )(
        weights, table, exps, far(classes), far(gain), column_pool(TC), row_pool(8, 8, 8, 0),
        *[far(jnp.asarray(t)) for t, _ in made],
    )
    return got[:7], got[7:]


def across_kernel(got, own, mgot, mown, send, part):
    received = got[...].reshape(NX * 8, 128)
    z = dot(mgot[...], received, precision=EXACT) + dot(mown[...], own[:32], precision=EXACT)
    z = z.T
    part[...] = z
    lane = lax.broadcasted_iota(jnp.int32, (8, 128), 1)
    coarse = z[80:88]
    up = jnp.where(lane < 40, z[0:8], jnp.where(lane < 80, z[64:72], coarse))
    down = jnp.where(lane < 40, z[56:64], jnp.where(lane < 80, z[72:80], coarse))
    py = lax.axis_index("gy")
    for p in range(NY):
        send[p] = jnp.where(p < py, up, down)


def across(got, own, ops):
    return pl.pallas_call(
        across_kernel,
        in_specs=[VMEM] * 4,
        out_specs=[VMEM] * 2,
        out_shape=[pltpu.VMEM((NY, 8, 128), F32), pltpu.VMEM((128, 128), F32)],
        compiler_params=params(),
        name="across",
    )(near(got), near(own), near(ops[2]), near(ops[3]))


def side(strip_lo, strip_hi):
    rows = strip_lo.shape[1]
    empty = jnp.zeros((rows, 128 - 2 * HALO), F32)
    return jnp.concatenate([strip_hi.astype(F32).T, empty, strip_lo.astype(F32).T], axis=1).astype(BF16)


def edges_kernel(first, final, lo, hi, top, bottom):
    top[:, :TC] = first[...]
    top[:, TC:] = side(lo[:, :128], hi[:, :128])[:HALO]
    bottom[:, :TC] = final[...]
    bottom[:, TC:] = side(lo[:, TR - 128 :], hi[:, TR - 128 :])[128 - HALO :]


def edges(first, final, lo, hi):
    return pl.pallas_call(
        edges_kernel,
        in_specs=[VMEM] * 4,
        out_specs=[VMEM] * 2,
        out_shape=[pltpu.VMEM((HALO, EC), BF16)] * 2,
        compiler_params=params(),
        name="edges",
    )(near(first), near(final), near(lo), near(hi))


def fine_blocks(last, wait, values, cols, rows, half, out_ref, store):
    def across_block(b):
        wait(b)
        block = values[b * BLK : (b + 1) * BLK]
        tile = [block[:, 128 * n : 128 * (n + 1)] for n in range(5)]
        join = lambda *which: jnp.concatenate([tile[n] for n in which], axis=1)
        at = slice(b * BLK, (b + 1) * BLK)
        half[at, :256] = dot(join(4, 0, 1, 2), cols[...]).astype(BF16)
        half[at, 256:512] = dot(join(1, 2, 3, 4), cols[...]).astype(BF16)
        if not last:
            half[at, 512:] = dot(join(3, 4, 0), cols[:384, :128]).astype(BF16)

    across_block(0)
    for b in range(NB):
        if b + 1 < NB:
            across_block(b + 1)
        first = min(max(b * BLK - 16, 0), ER - BLK - 32)
        which = (b * BLK - first) // 16
        got = dot(rows[which], half[first : first + BLK + 32]) + 1.0
        if last:
            begin, end = max(b * BLK, HALO), min((b + 1) * BLK, HALO + TR)
            out_ref[begin - HALO : end - HALO] = got[begin - b * BLK : end - b * BLK]
            store(b, begin - HALO, end - begin)
        else:
            out_ref[b * BLK : (b + 1) * BLK] = got
            store(b, b * BLK, BLK)


def fine_kernel(last, dose, cols, rows, out, buf, half, made, lsem, ssem):
    loads, stores = [], []
    for b in range(NB):
        at = pl.ds(b * BLK, BLK)
        loads.append(pltpu.make_async_copy(dose.at[at], buf.at[at], lsem.at[b]))
        loads[-1].start()

    def store(b, begin, count):
        at = pl.ds(begin, count)
        stores.append(pltpu.make_async_copy(made.at[at], out.at[at], ssem.at[b]))
        stores[-1].start()

    fine_blocks(last, lambda b: loads[b].wait(), buf, cols, rows, half, made, store)
    for copy in stores:
        copy.wait()


def fine_cost():
    return pl.CostEstimate(flops=2 * ER * EC * (EC + 208), bytes_accessed=6 * ER * EC, transcendentals=0)


def fine(dose, ops, last):
    shape = (TR, TC) if last else (ER, EC)
    return pl.pallas_call(
        functools.partial(fine_kernel, last),
        in_specs=[HBM, VMEM, VMEM],
        out_specs=HBM,
        out_shape=pltpu.HBM(shape, F32),
        scratch_shapes=[
            pltpu.VMEM((ER, EC), BF16),
            pltpu.VMEM((ER, shape[1]), BF16),
            pltpu.VMEM(shape, F32),
            DMA((NB,)),
            DMA((NB,)),
        ],
        compiler_params=params(),
        cost_estimate=fine_cost(),
        name="fine",
    )(far(dose), near(ops[7]), near(ops[8]))


def first_kernel(dose, lo, hi, above, below, cols, rows, out, whole, buf, half, made, lsem, ssem, wsem):
    load = pltpu.make_async_copy(dose, buf.at[pl.ds(HALO, TR), pl.ds(0, TC)], lsem)
    load.start()
    buf[:HALO] = above[...]
    buf[HALO + TR :] = below[...]
    for n in range(TR // 128):
        at = slice(n * 128, (n + 1) * 128)
        buf[HALO + n * 128 : HALO + (n + 1) * 128, TC:] = side(lo[:, at], hi[:, at])
    load.wait()
    keep = pltpu.make_async_copy(buf, whole, wsem)
    keep.start()
    stores = []

    def store(b, begin, count):
        at = pl.ds(begin, count)
        stores.append(pltpu.make_async_copy(made.at[at], out.at[at], ssem.at[b]))
        stores[-1].start()

    fine_blocks(False, lambda b: None, buf, cols, rows, half, made, store)
    for copy in stores:
        copy.wait()
    keep.wait()


def first_fine(dose, lo, hi, above, below, ops):
    return pl.pallas_call(
        first_kernel,
        in_specs=[HBM] + [VMEM] * 6,
        out_specs=[HBM, HBM],
        out_shape=[pltpu.HBM((ER, EC), F32), pltpu.HBM((ER, EC), BF16)],
        scratch_shapes=[
            pltpu.VMEM((ER, EC), BF16),
            pltpu.VMEM((ER, EC), BF16),
            pltpu.VMEM((ER, EC), F32),
            DMA,
            DMA((NB,)),
            DMA,
        ],
        compiler_params=params(),
        cost_estimate=fine_cost(),
        name="first_fine",
    )(far(dose), near(lo), near(hi), near(above), near(below), near(ops[7]), near(ops[8]))


def spread(got, part, matrix, cols, groups):
    m = 16 * groups
    stacked = jnp.concatenate([got[...].reshape(NY * 8, 128), part[...]], axis=0)
    y = dot(matrix[...], stacked, precision=EXACT)
    lane = lax.broadcasted_iota(jnp.int32, (m, 128), 1)
    fourth = jnp.where(lane < 120, y[2 * m : 3 * m], jnp.where(lane == 120, y[3 * m : 3 * m + 1], 0.0))
    a, b, c = pieces(jnp.where(lane < 40, y[:m], jnp.where(lane < 80, y[m : 2 * m], fourth)))
    return dot(a, cols) + dot(b, cols) + dot(c, cols)


def update(b, rows, skip, dose, short, grid, out):
    lanes = out.shape[1]
    t = (lax.broadcasted_iota(jnp.int32, (8, lanes), 0).astype(F32) + 0.5) / 16.0
    for n in range(rows // 16):
        row = b * rows + 16 * n
        at = slice(row, row + 16)
        a, m, c = (grid[16 * b + n + k : 16 * b + n + k + 1] for k in range(3))
        back = jnp.concatenate([a + (t + 0.5) * (m - a), m + t * (c - m)], axis=0)
        old = dose[skip + row : skip + row + 16].astype(F32)
        out[at] = (old * 2.0 / (short[at] + back)).astype(out.dtype)


def fetch(dose, short, dbuf, sbuf, blocks, rows, skip, sems):
    loads = []
    for b in range(blocks):
        at, lanes = pl.ds(b * rows, rows), pl.ds(0, dbuf.shape[1])
        loads.append(
            (
                pltpu.make_async_copy(
                    dose.at[pl.ds(b * rows + skip, rows), lanes], dbuf.at[at], sems.at[0, b]
                ),
                pltpu.make_async_copy(short.at[at], sbuf.at[at], sems.at[1, b]),
            )
        )
        for copy in loads[-1]:
            copy.start()
    return loads


def step_kernel(got, part, matrix, cols, dose, short, cpool, rpool, out, send, own, dbuf, sbuf, made, grid, sums, lsem, ssem):
    loads = fetch(dose, short, dbuf, sbuf, NB, BLK, 0, lsem)
    grid[...] = spread(got, part, matrix, cols[...], NB)
    stores = []
    for b in range(NB):
        for copy in loads[b]:
            copy.wait()
        update(b, BLK, 0, dbuf, sbuf, grid, made)
        at = pl.ds(b * BLK, BLK)
        stores.append(pltpu.make_async_copy(made.at[at], out.at[at], ssem.at[b]))
        stores[-1].start()
        pooled = dot(made[b * BLK : (b + 1) * BLK], cpool[...])
        pooled = jnp.sum(pooled.reshape(BLK // 16, 16, 128), axis=1)
        sums[16 * b : 16 * b + 16] = jnp.concatenate([pooled, jnp.zeros((16 - BLK // 16, 128), F32)], axis=0)
    pooled_out(sums[...], rpool, lax.axis_index("gx"), send, own)
    for copy in stores:
        copy.wait()


def step(got, part, dose, short, ops):
    return pl.pallas_call(
        step_kernel,
        in_specs=[VMEM] * 4 + [HBM] * 2 + [VMEM] * 2,
        out_specs=[HBM, VMEM, VMEM],
        out_shape=[
            pltpu.HBM((ER, EC), BF16),
            pltpu.VMEM((NX, 8, 128), F32),
            pltpu.VMEM((128, 128), F32),
        ],
        scratch_shapes=[
            pltpu.VMEM((ER, EC), BF16),
            pltpu.VMEM((ER, EC), F32),
            pltpu.VMEM((ER, EC), BF16),
            pltpu.VMEM((NB * 16, EC), F32),
            pltpu.VMEM((NB * 16, 128), F32),
            DMA((2, NB)),
            DMA((NB,)),
        ],
        compiler_params=params(),
        name="step",
    )(near(got), near(part), near(ops[0]), near(ops[4]), far(dose), far(short), near(ops[5]), near(ops[6]))


def finish_kernel(got, part, matrix, cols, dose, short, out, dbuf, sbuf, made, grid, lsem, ssem):
    groups = TR // SB
    loads = fetch(dose, short, dbuf, sbuf, groups, SB, HALO, lsem)
    grid[...] = spread(got, part, matrix, cols[:, :TC], groups)
    stores = []
    for b in range(groups):
        for copy in loads[b]:
            copy.wait()
        update(b, SB, 0, dbuf, sbuf, grid, made)
        at = pl.ds(b * SB, SB)
        stores.append(pltpu.make_async_copy(made.at[at], out.at[at], ssem.at[b]))
        stores[-1].start()
    for copy in stores:
        copy.wait()


def finish(got, part, dose, short, ops):
    groups = TR // SB
    return pl.pallas_call(
        finish_kernel,
        in_specs=[VMEM] * 4 + [HBM] * 2,
        out_specs=HBM,
        out_shape=pltpu.HBM((TR, TC), F32),
        scratch_shapes=[
            pltpu.VMEM((TR, TC), BF16),
            pltpu.VMEM((TR, TC), F32),
            pltpu.VMEM((TR, TC), F32),
            pltpu.VMEM((groups * 16, TC), F32),
            DMA((2, groups)),
            DMA((groups,)),
        ],
        compiler_params=params(),
        name="finish",
    )(near(got), near(part), near(ops[1]), near(ops[4]), far(dose), far(short))


def shifted(x, axis, by):
    n = lax.axis_size(axis)
    return lax.ppermute(x, axis, [(i, i + by) for i in range(n) if 0 <= i + by < n])


def exchanged(x, axis):
    return lax.all_to_all(x, axis, 0, 0, tiled=True)


def local(classes, exponents, gain_field, level_table, level_weights):
    (tile, first, final, lo, hi, send, own), ops = start(
        level_weights, level_table, exponents, classes, gain_field
    )
    left, right = shifted(hi, "gx", 1), shifted(lo, "gx", -1)
    got = exchanged(send, "gx")
    top, bottom = edges(first, final, left, right)
    above, below = shifted(bottom, "gy", 1), shifted(top, "gy", -1)
    send, part = across(got, own, ops)
    got = exchanged(send, "gy")
    short, dose = first_fine(tile, left, right, above, below, ops)
    for sweep in range(1, ITERS):
        dose, send, own = step(got, part, dose, short, ops)
        got = exchanged(send, "gx")
        short = fine(dose, ops, sweep == ITERS - 1)
        send, part = across(got, own, ops)
        got = exchanged(send, "gy")
    return finish(got, part, dose, short, ops)


def solution(mesh):
    in_specs = (P("gy", "gx"), P("gy", "gx"), P("gy", "gx"), P(), P())
    return jax.shard_map(local, mesh=mesh, in_specs=in_specs, out_specs=P("gy", "gx"), check_vma=False)
```

time: 187 us -> 144 us (0.77)
  local copies, waits for them, and re-layouts: 48.3 us -> 3.73 us
  Pallas kernels: 37.7 us -> 43.5 us
  waiting for transfers between devices: 7.59 us -> 4.99 us
    unnamed x113 -> x9, local copies, waits for them, and re-layouts: 48.3 us -> 3.73 us
    pallas_call x15 -> x14, Pallas kernels: 37.7 us -> 43.5 us  [the longest x3 13.2 us: fine(): pl.pallas_call(functools.partial(fine_kernel, last), in_specs=[HBM, VMEM,...]
    ppermute x4, waiting for transfers between devices: 6.91 us -> 3.65 us  [shifted(): lax.ppermute(x, axis, [(i, i + by) for i in range(n) if 0 <= i + by < n])]
  transfers between devices with their start and end apart: 9 -> 9, of which waited for: 3 -> 5; matrix products, arithmetic and copies ran while one was open for 0% -> 0% of each run, Pallas kernels for 4% -> 13%
where the time goes in v1:
time: 144 us; the launch traced here: 143 us
  starting transfers between devices  47.6 us (33%)
  Pallas kernels  43.5 us (30%)
  blocking collectives  43.3 us (30%)
  waiting for transfers between devices  4.99 us (3%)
  local copies, waits for them, and re-layouts  3.73 us (3%)
    all_to_all x3, blocking collectives, exchanged(): return lax.all_to_all(x, axis, 0, 0, tiled=True)  43.3 us
    all_to_all x5, starting transfers between devices, exchanged(): return lax.all_to_all(x, axis, 0, 0, tiled=True)  35.8 us
    pallas_call x3, Pallas kernels, fine(): pl.pallas_call(functools.partial(fine_kernel, last), in_specs=[HBM, VMEM,...  13.2 us
    pallas_call x3, Pallas kernels, step(): pl.pallas_call(step_kernel, in_specs=[VMEM] * 4 + [HBM] * 2 + [VMEM] * 2,...  13.1 us
    ppermute x4, starting transfers between devices, shifted(): lax.ppermute(x, axis, [(i, i + by) for i in range(n) if 0 <= i + by < n])  11.8 us
    pallas_call x1, Pallas kernels, start(): pl.pallas_call(functools.partial(start_kernel, picks), in_specs=[SMEM, SM...  5.86 us
    pallas_call x1, Pallas kernels, first_fine(): pl.pallas_call(first_kernel, in_specs=[HBM] + [VMEM] * 6, out_specs=[HBM,...  4.27 us
    pallas_call x4, Pallas kernels, across(): pl.pallas_call(across_kernel, in_specs=[VMEM] * 4, out_specs=[VMEM] * 2,...  3.93 us
  transfers between devices with their start and end apart: 9, of which 5 were waited for; matrix products, arithmetic and copies ran while one was open for 0% of the time, Pallas kernels for 13%

profile of v1, /device:TPU:1, one launch (start us, length us, event | category | flops | bytes accessed | tf_op | source)
XLA Modules:
  0.0 143.4 jit_solution(962450062619196226)
XLA Ops:
  3.7 5.9 %start.1 = (bf16[1024,512]{1,0:T(8,128)(2,1)}, bf16[16,512]{1,0:T(8,128)(2,1)S(1)}, bf16[16,512]{1,0:T(8,128)(2,1)S(1)}, bf16[16,1024]{1,0:T(8,128)(2,1)S(1)}, b...) custom-call(f32[3]{0:T(128)S(1)} %copy-done.2, ...), custom_call_target="tpu_custom_call" | custom-call | tf_op jit(solution)/shard_map/start/pallas_call | solution.py:296
  9.6 11.9 %all-to-all-start = ((f32[32,8,128]{2,1,0:T(8,128)}), f32[32,8,128]{2,1,0:T(8,128)S(1)}, u32[]{:S(2)}, u32[]{:S(2)}) async-start(f32[32,8,128]{2,1,0:T(8,128)} %get-tuple-element.42), calls=%async_computation | async-start | bytes 262144 | tf_op jit(solution)/shard_map/all_to_all | solution.py:615
  21.5 3.1 %collective-permute-start = (bf16[16,1024]{1,0:T(8,128)(2,1)S(1)}, bf16[16,1024]{1,0:T(8,128)(2,1)S(1)}, u32[]{:S(2)}, u32[]{:S(2)}) collective-permute-start(bf16[16,1024]{1,0:T(8,128)(2,1)S(1)} %get-tuple-element.51), channel_id=1, source_target_pairs={{0,8},{8,16},{16,24},{24,32},{32,40},{40,48},{48,56},{56,64},{64,7... | collective-permute-start | bytes 98312 | tf_op jit(solution)/shard_map/ppermute | solution.py:611
  24.6 1.3 collective-permute-start.1
  25.9 3.6 %collective-permute-done.1.hi = bf16[16,1024]{1,0:T(8,128)(2,1)S(1)} collective-permute-done((bf16[16,1024]{1,0:T(8,128)(2,1)S(1)}, bf16[16,1024]{1,0:T(8,128)(2,1)S(1)}, u32[]{:S(2)}, u32[]{:S(2)}) %collective-permute-start.1) | collective-permute-done | bytes 32800 | tf_op jit(solution)/shard_map/ppermute | solution.py:611
  29.7 5.5 %collective-permute-start.2 = (bf16[16,640]{1,0:T(8,128)(2,1)S(1)}, bf16[16,640]{1,0:T(8,128)(2,1)S(1)}, u32[]{:S(2)}, u32[]{:S(2)}) collective-permute-start(bf16[16,640]{1,0:T(8,128)(2,1)S(1)} %get-tuple-element.55), channel_id=1, source_target_pairs={{0,1},{1,2},{2,3},{3,4},{4,5},{5,6},{6,7},{8,9},{9,10},{10,11},{11... | collective-permute-start | bytes 61448 | tf_op jit(solution)/shard_map/ppermute | solution.py:611
  35.2 1.9 %collective-permute-start.3 = (bf16[16,640]{1,0:T(8,128)(2,1)S(1)}, bf16[16,640]{1,0:T(8,128)(2,1)S(1)}, u32[]{:S(2)}, u32[]{:S(2)}) collective-permute-start(bf16[16,640]{1,0:T(8,128)(2,1)S(1)} %get-tuple-element.56), channel_id=1, source_target_pairs={{1,0},{2,1},{3,2},{4,3},{5,4},{6,5},{7,6},{9,8},{10,9},{11,10},{12... | collective-permute-start | bytes 61448 | tf_op jit(solution)/shard_map/ppermute | solution.py:611
  37.2 1.0 across.4
  38.2 5.0 %all-to-all-start.1 = ((f32[8,8,128]{2,1,0:T(8,128)}), f32[8,8,128]{2,1,0:T(8,128)S(1)}, u32[]{:S(2)}, u32[]{:S(2)}) async-start(f32[8,8,128]{2,1,0:T(8,128)} %get-tuple-element.46), calls=%async_computation.1 | async-start | bytes 65536 | tf_op jit(solution)/shard_map/all_to_all | solution.py:615
  43.2 4.3 %first_fine.1 = (f32[1056,640]{1,0:T(8,128)}, bf16[1056,640]{1,0:T(8,128)(2,1)}) custom-call(bf16[1024,512]{1,0:T(8,128)(2,1)} %get-tuple-element.50.dose, bf16[16,1024]{1,0:T(8,128)(2,1)S(1)} %collective-permute-done.lo, bf16[16,1024]{1,0:T(8,128)(2,1)S(1)} %collective-permute-done.1.hi, bf16[16,640]{1,0:T(8,128)(2,1)S(1)} %collective-permute-done.2.above, ...), custom_call_target="tpu_custom_call" | custom-call | flops 1146224640 | bytes 4055040 | tf_op jit(solution)/shard_map/first_fine/pallas_call | solution.py:472
  47.9 4.4 %step.3 = (bf16[1056,640]{1,0:T(8,128)(2,1)}, f32[32,8,128]{2,1,0:T(8,128)S(1)}, f32[128,128]{1,0:T(8,128)S(1)}) custom-call(f32[8,8,128]{2,1,0:T(8,128)S(1)} %all-to-all-done.1.got, f32[128,128]{1,0:T(8,128)S(1)} %get-tuple-element.47.part, f32[296,192]{1,0:T(8,128)S(1)} %get-tuple-element.48.matrix, bf16[128,640]{1,0:T(8,128)(2,1)S(1)} %get-tuple-element.49.cols, ...), custom_call_target="tpu_custom_call" | custom-call | tf_op jit(solution)/shard_map/step/pallas_call | solution.py:550
  52.3 18.4 %all_to_all.40.got = f32[32,8,128]{2,1,0:T(8,128)S(1)} all-to-all(f32[32,8,128]{2,1,0:T(8,128)S(1)} %get-tuple-element.63), channel_id=1, replica_groups=mesh['gx'=32,'gy'=8] {'gx'}, dimensions={0} | all-to-all | bytes 262144 | tf_op jit(solution)/shard_map/all_to_all | solution.py:615
  70.7 1.0 across.5
  71.7 6.1 %all-to-all-start.3 = ((f32[8,8,128]{2,1,0:T(8,128)}), f32[8,8,128]{2,1,0:T(8,128)S(1)}, u32[]{:S(2)}, u32[]{:S(2)}) async-start(f32[8,8,128]{2,1,0:T(8,128)} %get-tuple-element.65), calls=%async_computation.3 | async-start | bytes 65536 | tf_op jit(solution)/shard_map/all_to_all | solution.py:615
  77.8 4.6 %fine.3.short = f32[1056,640]{1,0:T(8,128)} custom-call(bf16[1056,640]{1,0:T(8,128)(2,1)} %get-tuple-element.67.dose, bf16[512,256]{1,0:T(8,128)(2,1)S(1)} %get-tuple-element.57.cols, bf16[3,176,208]{2,1,0:T(8,128)(2,1)S(1)} %get-tuple-element.58.rows), custom_call_target="tpu_custom_call" | custom-call | flops 1146224640 | bytes 4055040 | tf_op jit(solution)/shard_map/fine/pallas_call | solution.py:429
  82.5 4.4 %step.4 = (bf16[1056,640]{1,0:T(8,128)(2,1)}, f32[32,8,128]{2,1,0:T(8,128)S(1)}, f32[128,128]{1,0:T(8,128)S(1)}) custom-call(f32[8,8,128]{2,1,0:T(8,128)S(1)} %all-to-all-done.3.got, f32[128,128]{1,0:T(8,128)S(1)} %get-tuple-element.66.part, f32[296,192]{1,0:T(8,128)S(1)} %get-tuple-element.48.matrix, bf16[128,640]{1,0:T(8,128)(2,1)S(1)} %get-tuple-element.49.cols, ...), custom_call_target="tpu_custom_call" | custom-call | tf_op jit(solution)/shard_map/step/pallas_call | solution.py:550
  86.9 12.4 %all_to_all.41.got = f32[32,8,128]{2,1,0:T(8,128)S(1)} all-to-all(f32[32,8,128]{2,1,0:T(8,128)S(1)} %get-tuple-element.68), channel_id=1, replica_groups=mesh['gx'=32,'gy'=8] {'gx'}, dimensions={0} | all-to-all | bytes 262144 | tf_op jit(solution)/shard_map/all_to_all | solution.py:615
  100.3 6.4 %all-to-all-start.5 = ((f32[8,8,128]{2,1,0:T(8,128)}), f32[8,8,128]{2,1,0:T(8,128)S(1)}, u32[]{:S(2)}, u32[]{:S(2)}) async-start(f32[8,8,128]{2,1,0:T(8,128)} %get-tuple-element.70), calls=%async_computation.5 | async-start | bytes 65536 | tf_op jit(solution)/shard_map/all_to_all | solution.py:615
  106.7 4.6 %fine.4.short = f32[1056,640]{1,0:T(8,128)} custom-call(bf16[1056,640]{1,0:T(8,128)(2,1)} %get-tuple-element.72.dose, bf16[512,256]{1,0:T(8,128)(2,1)S(1)} %get-tuple-element.57.cols, bf16[3,176,208]{2,1,0:T(8,128)(2,1)S(1)} %get-tuple-element.58.rows), custom_call_target="tpu_custom_call" | custom-call | flops 1146224640 | bytes 4055040 | tf_op jit(solution)/shard_map/fine/pallas_call | solution.py:429
  111.4 4.4 %step.5 = (bf16[1056,640]{1,0:T(8,128)(2,1)}, f32[32,8,128]{2,1,0:T(8,128)S(1)}, f32[128,128]{1,0:T(8,128)S(1)}) custom-call(f32[8,8,128]{2,1,0:T(8,128)S(1)} %all-to-all-done.5.got, f32[128,128]{1,0:T(8,128)S(1)} %get-tuple-element.71.part, f32[296,192]{1,0:T(8,128)S(1)} %get-tuple-element.48.matrix, bf16[128,640]{1,0:T(8,128)(2,1)S(1)} %get-tuple-element.49.cols, ...), custom_call_target="tpu_custom_call" | custom-call | tf_op jit(solution)/shard_map/step/pallas_call | solution.py:550
  115.8 12.4 %all_to_all.42.got = f32[32,8,128]{2,1,0:T(8,128)S(1)} all-to-all(f32[32,8,128]{2,1,0:T(8,128)S(1)} %get-tuple-element.73), channel_id=1, replica_groups=mesh['gx'=32,'gy'=8] {'gx'}, dimensions={0} | all-to-all | bytes 262144 | tf_op jit(solution)/shard_map/all_to_all | solution.py:615
  129.2 6.4 %all-to-all-start.7 = ((f32[8,8,128]{2,1,0:T(8,128)}), f32[8,8,128]{2,1,0:T(8,128)S(1)}, u32[]{:S(2)}, u32[]{:S(2)}) async-start(f32[8,8,128]{2,1,0:T(8,128)} %get-tuple-element.75), calls=%async_computation.7 | async-start | bytes 65536 | tf_op jit(solution)/shard_map/all_to_all | solution.py:615
  135.6 4.1 %fine.5.short = f32[1024,512]{1,0:T(8,128)} custom-call(bf16[1056,640]{1,0:T(8,128)(2,1)} %get-tuple-element.78.dose, bf16[512,256]{1,0:T(8,128)(2,1)S(1)} %get-tuple-element.57.cols, bf16[3,176,208]{2,1,0:T(8,128)(2,1)S(1)} %get-tuple-element.58.rows), custom_call_target="tpu_custom_call" | custom-call | flops 1146224640 | bytes 4055040 | tf_op jit(solution)/shard_map/fine/pallas_call | solution.py:429
  140.3 2.9 %finish.1 = f32[1024,512]{1,0:T(8,128)} custom-call(f32[8,8,128]{2,1,0:T(8,128)S(1)} %all-to-all-done.7.got, f32[128,128]{1,0:T(8,128)S(1)} %get-tuple-element.76.part, f32[392,192]{1,0:T(8,128)S(1)} %get-tuple-element.77.matrix, bf16[128,640]{1,0:T(8,128)(2,1)S(1)} %get-tuple-element.49.cols, bf16[1056,640]{1,0:T(8,128)(2,1)} %get-tuple-element.78.dose, ...), custom_call_target="tpu_custom_call" | custom-call | tf_op jit(solution)/shard_map/finish/pallas_call | solution.py:591
  (20 shorter events, 7.2 us)
Async XLA Ops:
  0.8 0.9 copy-start
  1.7 0.8 copy-start.1
  2.4 0.7 copy-start.2
  3.1 0.7 copy-start.3
  9.6 27.5 %all-to-all-start = ((f32[32,8,128]{2,1,0:T(8,128)}), f32[32,8,128]{2,1,0:T(8,128)S(1)}, u32[]{:S(2)}, u32[]{:S(2)}) async-start(f32[32,8,128]{2,1,0:T(8,128)} %get-tuple-element.42), calls=%async_computation | async-start | bytes 262144 | tf_op jit(solution)/shard_map/all_to_all | solution.py:615
  21.5 4.4 %collective-permute-start = (bf16[16,1024]{1,0:T(8,128)(2,1)S(1)}, bf16[16,1024]{1,0:T(8,128)(2,1)S(1)}, u32[]{:S(2)}, u32[]{:S(2)}) collective-permute-start(bf16[16,1024]{1,0:T(8,128)(2,1)S(1)} %get-tuple-element.51), channel_id=1, source_target_pairs={{0,8},{8,16},{16,24},{24,32},{32,40},{40,48},{48,56},{56,64},{64,7... | collective-permute-start | bytes 98312 | tf_op jit(solution)/shard_map/ppermute | solution.py:611
  24.6 5.0 %collective-permute-start.1 = (bf16[16,1024]{1,0:T(8,128)(2,1)S(1)}, bf16[16,1024]{1,0:T(8,128)(2,1)S(1)}, u32[]{:S(2)}, u32[]{:S(2)}) collective-permute-start(bf16[16,1024]{1,0:T(8,128)(2,1)S(1)} %get-tuple-element.52), channel_id=1, source_target_pairs={{8,0},{16,8},{24,16},{32,24},{40,32},{48,40},{56,48},{64,56},{72,6... | collective-permute-start | bytes 98312 | tf_op jit(solution)/shard_map/ppermute | solution.py:611
  29.7 13.4 %collective-permute-start.2 = (bf16[16,640]{1,0:T(8,128)(2,1)S(1)}, bf16[16,640]{1,0:T(8,128)(2,1)S(1)}, u32[]{:S(2)}, u32[]{:S(2)}) collective-permute-start(bf16[16,640]{1,0:T(8,128)(2,1)S(1)} %get-tuple-element.55), channel_id=1, source_target_pairs={{0,1},{1,2},{2,3},{3,4},{4,5},{5,6},{6,7},{8,9},{9,10},{10,11},{11... | collective-permute-start | bytes 61448 | tf_op jit(solution)/shard_map/ppermute | solution.py:611
  35.2 8.0 %collective-permute-start.3 = (bf16[16,640]{1,0:T(8,128)(2,1)S(1)}, bf16[16,640]{1,0:T(8,128)(2,1)S(1)}, u32[]{:S(2)}, u32[]{:S(2)}) collective-permute-start(bf16[16,640]{1,0:T(8,128)(2,1)S(1)} %get-tuple-element.56), channel_id=1, source_target_pairs={{1,0},{2,1},{3,2},{4,3},{5,4},{6,5},{7,6},{9,8},{10,9},{11,10},{12... | collective-permute-start | bytes 61448 | tf_op jit(solution)/shard_map/ppermute | solution.py:611
  38.2 9.7 %all-to-all-start.1 = ((f32[8,8,128]{2,1,0:T(8,128)}), f32[8,8,128]{2,1,0:T(8,128)S(1)}, u32[]{:S(2)}, u32[]{:S(2)}) async-start(f32[8,8,128]{2,1,0:T(8,128)} %get-tuple-element.46), calls=%async_computation.1 | async-start | bytes 65536 | tf_op jit(solution)/shard_map/all_to_all | solution.py:615
  71.7 10.8 %all-to-all-start.3 = ((f32[8,8,128]{2,1,0:T(8,128)}), f32[8,8,128]{2,1,0:T(8,128)S(1)}, u32[]{:S(2)}, u32[]{:S(2)}) async-start(f32[8,8,128]{2,1,0:T(8,128)} %get-tuple-element.65), calls=%async_computation.3 | async-start | bytes 65536 | tf_op jit(solution)/shard_map/all_to_all | solution.py:615
  100.3 11.1 %all-to-all-start.5 = ((f32[8,8,128]{2,1,0:T(8,128)}), f32[8,8,128]{2,1,0:T(8,128)S(1)}, u32[]{:S(2)}, u32[]{:S(2)}) async-start(f32[8,8,128]{2,1,0:T(8,128)} %get-tuple-element.70), calls=%async_computation.5 | async-start | bytes 65536 | tf_op jit(solution)/shard_map/all_to_all | solution.py:615
  129.2 11.1 %all-to-all-start.7 = ((f32[8,8,128]{2,1,0:T(8,128)}), f32[8,8,128]{2,1,0:T(8,128)S(1)}, u32[]{:S(2)}, u32[]{:S(2)}) async-start(f32[8,8,128]{2,1,0:T(8,128)} %get-tuple-element.75), calls=%async_computation.7 | async-start | bytes 65536 | tf_op jit(solution)/shard_map/all_to_all | solution.py:615

commit v2 on v1

v2 whole, which is shorter than its diff:
```python
import functools

import jax
import jax.numpy as jnp
import ml_dtypes
import numpy as np
from jax import lax
from jax.experimental import pallas as pl
from jax.experimental.pallas import tpu as pltpu
from jax.sharding import PartitionSpec as P

HW = 4
CLASSES = 8
SB = 128
ITERS = 4
NX, NY = 32, 8
TR, TC = 1024, 512
HALO = HW * ITERS
ER = TR + 2 * HALO
EC = TC + 128
BLK = 176
NB = ER // BLK
QC, QR = 36, 68
F32, BF16 = jnp.float32, jnp.bfloat16
EXACT = lax.Precision.HIGHEST


def gauss_taps():
    offsets = np.arange(-HW, HW + 1).astype(np.float32)
    weights = np.exp(-(offsets * offsets) / np.float32(HW * HW)).astype(np.float32)
    return weights / weights.sum(dtype=np.float32)


def blur_operator(n):
    taps = gauss_taps().astype(np.float64)
    out = np.zeros((n, n))
    for k in range(-HW, HW + 1):
        out += taps[k + HW] * np.eye(n, k=k)
    return out


def up_operator(n, factor):
    target = np.arange(n * factor)
    lower = (target - factor // 2) // factor
    t = (target - factor // 2 - factor * lower + 0.5) / factor
    out = np.zeros((n * factor, n))
    np.add.at(out, (target, np.clip(lower, 0, n - 1)), 1 - t)
    np.add.at(out, (target, np.clip(lower + 1, 0, n - 1)), t)
    return out


def level_operators(n_second):
    third, fourth = n_second // 4, n_second // 16
    return (
        blur_operator(n_second),
        up_operator(third, 4) @ blur_operator(third),
        up_operator(third, 4) @ up_operator(fourth, 4) @ blur_operator(fourth),
    )


@functools.cache
def column_matrices():
    second, third, fourth = level_operators(NX * 32)
    got = np.zeros((NX, 128, 256), np.float32)
    own = np.zeros((NX, 128, 32), np.float32)
    for px in range(NX):
        for q in range(QC):
            g = min(max(32 * px + q - 2, 0), NX * 32 - 1)
            for s in np.nonzero(second[g])[0]:
                p, j = divmod(int(s), 32)
                if p == px:
                    own[px, q, j] = second[g, s]
                else:
                    assert j >= 24 if p < px else j < 8
                    got[px, q, p * 8 + j % 8] = second[g, s]
            got[px, 40 + q] = third[g]
            for j in range(2):
                got[px, 80 + q, j::8] = fourth[g, j::2]
        got[px, 120, 0::8] = 1
        got[px, 120, 1::8] = 1
    return got, own


def row_matrices(groups, first, step, length):
    second, third, fourth = level_operators(NY * 64)
    m = 16 * groups
    out = np.zeros((NY, 3 * m + 8, 192), np.float32)
    for py in range(NY):
        for b in range(groups):
            for k in range(length):
                row, q = b * 16 + k, first + step * b + k
                g = min(max(64 * py + q - 2, 0), NY * 64 - 1)
                for s in np.nonzero(second[g])[0]:
                    p, j = divmod(int(s), 64)
                    assert p == py or (j >= 56 if p < py else j < 8)
                    out[py, row, 64 + j if p == py else p * 8 + j % 8] = second[g, s]
                for s in np.nonzero(third[g])[0]:
                    p, j = divmod(int(s), 16)
                    assert p == py or (j >= 8 if p < py else j < 8)
                    out[py, m + row, 128 + j if p == py else p * 8 + j % 8] = third[g, s]
                for s in np.nonzero(fourth[g])[0]:
                    p, j = divmod(int(s), 4)
                    out[py, 2 * m + row, p * 8 + j] = fourth[g, s]
        out[py, 3 * m, 4:64:8] = 1
    return out


@functools.cache
def column_spread():
    out = np.zeros((128, EC), np.float32)
    for lane in range(EC):
        cell = lane if lane < TC + HALO else lane - EC
        if cell < -HALO:
            continue
        lower = (cell - 8) // 16
        t = (cell - 8 - 16 * lower + 0.5) / 16
        for level in range(3):
            out[40 * level + lower + 2, lane] += 1 - t
            out[40 * level + lower + 3, lane] += t
        out[120, lane] = 1
    return out.astype(ml_dtypes.bfloat16)


@functools.cache
def column_pool(lanes):
    out = np.zeros((lanes, 128), np.float32)
    cell = np.arange(TC)
    out[cell, cell // 16] = 1
    out[cell, 32 + cell // 64] = 1
    out[cell, 40 + cell // 256] = 1
    return out.astype(ml_dtypes.bfloat16)


@functools.cache
def row_pool(groups, stride, real, first):
    out = np.zeros((128, groups * stride), np.float32)
    for b in range(groups):
        for k in range(real):
            s = b * real + k - first
            if 0 <= s < TR // 16:
                at = b * stride + k
                out[s, at] = 2.0**-8
                out[64 + s // 4, at] = 2.0**-12
                out[80 + s // 16, at] = 2.0**-16
                out[84, at] = 1.0 / (TR * NY * TC * NX)
    return out.astype(ml_dtypes.bfloat16)


def fine_taps():
    return gauss_taps().astype(ml_dtypes.bfloat16)


@functools.cache
def fine_columns():
    out = np.zeros((512, 256), ml_dtypes.bfloat16)
    taps, lane = fine_taps(), np.arange(256)
    for k in range(-HW, HW + 1):
        out[lane + 128 + k, lane] = taps[k + HW]
    return out


@functools.cache
def fine_rows():
    out = np.zeros((3, BLK, BLK + 32), ml_dtypes.bfloat16)
    taps = fine_taps()
    for which in range(3):
        for r in range(BLK):
            for k in range(-HW, HW + 1):
                c = r + 16 * which + k
                if 0 <= c < BLK + 32:
                    out[which, r, c] = taps[k + HW]
    return out


VMEM = pl.BlockSpec(memory_space=pltpu.VMEM)
SMEM = pl.BlockSpec(memory_space=pltpu.SMEM)
HBM = pl.BlockSpec(memory_space=pl.ANY)
DMA = pltpu.SemaphoreType.DMA


def params(mib=24):
    return pltpu.CompilerParams(vmem_limit_bytes=mib * 2**20)


def near(x):
    return pltpu.with_memory_space_constraint(x, pltpu.VMEM)


def far(x):
    return pltpu.with_memory_space_constraint(x, pltpu.HBM)


def dot(a, b, **kw):
    return jnp.dot(a, b, preferred_element_type=F32, **kw)


def pieces(x):
    first = x.astype(BF16)
    rest = x - first.astype(F32)
    second = rest.astype(BF16)
    return first, second, (rest - second.astype(F32)).astype(BF16)


def pooled_out(sums, row_pool_ref, px, send_ref, own_ref):
    a, b, c = pieces(sums)
    rows = row_pool_ref[...]
    pooled = (dot(rows, a) + dot(rows, b) + dot(rows, c)).T
    own_ref[...] = pooled
    lane = lax.broadcasted_iota(jnp.int32, (8, 128), 1)
    coarse = jnp.where(lane < 80, pooled[32:40], pooled[40:48])
    left = jnp.where(lane < 64, pooled[0:8], coarse)
    right = jnp.where(lane < 64, pooled[24:32], coarse)
    for p in range(NX):
        send_ref[p] = jnp.where(p < px, left, right)


def start_kernel(table, exps, classes, gain, cpool_far, rpool_far, dose, lo, hi, send, own, *scratch):
    cbuf, gbuf, cpool, rpool, sums, csem, gsem, tsem = scratch
    steps = TR // SB
    loads = []
    for i in range(steps):
        rows = pl.ds(i * SB, SB)
        loads.append(
            (
                pltpu.make_async_copy(classes.at[rows], cbuf.at[rows], csem.at[i]),
                pltpu.make_async_copy(gain.at[rows], gbuf.at[rows], gsem.at[i]),
            )
        )
        for copy in loads[-1]:
            copy.start()
    tables = (
        pltpu.make_async_copy(cpool_far, cpool, tsem.at[0]),
        pltpu.make_async_copy(rpool_far, rpool, tsem.at[1]),
    )
    for copy in tables:
        copy.start()
    for i in range(steps):
        for copy in loads[i]:
            copy.wait()
        rows = slice(i * SB, (i + 1) * SB)
        for k in range(TC // SB):
            e = exps[i, k]
            scale = jnp.where(e > 0, 2.0, jnp.where(e < 0, 0.5, 1.0)).astype(F32)
            at = slice(k * SB, (k + 1) * SB)
            c = cbuf[rows, at]
            level = jnp.zeros((SB, SB), F32)
            for j in range(1, CLASSES):
                level = jnp.where(c == j, table[j] * scale, level)
            value = (level * gbuf[rows, at].astype(F32)).astype(BF16)
            dose[rows, at] = value
            if k == 0:
                lo[:, rows] = value.astype(F32).T[:HALO].astype(BF16)
            if k == TC // SB - 1:
                hi[:, rows] = value.astype(F32).T[SB - HALO :].astype(BF16)
        if i == 0:
            for copy in tables:
                copy.wait()
        across = dot(dose[rows], cpool[...])
        sums[8 * i : 8 * i + 8] = jnp.sum(across.reshape(8, 16, 128), axis=1)
    pooled_out(sums[...], rpool, lax.axis_index("gx"), send, own)


def start(table, exps, classes, gain):
    steps = TR // SB
    return pl.pallas_call(
        start_kernel,
        in_specs=[SMEM, SMEM] + [HBM] * 4,
        out_specs=[VMEM] * 5,
        out_shape=[
            pltpu.VMEM((TR, TC), BF16),
            pltpu.VMEM((HALO, TR), BF16),
            pltpu.VMEM((HALO, TR), BF16),
            pltpu.VMEM((NX, 8, 128), F32),
            pltpu.VMEM((128, 128), F32),
        ],
        scratch_shapes=[
            pltpu.VMEM((TR, TC), jnp.int32),
            pltpu.VMEM((TR, TC), BF16),
            pltpu.VMEM((TC, 128), BF16),
            pltpu.VMEM((128, TR // 16), BF16),
            pltpu.VMEM((TR // 16, 128), F32),
            DMA((steps,)),
            DMA((steps,)),
            DMA((2,)),
        ],
        compiler_params=params(),
        name="start",
    )(far(table), far(exps), far(classes), far(gain), far(jnp.asarray(column_pool(TC))), far(jnp.asarray(row_pool(8, 8, 8, 0))))


def operators():
    mgot, mown = column_matrices()
    return [
        (row_matrices(NB, 0, BLK // 16, BLK // 16 + 2), 1),
        (mgot, 0),
        (mown, 0),
        (column_spread(), None),
        (column_pool(EC), None),
        (row_pool(NB, 16, BLK // 16, 1), None),
        (fine_rows(), None),
    ]


def weighted(ref, weights, m):
    for level in range(3):
        at = slice(m * level, m * (level + 1))
        ref[at] = ref[at] * weights[level]
    ref[3 * m :] = ref[3 * m :] * weights[2]


def pick_kernel(picks, after, weights, *refs):
    n = len(picks)
    tables, outs, sems = refs[:n], refs[n : 2 * n], refs[-1]
    place = lax.axis_index("gx"), lax.axis_index("gy")
    copies = []
    for i, pick in enumerate(picks):
        source = tables[i] if pick is None else tables[i].at[place[pick]]
        copies.append(pltpu.make_async_copy(source, outs[i], sems.at[i]))
        copies[-1].start()
    for copy in copies:
        copy.wait()
    weighted(outs[0], weights, 16 * NB)


def pick(after, weights):
    made = operators()
    picks = [at for _, at in made]
    outs = [pltpu.VMEM(t.shape if at is None else t.shape[1:], t.dtype) for t, at in made]
    return pl.pallas_call(
        functools.partial(pick_kernel, picks),
        in_specs=[HBM, SMEM] + [HBM] * len(made),
        out_specs=[VMEM] * len(made),
        out_shape=outs,
        scratch_shapes=[DMA((len(made),))],
        compiler_params=params(),
        name="pick",
    )(near(after), far(weights), *[far(jnp.asarray(t)) for t, _ in made])


def side(strip_lo, strip_hi):
    rows = strip_lo.shape[1]
    empty = jnp.zeros((rows, 128 - 2 * HALO), F32)
    return jnp.concatenate([strip_hi.astype(F32).T, empty, strip_lo.astype(F32).T], axis=1)


def across_kernel(first, *refs):
    if first:
        tile, lo, hi, got, own, mgot, mown, send, part = refs
    else:
        _, got, own, mgot, mown, send, part = refs
    received = got[...].reshape(NX * 8, 128)
    z = dot(mgot[...], received, precision=EXACT) + dot(mown[...], own[:32], precision=EXACT)
    z = z.T
    part[...] = z
    lane = lax.broadcasted_iota(jnp.int32, (8, 128), 1)
    coarse = z[80:88]
    up = jnp.where(lane < 40, z[0:8], jnp.where(lane < 80, z[64:72], coarse))
    down = jnp.where(lane < 40, z[56:64], jnp.where(lane < 80, z[72:80], coarse))
    py = lax.axis_index("gy")
    for p in range(NY):
        send[p, :8] = jnp.where(p < py, up, down)
    if first:
        for n in range(EC // 128):
            lanes = slice(128 * n, 128 * n + 128)
            if n < TC // 128:
                top, bottom = tile[:HALO, lanes].astype(F32), tile[TR - HALO :, lanes].astype(F32)
            else:
                top = side(lo[:, :128], hi[:, :128])[:HALO]
                bottom = side(lo[:, TR - 128 :], hi[:, TR - 128 :])[128 - HALO :]
            for p in range(NY):
                send[p, 8 + HALO * n : 8 + HALO * (n + 1)] = jnp.where(p < py, top, bottom)


def across(first, extra, got, own, ops):
    count = 8 + HALO * (EC // 128) if first else 8
    specs = [VMEM] * 3 if first else [HBM]
    return pl.pallas_call(
        functools.partial(across_kernel, first),
        in_specs=specs + [VMEM] * 4,
        out_specs=[VMEM] * 2,
        out_shape=[pltpu.VMEM((NY, count, 128), F32), pltpu.VMEM((128, 128), F32)],
        compiler_params=params(),
        name="across",
    )(*([near(x) for x in extra] if first else [far(x) for x in extra]), near(got), near(own), near(ops[1]), near(ops[2]))


def column_pass(block, cols, half, at):
    tile = [block[:, 128 * n : 128 * (n + 1)] for n in range(EC // 128)]
    join = lambda *which: jnp.concatenate([tile[n] for n in which], axis=1)
    half[at, :256] = dot(join(4, 0, 1, 2), cols[...]).astype(BF16)
    half[at, 256:512] = dot(join(1, 2, 3, 4), cols[...]).astype(BF16)
    if half.shape[1] > TC:
        half[at, 512:] = dot(join(3, 4, 0), cols[:384, :128]).astype(BF16)


def first_half_kernel(tile, lo, hi, cols_far, half_far, dose_far, half, dose, cols, sems, csem):
    load = pltpu.make_async_copy(cols_far, cols, csem)
    load.start()
    stores = []
    for n in range(TR // SB):
        rows, begin = slice(n * SB, (n + 1) * SB), HALO + n * SB
        dose[begin : begin + SB, :TC] = tile[rows]
        dose[begin : begin + SB, TC:] = side(lo[:, rows], hi[:, rows]).astype(BF16)
        if n == 0:
            load.wait()
        column_pass(dose[begin : begin + SB], cols, half, slice(begin, begin + SB))
        at = pl.ds(begin, SB)
        stores.append(pltpu.make_async_copy(half.at[at], half_far.at[at], sems.at[0, n]))
        stores[-1].start()
        stores.append(pltpu.make_async_copy(dose.at[at], dose_far.at[at], sems.at[1, n]))
        stores[-1].start()
    for copy in stores:
        copy.wait()


def half_cost():
    return pl.CostEstimate(flops=4 * ER * EC * EC, bytes_accessed=6 * ER * EC, transcendentals=0)


def first_half(tile, lo, hi):
    return pl.pallas_call(
        first_half_kernel,
        in_specs=[VMEM] * 3 + [HBM],
        out_specs=[HBM, HBM],
        out_shape=[pltpu.HBM((ER, EC), BF16)] * 2,
        scratch_shapes=[
            pltpu.VMEM((ER, EC), BF16),
            pltpu.VMEM((ER, EC), BF16),
            pltpu.VMEM((512, 256), BF16),
            DMA((2, TR // SB)),
            DMA,
        ],
        compiler_params=params(),
        cost_estimate=half_cost(),
        name="first_half",
    )(near(tile), near(lo), near(hi), far(jnp.asarray(fine_columns())))


def half_kernel(dose, cols_far, half_far, half, cols, sems, csem):
    load = pltpu.make_async_copy(cols_far, cols, csem)
    load.start()
    load.wait()
    stores = []
    for b in range(NB):
        column_pass(dose[b * BLK : (b + 1) * BLK], cols, half, slice(b * BLK, (b + 1) * BLK))
        at = pl.ds(b * BLK, BLK)
        stores.append(pltpu.make_async_copy(half.at[at], half_far.at[at], sems.at[b]))
        stores[-1].start()
    for copy in stores:
        copy.wait()


def half_of(dose, lanes):
    return pl.pallas_call(
        half_kernel,
        in_specs=[VMEM, HBM],
        out_specs=HBM,
        out_shape=pltpu.HBM((ER, lanes), BF16),
        scratch_shapes=[pltpu.VMEM((ER, lanes), BF16), pltpu.VMEM((512, 256), BF16), DMA((NB,)), DMA],
        compiler_params=params(),
        cost_estimate=half_cost(),
        name="half",
    )(near(dose), far(jnp.asarray(fine_columns())))


def spread(received, part, matrix, cols, groups):
    m = 16 * groups
    y = dot(matrix[...], jnp.concatenate([received, part[...]], axis=0), precision=EXACT)
    lane = lax.broadcasted_iota(jnp.int32, (m, 128), 1)
    fourth = jnp.where(lane < 120, y[2 * m : 3 * m], jnp.where(lane == 120, y[3 * m : 3 * m + 1], 0.0))
    a, b, c = pieces(jnp.where(lane < 40, y[:m], jnp.where(lane < 80, y[m : 2 * m], fourth)))
    return dot(a, cols) + dot(b, cols) + dot(c, cols)


def short_range(b, rows, half):
    begin = min(max(b * BLK - 16, 0), ER - BLK - 32)
    return dot(rows[(b * BLK - begin) // 16], half[begin : begin + BLK + 32])


def update(b, old_rows, short, grid, out, skip):
    count, lanes = out.shape
    t = (lax.broadcasted_iota(jnp.int32, (8, lanes), 0).astype(F32) + 0.5) / 16.0
    for n in range(BLK // 16):
        row = b * BLK + 16 * n
        if not skip <= row < skip + count:
            continue
        a, m, c = (grid[16 * b + n + k : 16 * b + n + k + 1] for k in range(3))
        back = jnp.concatenate([a + (t + 0.5) * (m - a), m + t * (c - m)], axis=0)
        full = 1.0 + (short[16 * n : 16 * n + 16] + back)
        out[row - skip : row - skip + 16] = (old_rows(row).astype(F32) * 2.0 / full).astype(out.dtype)


def step_kernel(first, got, part, matrix, cols, dose, half, rows, cpool, rpool, *refs):
    if first:
        fcols_far, out, send, own, hbuf, grid, sums, lsem, dbuf, fcols, dsem, fsem = refs
        fetch = pltpu.make_async_copy(fcols_far, fcols, fsem)
        fetch.start()
    else:
        out, send, own, hbuf, grid, sums, lsem = refs
        dbuf = dose
    loads = []
    for b in range(NB):
        begin, end = b * BLK, (b + 1) * BLK
        if first:
            begin, end = max(begin, HALO), min(end, ER - HALO)
        at = pl.ds(begin, end - begin)
        loads.append([pltpu.make_async_copy(half.at[at], hbuf.at[at], lsem.at[b])])
        if first:
            loads[-1].append(pltpu.make_async_copy(dose.at[at], dbuf.at[at], dsem.at[b]))
        for copy in loads[-1]:
            copy.start()
    received = got[:, :8].reshape(NY * 8, 128)
    grid[...] = spread(received, part, matrix, cols[...], NB)
    if first:
        py = lax.axis_index("gy")
        fetch.wait()
        for row, p, real in ((0, jnp.maximum(py - 1, 0), py > 0), (ER - HALO, jnp.minimum(py + 1, NY - 1), py < NY - 1)):
            tiles = [got[p, 8 + HALO * n : 8 + HALO * (n + 1)] for n in range(EC // 128)]
            values = jnp.where(real, jnp.concatenate(tiles, axis=1), 0.0).astype(BF16)
            dbuf[row : row + HALO] = values
            column_pass(values, fcols, hbuf, slice(row, row + HALO))

    def ready(b):
        for copy in loads[b]:
            copy.wait()

    ready(0)
    for b in range(NB):
        if b + 1 < NB:
            ready(b + 1)
        update(b, lambda row: dbuf[row : row + 16], short_range(b, rows, hbuf), grid, out, 0)
        pooled = dot(out[b * BLK : (b + 1) * BLK], cpool[...])
        pooled = jnp.sum(pooled.reshape(BLK // 16, 16, 128), axis=1)
        sums[16 * b : 16 * b + 16] = jnp.concatenate([pooled, jnp.zeros((16 - BLK // 16, 128), F32)], axis=0)
    pooled_out(sums[...], rpool, lax.axis_index("gx"), send, own)


def step(first, got, part, dose, half, ops):
    scratch = [
        pltpu.VMEM((ER, EC), BF16),
        pltpu.VMEM((NB * 16, EC), F32),
        pltpu.VMEM((NB * 16, 128), F32),
        DMA((NB,)),
    ]
    more = [pltpu.VMEM((ER, EC), BF16), pltpu.VMEM((512, 256), BF16), DMA((NB,)), DMA] if first else []
    return pl.pallas_call(
        functools.partial(step_kernel, first),
        in_specs=[VMEM] * 4 + [HBM if first else VMEM, HBM] + [VMEM] * 3 + ([HBM] if first else []),
        out_specs=[VMEM] * 3,
        out_shape=[
            pltpu.VMEM((ER, EC), BF16),
            pltpu.VMEM((NX, 8, 128), F32),
            pltpu.VMEM((128, 128), F32),
        ],
        scratch_shapes=scratch + more,
        input_output_aliases={} if first else {4: 0},
        compiler_params=params(),
        name="first_step" if first else "step",
    )(
        near(got), near(part), near(ops[0]), near(ops[3]), far(dose) if first else near(dose), far(half),
        near(ops[6]), near(ops[4]), near(ops[5]), *([far(jnp.asarray(fine_columns()))] if first else []),
    )


def finish_kernel(got, part, matrix, cols, dose, half, rows, out, hbuf, made, grid, lsem, ssem):
    loads = []
    for b in range(NB):
        at = pl.ds(b * BLK, BLK)
        loads.append(pltpu.make_async_copy(half.at[at], hbuf.at[at], lsem.at[b]))
        loads[-1].start()
    grid[...] = spread(got[...].reshape(NY * 8, 128), part, matrix, cols[:, :TC], NB)
    stores = []
    loads[0].wait()
    for b in range(NB):
        if b + 1 < NB:
            loads[b + 1].wait()
        update(b, lambda row: dose[row : row + 16, :TC], short_range(b, rows, hbuf), grid, made, HALO)
        begin, end = max(b * BLK - HALO, 0), min((b + 1) * BLK - HALO, TR)
        at = pl.ds(begin, end - begin)
        stores.append(pltpu.make_async_copy(made.at[at], out.at[at], ssem.at[b]))
        stores[-1].start()
    for copy in stores:
        copy.wait()


def finish(got, part, dose, half, ops):
    return pl.pallas_call(
        finish_kernel,
        in_specs=[VMEM] * 5 + [HBM, VMEM],
        out_specs=HBM,
        out_shape=pltpu.HBM((TR, TC), F32),
        scratch_shapes=[
            pltpu.VMEM((ER, TC), BF16),
            pltpu.VMEM((TR, TC), F32),
            pltpu.VMEM((NB * 16, TC), F32),
            DMA((NB,)),
            DMA((NB,)),
        ],
        compiler_params=params(),
        name="finish",
    )(near(got), near(part), near(ops[0]), near(ops[3]), near(dose), far(half), near(ops[6]))


def shifted(x, axis, by):
    n = lax.axis_size(axis)
    return lax.ppermute(x, axis, [(i, i + by) for i in range(n) if 0 <= i + by < n])


def exchanged(x, axis):
    return lax.all_to_all(x, axis, 0, 0, tiled=True)


def local(classes, exponents, gain_field, level_table, level_weights):
    tile, lo, hi, send, own = start(level_table, exponents, classes, gain_field)
    left, right = shifted(hi, "gx", 1), shifted(lo, "gx", -1)
    got = exchanged(send, "gx")
    ops = pick(left, level_weights)
    send, part = across(True, (tile, left, right), got, own, ops)
    got = exchanged(send, "gy")
    half, dose = first_half(tile, left, right)
    dose, send, own = step(True, got, part, dose, half, ops)
    for sweep in range(2, ITERS + 1):
        got = exchanged(send, "gx")
        half = half_of(dose, EC if sweep < ITERS else TC)
        send, part = across(False, (half,), got, own, ops)
        got = exchanged(send, "gy")
        if sweep < ITERS:
            dose, send, own = step(False, got, part, dose, half, ops)
    return finish(got, part, dose, half, ops)


def solution(mesh):
    in_specs = (P("gy", "gx"), P("gy", "gx"), P("gy", "gx"), P(), P())
    return jax.shard_map(local, mesh=mesh, in_specs=in_specs, out_specs=P("gy", "gx"), check_vma=False)
```

time: 144 us -> 137 us (0.951)
  waiting for transfers between devices: 4.99 us -> 26.2 us
  blocking collectives: 43.3 us -> 27.6 us
  starting transfers between devices: 47.6 us -> 39.3 us
  local copies, waits for them, and re-layouts: 3.73 us -> 1.34 us
  Pallas kernels: 43.5 us -> 41.4 us
    all_to_all x5, waiting for transfers between devices: 1.34 us -> 24.6 us  [exchanged(): return lax.all_to_all(x, axis, 0, 0, tiled=True)]
    all_to_all x3, blocking collectives: 43.3 us -> 27.6 us  [exchanged(): return lax.all_to_all(x, axis, 0, 0, tiled=True)]
    ppermute x4 -> x2, starting transfers between devices: 11.8 us -> 4.43 us  [shifted(): lax.ppermute(x, axis, [(i, i + by) for i in range(n) if 0 <= i + by < n])]
    unnamed x9 -> x1, local copies, waits for them, and re-layouts: 3.73 us -> 1.34 us
    pallas_call x14, Pallas kernels: 43.5 us -> 41.4 us  [the longest x3 15.6 us: step(): pl.pallas_call(functools.partial(step_kernel, first), in_specs=[VMEM] * 4...]
    ppermute x4 -> x2, waiting for transfers between devices: 3.65 us -> 1.6 us  [shifted(): lax.ppermute(x, axis, [(i, i + by) for i in range(n) if 0 <= i + by < n])]
  transfers between devices with their start and end apart: 9 -> 7, of which waited for: 5 -> 6; matrix products, arithmetic and copies ran while one was open for 0% -> 0% of each run, Pallas kernels for 13% -> 10%
where the time goes in v2:
time: 137 us; the launch traced here: 136 us
  Pallas kernels  41.4 us (30%)
  starting transfers between devices  39.3 us (29%)
  blocking collectives  27.6 us (20%)
  waiting for transfers between devices  26.2 us (19%)
    all_to_all x5, starting transfers between devices, exchanged(): return lax.all_to_all(x, axis, 0, 0, tiled=True)  34.9 us
    all_to_all x3, blocking collectives, exchanged(): return lax.all_to_all(x, axis, 0, 0, tiled=True)  27.6 us
    all_to_all x5, waiting for transfers between devices, exchanged(): return lax.all_to_all(x, axis, 0, 0, tiled=True)  24.6 us
    pallas_call x3, Pallas kernels, step(): pl.pallas_call(functools.partial(step_kernel, first), in_specs=[VMEM] * 4...  15.6 us
    pallas_call x3, Pallas kernels, half_of(): pl.pallas_call(half_kernel, in_specs=[VMEM, HBM], out_specs=HBM, out_shap...  7.85 us
    pallas_call x1, Pallas kernels, start(): pl.pallas_call(start_kernel, in_specs=[SMEM, SMEM] + [HBM] * 4, out_specs...  6.01 us
    ppermute x2, starting transfers between devices, shifted(): lax.ppermute(x, axis, [(i, i + by) for i in range(n) if 0 <= i + by < n])  4.43 us
    pallas_call x1, Pallas kernels, first_half(): pl.pallas_call(first_half_kernel, in_specs=[VMEM] * 3 + [HBM], out_specs=...  3.8 us
  transfers between devices with their start and end apart: 7, of which 6 were waited for; matrix products, arithmetic and copies ran while one was open for 0% of the time, Pallas kernels for 10%

profile of v2, /device:TPU:1, one launch (start us, length us, event | category | flops | bytes accessed | tf_op | source)
XLA Modules:
  0.0 136.1 jit_solution(14498468999489124501)
XLA Ops:
  1.3 6.0 %start.1 = (bf16[1024,512]{1,0:T(8,128)(2,1)S(1)}, bf16[16,1024]{1,0:T(8,128)(2,1)S(1)}, bf16[16,1024]{1,0:T(8,128)(2,1)S(1)}, f32[32,8,128]{2,1,0:T(8,128)}, f32[128,128]{1,0:T(8,128)S(1)}) custom-call(f32[8]{0:T(128)} %table.1, s32[8,4]{1,0:T(8,128)} %copy.18.exps, s32[1024,512]{1,0:T(8,128)} %classes.1, bf16[1024,512]{1,0:T(8,128)(2,1)} %gain.1, ...), custom_call_target="tpu_custom_call" | custom-call | tf_op jit(solution)/shard_map/start/pallas_call | solution.py:265
  7.4 11.9 %all-to-all-start = ((f32[32,8,128]{2,1,0:T(8,128)}), f32[32,8,128]{2,1,0:T(8,128)S(1)}, u32[]{:S(2)}, u32[]{:S(2)}) async-start(f32[32,8,128]{2,1,0:T(8,128)} %get-tuple-element.39), calls=%async_computation | async-start | bytes 262144 | tf_op jit(solution)/shard_map/all_to_all | solution.py:610
  19.2 3.1 %collective-permute-start = (bf16[16,1024]{1,0:T(8,128)(2,1)S(1)}, bf16[16,1024]{1,0:T(8,128)(2,1)S(1)}, u32[]{:S(2)}, u32[]{:S(2)}) collective-permute-start(bf16[16,1024]{1,0:T(8,128)(2,1)S(1)} %get-tuple-element.37), channel_id=1, source_target_pairs={{0,8},{8,16},{16,24},{24,32},{32,40},{40,48},{48,56},{56,64},{64,7... | collective-permute-start | bytes 98312 | tf_op jit(solution)/shard_map/ppermute | solution.py:606
  23.7 2.0 %pick.1 = (f32[296,192]{1,0:T(8,128)S(1)}, f32[128,256]{1,0:T(8,128)S(1)}, f32[128,32]{1,0:T(8,128)S(1)}, bf16[128,640]{1,0:T(8,128)(2,1)S(1)}, bf16[640,128]{1,...) custom-call(bf16[16,1024]{1,0:T(8,128)(2,1)S(1)} %collective-permute-done.after.refs_1_.lo, ...), custom_call_target="tpu_custom_call" | custom-call | tf_op jit(solution)/shard_map/pick/pallas_call | solution.py:329
  25.7 1.6 %collective-permute-done.1.refs_2_.hi = bf16[16,1024]{1,0:T(8,128)(2,1)S(1)} collective-permute-done((bf16[16,1024]{1,0:T(8,128)(2,1)S(1)}, bf16[16,1024]{1,0:T(8,128)(2,1)S(1)}, u32[]{:S(2)}, u32[]{:S(2)}) %collective-permute-start.1) | collective-permute-done | bytes 32800 | tf_op jit(solution)/shard_map/ppermute | solution.py:606
  29.6 6.8 %all-to-all-start.1 = ((f32[8,88,128]{2,1,0:T(8,128)}), f32[8,88,128]{2,1,0:T(8,128)S(1)}, u32[]{:S(2)}, u32[]{:S(2)}) async-start(f32[8,88,128]{2,1,0:T(8,128)} %get-tuple-element.43), calls=%async_computation.1 | async-start | bytes 720896 | tf_op jit(solution)/shard_map/all_to_all | solution.py:610
  36.3 3.8 %first_half.1 = (bf16[1056,640]{1,0:T(8,128)(2,1)}, bf16[1056,640]{1,0:T(8,128)(2,1)}) custom-call(bf16[1024,512]{1,0:T(8,128)(2,1)S(1)} %get-tuple-element.36.refs_0_.tile, bf16[16,1024]{1,0:T(8,128)(2,1)S(1)} %collective-permute-done.after.refs_1_.lo, bf16[16,1024]{1,0:T(8,128)(2,1)S(1)} %collective-permute-done.1.refs_2_.hi, ...), custom_call_target="tpu_custom_call" | custom-call | flops 1730150400 | bytes 4055040 | tf_op jit(solution)/shard_map/first_half/pallas_call | solution.py:421
  40.1 3.9 %all-to-all-done.1.got = f32[8,88,128]{2,1,0:T(8,128)S(1)} async-done(((f32[8,88,128]{2,1,0:T(8,128)}), f32[8,88,128]{2,1,0:T(8,128)S(1)}, u32[]{:S(2)}, u32[]{:S(2)}) %all-to-all-start.1) | async-done | bytes 360480 | tf_op jit(solution)/shard_map/all_to_all | solution.py:610
  44.1 5.3 %first_step.1 = (bf16[1056,640]{1,0:T(8,128)(2,1)S(1)}, f32[32,8,128]{2,1,0:T(8,128)}, f32[128,128]{1,0:T(8,128)S(1)}) custom-call(f32[8,88,128]{2,1,0:T(8,128)S(1)} %all-to-all-done.1.got, f32[128,128]{1,0:T(8,128)S(1)} %get-tuple-element.44.part, f32[296,192]{1,0:T(8,128)S(1)} %get-tuple-element.45.matrix, bf16[128,640]{1,0:T(8,128)(2,1)S(1)} %get-tuple-element.46.cols, ...), custom_call_target="tpu_custom_call" | custom-call | tf_op jit(solution)/shard_map/first_step/pallas_call | solution.py:546
  49.4 8.5 %all-to-all-start.2 = ((f32[32,8,128]{2,1,0:T(8,128)}), f32[32,8,128]{2,1,0:T(8,128)S(1)}, u32[]{:S(2)}, u32[]{:S(2)}) async-start(f32[32,8,128]{2,1,0:T(8,128)} %get-tuple-element.53), calls=%async_computation.2 | async-start | bytes 262144 | tf_op jit(solution)/shard_map/all_to_all | solution.py:610
  57.9 2.7 %half.3.refs_0_ = bf16[1056,640]{1,0:T(8,128)(2,1)} custom-call(bf16[1056,640]{1,0:T(8,128)(2,1)S(1)} %get-tuple-element.52.dose, bf16[512,256]{1,0:T(8,128)(2,1)} %constant.29.clone.cols_far.refs_0_), custom_call_target="tpu_custom_call" | custom-call | flops 1730150400 | bytes 4055040 | tf_op jit(solution)/shard_map/half/pallas_call | solution.py:454
  60.6 6.4 %all-to-all-done.2.refs_1_ = f32[32,8,128]{2,1,0:T(8,128)S(1)} async-done(((f32[32,8,128]{2,1,0:T(8,128)}), f32[32,8,128]{2,1,0:T(8,128)S(1)}, u32[]{:S(2)}, u32[]{:S(2)}) %all-to-all-start.2) | async-done | bytes 131104 | tf_op jit(solution)/shard_map/all_to_all | solution.py:610
  67.4 9.4 %all_to_all.40.got = f32[8,8,128]{2,1,0:T(8,128)S(1)} all-to-all(f32[8,8,128]{2,1,0:T(8,128)S(1)} %get-tuple-element.55), channel_id=1, replica_groups=mesh['gx'=32,'gy'=8] {'gy'}, dimensions={0} | all-to-all | bytes 65536 | tf_op jit(solution)/shard_map/all_to_all | solution.py:610
  76.8 5.2 %step.2 = (bf16[1056,640]{1,0:T(8,128)(2,1)S(1)}, f32[32,8,128]{2,1,0:T(8,128)}, f32[128,128]{1,0:T(8,128)S(1)}) custom-call(f32[8,8,128]{2,1,0:T(8,128)S(1)} %all_to_all.40.got, f32[128,128]{1,0:T(8,128)S(1)} %get-tuple-element.56.part, f32[296,192]{1,0:T(8,128)S(1)} %get-tuple-element.45.matrix, ...), custom_call_target="tpu_custom_call", output_to_operand_aliasing={{0}: (4, {})} | custom-call | tf_op jit(solution)/shard_map/step/pallas_call | solution.py:546
  81.9 3.9 %all-to-all-start.4 = ((f32[32,8,128]{2,1,0:T(8,128)}), f32[32,8,128]{2,1,0:T(8,128)S(1)}, u32[]{:S(2)}, u32[]{:S(2)}) async-start(f32[32,8,128]{2,1,0:T(8,128)} %get-tuple-element.58), calls=%async_computation.4 | async-start | bytes 262144 | tf_op jit(solution)/shard_map/all_to_all | solution.py:610
  85.8 2.7 %half.4.refs_0_ = bf16[1056,640]{1,0:T(8,128)(2,1)} custom-call(bf16[1056,640]{1,0:T(8,128)(2,1)S(1)} %get-tuple-element.57.dose, bf16[512,256]{1,0:T(8,128)(2,1)} %constant.29.clone.cols_far.refs_0_), custom_call_target="tpu_custom_call" | custom-call | flops 1730150400 | bytes 4055040 | tf_op jit(solution)/shard_map/half/pallas_call | solution.py:454
  88.5 6.4 %all-to-all-done.4.refs_1_ = f32[32,8,128]{2,1,0:T(8,128)S(1)} async-done(((f32[32,8,128]{2,1,0:T(8,128)}), f32[32,8,128]{2,1,0:T(8,128)S(1)}, u32[]{:S(2)}, u32[]{:S(2)}) %all-to-all-start.4) | async-done | bytes 131104 | tf_op jit(solution)/shard_map/all_to_all | solution.py:610
  95.3 9.1 %all_to_all.41.got = f32[8,8,128]{2,1,0:T(8,128)S(1)} all-to-all(f32[8,8,128]{2,1,0:T(8,128)S(1)} %get-tuple-element.60), channel_id=1, replica_groups=mesh['gx'=32,'gy'=8] {'gy'}, dimensions={0} | all-to-all | bytes 65536 | tf_op jit(solution)/shard_map/all_to_all | solution.py:610
  104.5 5.2 %step.3 = (bf16[1056,640]{1,0:T(8,128)(2,1)S(1)}, f32[32,8,128]{2,1,0:T(8,128)}, f32[128,128]{1,0:T(8,128)S(1)}) custom-call(f32[8,8,128]{2,1,0:T(8,128)S(1)} %all_to_all.41.got, f32[128,128]{1,0:T(8,128)S(1)} %get-tuple-element.61.part, f32[296,192]{1,0:T(8,128)S(1)} %get-tuple-element.45.matrix, ...), custom_call_target="tpu_custom_call", output_to_operand_aliasing={{0}: (4, {})} | custom-call | tf_op jit(solution)/shard_map/step/pallas_call | solution.py:546
  109.7 3.9 %all-to-all-start.6 = ((f32[32,8,128]{2,1,0:T(8,128)}), f32[32,8,128]{2,1,0:T(8,128)S(1)}, u32[]{:S(2)}, u32[]{:S(2)}) async-start(f32[32,8,128]{2,1,0:T(8,128)} %get-tuple-element.63), calls=%async_computation.6 | async-start | bytes 262144 | tf_op jit(solution)/shard_map/all_to_all | solution.py:610
  113.5 2.4 %half.5.refs_0_ = bf16[1056,512]{1,0:T(8,128)(2,1)} custom-call(bf16[1056,640]{1,0:T(8,128)(2,1)S(1)} %get-tuple-element.62.dose, bf16[512,256]{1,0:T(8,128)(2,1)} %constant.29.clone.cols_far.refs_0_), custom_call_target="tpu_custom_call" | custom-call | flops 1730150400 | bytes 4055040 | tf_op jit(solution)/shard_map/half/pallas_call | solution.py:454
  115.9 6.7 %all-to-all-done.6.refs_1_ = f32[32,8,128]{2,1,0:T(8,128)S(1)} async-done(((f32[32,8,128]{2,1,0:T(8,128)}), f32[32,8,128]{2,1,0:T(8,128)S(1)}, u32[]{:S(2)}, u32[]{:S(2)}) %all-to-all-start.6) | async-done | bytes 131104 | tf_op jit(solution)/shard_map/all_to_all | solution.py:610
  123.1 9.1 %all_to_all.42.got = f32[8,8,128]{2,1,0:T(8,128)S(1)} all-to-all(f32[8,8,128]{2,1,0:T(8,128)S(1)} %get-tuple-element.65), channel_id=1, replica_groups=mesh['gx'=32,'gy'=8] {'gy'}, dimensions={0} | all-to-all | bytes 65536 | tf_op jit(solution)/shard_map/all_to_all | solution.py:610
  132.2 3.8 %finish.1 = f32[1024,512]{1,0:T(8,128)} custom-call(f32[8,8,128]{2,1,0:T(8,128)S(1)} %all_to_all.42.got, f32[128,128]{1,0:T(8,128)S(1)} %get-tuple-element.66.part, f32[296,192]{1,0:T(8,128)S(1)} %get-tuple-element.45.matrix, bf16[128,640]{1,0:T(8,128)(2,1)S(1)} %get-tuple-element.46.cols, bf16[1056,640]{1,0:T(8,128)(2,1)S(1)} %get-tuple-element.62.dose, ...), custom_call_target="tpu_custom_call" | custom-call | tf_op jit(solution)/shard_map/finish/pallas_call | solution.py:587
  (8 shorter events, 6.0 us)
Async XLA Ops:
  7.4 21.0 %all-to-all-start = ((f32[32,8,128]{2,1,0:T(8,128)}), f32[32,8,128]{2,1,0:T(8,128)S(1)}, u32[]{:S(2)}, u32[]{:S(2)}) async-start(f32[32,8,128]{2,1,0:T(8,128)} %get-tuple-element.39), calls=%async_computation | async-start | bytes 262144 | tf_op jit(solution)/shard_map/all_to_all | solution.py:610
  19.2 4.4 %collective-permute-start = (bf16[16,1024]{1,0:T(8,128)(2,1)S(1)}, bf16[16,1024]{1,0:T(8,128)(2,1)S(1)}, u32[]{:S(2)}, u32[]{:S(2)}) collective-permute-start(bf16[16,1024]{1,0:T(8,128)(2,1)S(1)} %get-tuple-element.37), channel_id=1, source_target_pairs={{0,8},{8,16},{16,24},{24,32},{32,40},{40,48},{48,56},{56,64},{64,7... | collective-permute-start | bytes 98312 | tf_op jit(solution)/shard_map/ppermute | solution.py:606
  22.4 5.0 %collective-permute-start.1 = (bf16[16,1024]{1,0:T(8,128)(2,1)S(1)}, bf16[16,1024]{1,0:T(8,128)(2,1)S(1)}, u32[]{:S(2)}, u32[]{:S(2)}) collective-permute-start(bf16[16,1024]{1,0:T(8,128)(2,1)S(1)} %get-tuple-element.38), channel_id=1, source_target_pairs={{8,0},{16,8},{24,16},{32,24},{40,32},{48,40},{56,48},{64,56},{72,6... | collective-permute-start | bytes 98312 | tf_op jit(solution)/shard_map/ppermute | solution.py:606
  29.6 14.5 %all-to-all-start.1 = ((f32[8,88,128]{2,1,0:T(8,128)}), f32[8,88,128]{2,1,0:T(8,128)S(1)}, u32[]{:S(2)}, u32[]{:S(2)}) async-start(f32[8,88,128]{2,1,0:T(8,128)} %get-tuple-element.43), calls=%async_computation.1 | async-start | bytes 720896 | tf_op jit(solution)/shard_map/all_to_all | solution.py:610
  49.4 17.7 %all-to-all-start.2 = ((f32[32,8,128]{2,1,0:T(8,128)}), f32[32,8,128]{2,1,0:T(8,128)S(1)}, u32[]{:S(2)}, u32[]{:S(2)}) async-start(f32[32,8,128]{2,1,0:T(8,128)} %get-tuple-element.53), calls=%async_computation.2 | async-start | bytes 262144 | tf_op jit(solution)/shard_map/all_to_all | solution.py:610
  81.9 13.0 %all-to-all-start.4 = ((f32[32,8,128]{2,1,0:T(8,128)}), f32[32,8,128]{2,1,0:T(8,128)S(1)}, u32[]{:S(2)}, u32[]{:S(2)}) async-start(f32[32,8,128]{2,1,0:T(8,128)} %get-tuple-element.58), calls=%async_computation.4 | async-start | bytes 262144 | tf_op jit(solution)/shard_map/all_to_all | solution.py:610
  109.7 13.0 %all-to-all-start.6 = ((f32[32,8,128]{2,1,0:T(8,128)}), f32[32,8,128]{2,1,0:T(8,128)S(1)}, u32[]{:S(2)}, u32[]{:S(2)}) async-start(f32[32,8,128]{2,1,0:T(8,128)} %get-tuple-element.63), calls=%async_computation.6 | async-start | bytes 262144 | tf_op jit(solution)/shard_map/all_to_all | solution.py:610

commit v3 on v2

--- a/solution.py
+++ b/solution.py
@@ -62,7 +62,7 @@
 def column_matrices():
     second, third, fourth = level_operators(NX * 32)
     got = np.zeros((NX, 128, 256), np.float32)
-    own = np.zeros((NX, 128, 32), np.float32)
+    own = np.zeros((NX, 40, 32), np.float32)
     for px in range(NX):
         for q in range(QC):
             g = min(max(32 * px + q - 2, 0), NX * 32 - 1)
@@ -84,7 +84,7 @@
 def row_matrices(groups, first, step, length):
     second, third, fourth = level_operators(NY * 64)
     m = 16 * groups
-    out = np.zeros((NY, 3 * m + 8, 192), np.float32)
+    out = np.zeros((NY, 3 * m + 16, 144), np.float32)
     for py in range(NY):
         for b in range(groups):
             for k in range(length):
@@ -122,16 +122,6 @@
 
 
 @functools.cache
-def column_pool(lanes):
-    out = np.zeros((lanes, 128), np.float32)
-    cell = np.arange(TC)
-    out[cell, cell // 16] = 1
-    out[cell, 32 + cell // 64] = 1
-    out[cell, 40 + cell // 256] = 1
-    return out.astype(ml_dtypes.bfloat16)
-
-
-@functools.cache
 def row_pool(groups, stride, real, first):
     out = np.zeros((128, groups * stride), np.float32)
     for b in range(groups):
@@ -159,19 +149,6 @@
     return out
 
 
-@functools.cache
-def fine_rows():
-    out = np.zeros((3, BLK, BLK + 32), ml_dtypes.bfloat16)
-    taps = fine_taps()
-    for which in range(3):
-        for r in range(BLK):
-            for k in range(-HW, HW + 1):
-                c = r + 16 * which + k
-                if 0 <= c < BLK + 32:
-                    out[which, r, c] = taps[k + HW]
-    return out
-
-
 VMEM = pl.BlockSpec(memory_space=pltpu.VMEM)
 SMEM = pl.BlockSpec(memory_space=pltpu.SMEM)
 HBM = pl.BlockSpec(memory_space=pl.ANY)
@@ -201,11 +178,28 @@
     return first, second, (rest - second.astype(F32)).astype(BF16)
 
 
+def fill_rows(rows):
+    shape = (BLK, BLK + 32)
+    shift = lax.broadcasted_iota(jnp.int32, shape, 1) - lax.broadcasted_iota(jnp.int32, shape, 0)
+    for which in range(3):
+        band = jnp.zeros(shape, F32)
+        for k in range(-HW, HW + 1):
+            band = jnp.where(shift == 16 * which + k, float(fine_taps()[k + HW]), band)
+        rows[which] = band.astype(BF16)
+
+
+def fill_pool(cpool):
+    col = lax.broadcasted_iota(jnp.int32, cpool.shape, 0)
+    lane = lax.broadcasted_iota(jnp.int32, cpool.shape, 1)
+    group = jnp.where(lane < 32, col >> 4, jnp.where(lane < 40, 32 + (col >> 6), 40 + (col >> 8)))
+    cpool[...] = jnp.where((group == lane) & (col < TC), 1.0, 0.0).astype(BF16)
+
+
 def pooled_out(sums, row_pool_ref, px, send_ref, own_ref):
     a, b, c = pieces(sums)
     rows = row_pool_ref[...]
     pooled = (dot(rows, a) + dot(rows, b) + dot(rows, c)).T
-    own_ref[...] = pooled
+    own_ref[...] = pooled[:32]
     lane = lax.broadcasted_iota(jnp.int32, (8, 128), 1)
     coarse = jnp.where(lane < 80, pooled[32:40], pooled[40:48])
     left = jnp.where(lane < 64, pooled[0:8], coarse)
@@ -214,8 +208,9 @@
         send_ref[p] = jnp.where(p < px, left, right)
 
 
-def start_kernel(table, exps, classes, gain, cpool_far, rpool_far, dose, lo, hi, send, own, *scratch):
+def start_kernel(table, exps, classes, gain, rpool_far, mgot_far, mown_far, dose, lo, hi, send, own, mgot, mown, *scratch):
     cbuf, gbuf, cpool, rpool, sums, csem, gsem, tsem = scratch
+    px = lax.axis_index("gx")
     steps = TR // SB
     loads = []
     for i in range(steps):
@@ -229,17 +224,19 @@
         for copy in loads[-1]:
             copy.start()
     tables = (
-        pltpu.make_async_copy(cpool_far, cpool, tsem.at[0]),
-        pltpu.make_async_copy(rpool_far, rpool, tsem.at[1]),
+        pltpu.make_async_copy(rpool_far, rpool, tsem.at[0]),
+        pltpu.make_async_copy(mgot_far.at[px], mgot, tsem.at[1]),
+        pltpu.make_async_copy(mown_far.at[px], mown, tsem.at[2]),
     )
     for copy in tables:
         copy.start()
+    fill_pool(cpool)
     for i in range(steps):
         for copy in loads[i]:
             copy.wait()
         rows = slice(i * SB, (i + 1) * SB)
         for k in range(TC // SB):
-            e = exps[i, k]
+            e = exps[k, i]
             scale = jnp.where(e > 0, 2.0, jnp.where(e < 0, 0.5, 1.0)).astype(F32)
             at = slice(k * SB, (k + 1) * SB)
             c = cbuf[rows, at]
@@ -252,26 +249,28 @@
                 lo[:, rows] = value.astype(F32).T[:HALO].astype(BF16)
             if k == TC // SB - 1:
                 hi[:, rows] = value.astype(F32).T[SB - HALO :].astype(BF16)
-        if i == 0:
-            for copy in tables:
-                copy.wait()
         across = dot(dose[rows], cpool[...])
         sums[8 * i : 8 * i + 8] = jnp.sum(across.reshape(8, 16, 128), axis=1)
-    pooled_out(sums[...], rpool, lax.axis_index("gx"), send, own)
+    for copy in tables:
+        copy.wait()
+    pooled_out(sums[...], rpool, px, send, own)
 
 
 def start(table, exps, classes, gain):
     steps = TR // SB
+    mgot, mown = column_matrices()
     return pl.pallas_call(
         start_kernel,
-        in_specs=[SMEM, SMEM] + [HBM] * 4,
-        out_specs=[VMEM] * 5,
+        in_specs=[SMEM, SMEM] + [HBM] * 5,
+        out_specs=[VMEM] * 7,
         out_shape=[
             pltpu.VMEM((TR, TC), BF16),
             pltpu.VMEM((HALO, TR), BF16),
             pltpu.VMEM((HALO, TR), BF16),
-            pltpu.VMEM((NX, 8, 128), F32),
-            pltpu.VMEM((128, 128), F32),
+            pltpu.HBM((NX, 8, 128), F32),
+            pltpu.VMEM((32, 128), F32),
+            pltpu.VMEM(mgot.shape[1:], F32),
+            pltpu.VMEM(mown.shape[1:], F32),
         ],
         scratch_shapes=[
             pltpu.VMEM((TR, TC), jnp.int32),
@@ -281,60 +280,49 @@
             pltpu.VMEM((TR // 16, 128), F32),
             DMA((steps,)),
             DMA((steps,)),
-            DMA((2,)),
+            DMA((3,)),
         ],
         compiler_params=params(),
         name="start",
-    )(far(table), far(exps), far(classes), far(gain), far(jnp.asarray(column_pool(TC))), far(jnp.asarray(row_pool(8, 8, 8, 0))))
-
-
-def operators():
-    mgot, mown = column_matrices()
-    return [
-        (row_matrices(NB, 0, BLK // 16, BLK // 16 + 2), 1),
-        (mgot, 0),
-        (mown, 0),
-        (column_spread(), None),
-        (column_pool(EC), None),
-        (row_pool(NB, 16, BLK // 16, 1), None),
-        (fine_rows(), None),
-    ]
-
-
-def weighted(ref, weights, m):
-    for level in range(3):
-        at = slice(m * level, m * (level + 1))
-        ref[at] = ref[at] * weights[level]
-    ref[3 * m :] = ref[3 * m :] * weights[2]
-
-
-def pick_kernel(picks, after, weights, *refs):
-    n = len(picks)
-    tables, outs, sems = refs[:n], refs[n : 2 * n], refs[-1]
-    place = lax.axis_index("gx"), lax.axis_index("gy")
-    copies = []
-    for i, pick in enumerate(picks):
-        source = tables[i] if pick is None else tables[i].at[place[pick]]
-        copies.append(pltpu.make_async_copy(source, outs[i], sems.at[i]))
-        copies[-1].start()
+    )(
+        far(table), far(exps.T), far(classes), far(gain), far(jnp.asarray(row_pool(8, 8, 8, 0))),
+        far(jnp.asarray(mgot)), far(jnp.asarray(mown)),
+    )
+
+
+def pick_kernel(after, weights, matrix_far, spread_far, rpool_far, matrix, spread_near, rpool, buf, sems):
+    copies = (
+        pltpu.make_async_copy(matrix_far.at[lax.axis_index("gy")], buf, sems.at[0]),
+        pltpu.make_async_copy(spread_far, spread_near, sems.at[1]),
+        pltpu.make_async_copy(rpool_far, rpool, sems.at[2]),
+    )
+    for copy in copies:
+        copy.start()
     for copy in copies:
         copy.wait()
-    weighted(outs[0], weights, 16 * NB)
+    m, count = 16 * NB, buf.shape[0]
+    for level in range(3):
+        at = slice(m * level, m * (level + 1) if level < 2 else count)
+        scaled = buf[at] * weights[level]
+        first = scaled.astype(BF16)
+        matrix[at] = first
+        low = slice(count + at.start, count + at.stop)
+        matrix[low] = (scaled - first.astype(F32)).astype(BF16)
 
 
 def pick(after, weights):
-    made = operators()
-    picks = [at for _, at in made]
-    outs = [pltpu.VMEM(t.shape if at is None else t.shape[1:], t.dtype) for t, at in made]
+    table = row_matrices(NB, 0, BLK // 16, BLK // 16 + 2)
+    count, width = table.shape[1:]
+    more = [column_spread(), row_pool(NB, 16, BLK // 16, 1)]
     return pl.pallas_call(
-        functools.partial(pick_kernel, picks),
-        in_specs=[HBM, SMEM] + [HBM] * len(made),
-        out_specs=[VMEM] * len(made),
-        out_shape=outs,
-        scratch_shapes=[DMA((len(made),))],
+        pick_kernel,
+        in_specs=[HBM, SMEM] + [HBM] * 3,
+        out_specs=[VMEM] * 3,
+        out_shape=[pltpu.VMEM((2 * count, width), BF16)] + [pltpu.VMEM(t.shape, BF16) for t in more],
+        scratch_shapes=[pltpu.VMEM((count, width), F32), DMA((3,))],
         compiler_params=params(),
         name="pick",
-    )(near(after), far(weights), *[far(jnp.asarray(t)) for t, _ in made])
+    )(near(after), far(weights), *[far(jnp.asarray(t)) for t in [table, *more]])
 
 
 def side(strip_lo, strip_hi):
@@ -349,9 +337,10 @@
     else:
         _, got, own, mgot, mown, send, part = refs
     received = got[...].reshape(NX * 8, 128)
-    z = dot(mgot[...], received, precision=EXACT) + dot(mown[...], own[:32], precision=EXACT)
-    z = z.T
-    part[...] = z
+    z = dot(mgot[...], received, precision=EXACT)
+    mine = dot(mown[...], own[...], precision=EXACT)
+    z = jnp.concatenate([z[:40] + mine, z[40:]], axis=0).T
+    part[...] = z[:80]
     lane = lax.broadcasted_iota(jnp.int32, (8, 128), 1)
     coarse = z[80:88]
     up = jnp.where(lane < 40, z[0:8], jnp.where(lane < 80, z[64:72], coarse))
@@ -371,17 +360,17 @@
                 send[p, 8 + HALO * n : 8 + HALO * (n + 1)] = jnp.where(p < py, top, bottom)
 
 
-def across(first, extra, got, own, ops):
+def across(first, extra, got, own, mgot, mown):
     count = 8 + HALO * (EC // 128) if first else 8
     specs = [VMEM] * 3 if first else [HBM]
     return pl.pallas_call(
         functools.partial(across_kernel, first),
         in_specs=specs + [VMEM] * 4,
         out_specs=[VMEM] * 2,
-        out_shape=[pltpu.VMEM((NY, count, 128), F32), pltpu.VMEM((128, 128), F32)],
+        out_shape=[pltpu.VMEM((NY, count, 128), F32), pltpu.VMEM((80, 128), F32)],
         compiler_params=params(),
         name="across",
-    )(*([near(x) for x in extra] if first else [far(x) for x in extra]), near(got), near(own), near(ops[1]), near(ops[2]))
+    )(*([near(x) for x in extra] if first else [near(x) for x in extra]), near(got), near(own), near(mgot), near(mown))
 
 
 def column_pass(block, cols, half, at):
@@ -436,27 +425,21 @@
     )(near(tile), near(lo), near(hi), far(jnp.asarray(fine_columns())))
 
 
-def half_kernel(dose, cols_far, half_far, half, cols, sems, csem):
+def half_kernel(dose, cols_far, half, cols, csem):
     load = pltpu.make_async_copy(cols_far, cols, csem)
     load.start()
     load.wait()
-    stores = []
     for b in range(NB):
         column_pass(dose[b * BLK : (b + 1) * BLK], cols, half, slice(b * BLK, (b + 1) * BLK))
-        at = pl.ds(b * BLK, BLK)
-        stores.append(pltpu.make_async_copy(half.at[at], half_far.at[at], sems.at[b]))
-        stores[-1].start()
-    for copy in stores:
-        copy.wait()
 
 
 def half_of(dose, lanes):
     return pl.pallas_call(
         half_kernel,
         in_specs=[VMEM, HBM],
-        out_specs=HBM,
-        out_shape=pltpu.HBM((ER, lanes), BF16),
-        scratch_shapes=[pltpu.VMEM((ER, lanes), BF16), pltpu.VMEM((512, 256), BF16), DMA((NB,)), DMA],
+        out_specs=VMEM,
+        out_shape=pltpu.VMEM((ER, lanes), BF16),
+        scratch_shapes=[pltpu.VMEM((512, 256), BF16), DMA],
         compiler_params=params(),
         cost_estimate=half_cost(),
         name="half",
@@ -465,11 +448,14 @@
 
 def spread(received, part, matrix, cols, groups):
     m = 16 * groups
-    y = dot(matrix[...], jnp.concatenate([received, part[...]], axis=0), precision=EXACT)
+    count = matrix.shape[0] // 2
+    x, rest, _ = pieces(jnp.concatenate([received, part[...]], axis=0))
+    both = dot(matrix[...], x)
+    y = both[:count] + both[count:] + dot(matrix[:count], rest)
     lane = lax.broadcasted_iota(jnp.int32, (m, 128), 1)
     fourth = jnp.where(lane < 120, y[2 * m : 3 * m], jnp.where(lane == 120, y[3 * m : 3 * m + 1], 0.0))
-    a, b, c = pieces(jnp.where(lane < 40, y[:m], jnp.where(lane < 80, y[m : 2 * m], fourth)))
-    return dot(a, cols) + dot(b, cols) + dot(c, cols)
+    a, b, _ = pieces(jnp.where(lane < 40, y[:m], jnp.where(lane < 80, y[m : 2 * m], fourth)))
+    return dot(a, cols) + dot(b, cols)
 
 
 def short_range(b, rows, half):
@@ -490,44 +476,33 @@
         out[row - skip : row - skip + 16] = (old_rows(row).astype(F32) * 2.0 / full).astype(out.dtype)
 
 
-def step_kernel(first, got, part, matrix, cols, dose, half, rows, cpool, rpool, *refs):
+def step_kernel(first, got, part, matrix, cols, rpool, dose, half, *refs):
     if first:
-        fcols_far, out, send, own, hbuf, grid, sums, lsem, dbuf, fcols, dsem, fsem = refs
-        fetch = pltpu.make_async_copy(fcols_far, fcols, fsem)
-        fetch.start()
+        fcols_far, out, send, own, rows, cpool, grid, sums, hbuf, dbuf, fcols, lsem, fsem = refs
+        loads = [pltpu.make_async_copy(fcols_far, fcols, fsem)]
+        at = pl.ds(HALO, TR)
+        loads.append(pltpu.make_async_copy(half.at[at], hbuf.at[at], lsem.at[0]))
+        loads.append(pltpu.make_async_copy(dose.at[at], dbuf.at[at], lsem.at[1]))
+        for copy in loads:
+            copy.start()
     else:
-        out, send, own, hbuf, grid, sums, lsem = refs
-        dbuf = dose
-    loads = []
-    for b in range(NB):
-        begin, end = b * BLK, (b + 1) * BLK
-        if first:
-            begin, end = max(begin, HALO), min(end, ER - HALO)
-        at = pl.ds(begin, end - begin)
-        loads.append([pltpu.make_async_copy(half.at[at], hbuf.at[at], lsem.at[b])])
-        if first:
-            loads[-1].append(pltpu.make_async_copy(dose.at[at], dbuf.at[at], dsem.at[b]))
-        for copy in loads[-1]:
-            copy.start()
+        out, send, own, rows, cpool, grid, sums = refs
+        dbuf, hbuf = dose, half
+    fill_rows(rows)
+    fill_pool(cpool)
     received = got[:, :8].reshape(NY * 8, 128)
     grid[...] = spread(received, part, matrix, cols[...], NB)
     if first:
         py = lax.axis_index("gy")
-        fetch.wait()
+        loads[0].wait()
         for row, p, real in ((0, jnp.maximum(py - 1, 0), py > 0), (ER - HALO, jnp.minimum(py + 1, NY - 1), py < NY - 1)):
             tiles = [got[p, 8 + HALO * n : 8 + HALO * (n + 1)] for n in range(EC // 128)]
             values = jnp.where(real, jnp.concatenate(tiles, axis=1), 0.0).astype(BF16)
             dbuf[row : row + HALO] = values
             column_pass(values, fcols, hbuf, slice(row, row + HALO))
-
-    def ready(b):
-        for copy in loads[b]:
+        for copy in loads[1:]:
             copy.wait()
-
-    ready(0)
     for b in range(NB):
-        if b + 1 < NB:
-            ready(b + 1)
         update(b, lambda row: dbuf[row : row + 16], short_range(b, rows, hbuf), grid, out, 0)
         pooled = dot(out[b * BLK : (b + 1) * BLK], cpool[...])
         pooled = jnp.sum(pooled.reshape(BLK // 16, 16, 128), axis=1)
@@ -537,44 +512,39 @@
 
 def step(first, got, part, dose, half, ops):
     scratch = [
-        pltpu.VMEM((ER, EC), BF16),
+        pltpu.VMEM((3, BLK, BLK + 32), BF16),
+        pltpu.VMEM((EC, 128), BF16),
         pltpu.VMEM((NB * 16, EC), F32),
         pltpu.VMEM((NB * 16, 128), F32),
-        DMA((NB,)),
     ]
-    more = [pltpu.VMEM((ER, EC), BF16), pltpu.VMEM((512, 256), BF16), DMA((NB,)), DMA] if first else []
+    if first:
+        scratch += [pltpu.VMEM((ER, EC), BF16)] * 2 + [pltpu.VMEM((512, 256), BF16), DMA((2,)), DMA]
+    place = far if first else near
     return pl.pallas_call(
         functools.partial(step_kernel, first),
-        in_specs=[VMEM] * 4 + [HBM if first else VMEM, HBM] + [VMEM] * 3 + ([HBM] if first else []),
+        in_specs=[VMEM] * 5 + ([HBM] * 3 if first else [VMEM] * 2),
         out_specs=[VMEM] * 3,
         out_shape=[
             pltpu.VMEM((ER, EC), BF16),
-            pltpu.VMEM((NX, 8, 128), F32),
-            pltpu.VMEM((128, 128), F32),
+            pltpu.HBM((NX, 8, 128), F32),
+            pltpu.VMEM((32, 128), F32),
         ],
-        scratch_shapes=scratch + more,
-        input_output_aliases={} if first else {4: 0},
+        scratch_shapes=scratch,
+        input_output_aliases={} if first else {5: 0},
         compiler_params=params(),
         name="first_step" if first else "step",
     )(
-        near(got), near(part), near(ops[0]), near(ops[3]), far(dose) if first else near(dose), far(half),
-        near(ops[6]), near(ops[4]), near(ops[5]), *([far(jnp.asarray(fine_columns()))] if first else []),
+        near(got), near(part), *[near(x) for x in ops], place(dose), place(half),
+        *([far(jnp.asarray(fine_columns()))] if first else []),
     )
 
 
-def finish_kernel(got, part, matrix, cols, dose, half, rows, out, hbuf, made, grid, lsem, ssem):
-    loads = []
-    for b in range(NB):
-        at = pl.ds(b * BLK, BLK)
-        loads.append(pltpu.make_async_copy(half.at[at], hbuf.at[at], lsem.at[b]))
-        loads[-1].start()
+def finish_kernel(got, part, matrix, cols, dose, half, out, rows, made, grid, ssem):
+    fill_rows(rows)
     grid[...] = spread(got[...].reshape(NY * 8, 128), part, matrix, cols[:, :TC], NB)
     stores = []
-    loads[0].wait()
     for b in range(NB):
-        if b + 1 < NB:
-            loads[b + 1].wait()
-        update(b, lambda row: dose[row : row + 16, :TC], short_range(b, rows, hbuf), grid, made, HALO)
+        update(b, lambda row: dose[row : row + 16, :TC], short_range(b, rows, half), grid, made, HALO)
         begin, end = max(b * BLK - HALO, 0), min((b + 1) * BLK - HALO, TR)
         at = pl.ds(begin, end - begin)
         stores.append(pltpu.make_async_copy(made.at[at], out.at[at], ssem.at[b]))
@@ -586,19 +556,18 @@
 def finish(got, part, dose, half, ops):
     return pl.pallas_call(
         finish_kernel,
-        in_specs=[VMEM] * 5 + [HBM, VMEM],
+        in_specs=[VMEM] * 6,
         out_specs=HBM,
         out_shape=pltpu.HBM((TR, TC), F32),
         scratch_shapes=[
-            pltpu.VMEM((ER, TC), BF16),
+            pltpu.VMEM((3, BLK, BLK + 32), BF16),
             pltpu.VMEM((TR, TC), F32),
             pltpu.VMEM((NB * 16, TC), F32),
-            DMA((NB,)),
             DMA((NB,)),
         ],
         compiler_params=params(),
         name="finish",
-    )(near(got), near(part), near(ops[0]), near(ops[3]), near(dose), far(half), near(ops[6]))
+    )(near(got), near(part), near(ops[0]), near(ops[1]), near(dose), near(half))
 
 
 def shifted(x, axis, by):
@@ -611,18 +580,18 @@
 
 
 def local(classes, exponents, gain_field, level_table, level_weights):
-    tile, lo, hi, send, own = start(level_table, exponents, classes, gain_field)
+    tile, lo, hi, send, own, mgot, mown = start(level_table, exponents, classes, gain_field)
     left, right = shifted(hi, "gx", 1), shifted(lo, "gx", -1)
     got = exchanged(send, "gx")
-    ops = pick(left, level_weights)
-    send, part = across(True, (tile, left, right), got, own, ops)
+    send, part = across(True, (tile, left, right), got, own, mgot, mown)
     got = exchanged(send, "gy")
+    ops = pick(part, level_weights)
     half, dose = first_half(tile, left, right)
     dose, send, own = step(True, got, part, dose, half, ops)
     for sweep in range(2, ITERS + 1):
         got = exchanged(send, "gx")
         half = half_of(dose, EC if sweep < ITERS else TC)
-        send, part = across(False, (half,), got, own, ops)
+        send, part = across(False, (half,), got, own, mgot, mown)
         got = exchanged(send, "gy")
         if sweep < ITERS:
             dose, send, own = step(False, got, part, dose, half, ops)

time: 137 us -> 129 us (0.942)
  Pallas kernels: 41.4 us -> 32.2 us
  waiting for transfers between devices: 26.2 us -> 28.5 us
    pallas_call x9, Pallas kernels: 35.3 us -> 26.1 us  [the longest x3 11.3 us: step(): pl.pallas_call(functools.partial(step_kernel, first), in_specs=[VMEM] * 5...]
    ppermute x2, waiting for transfers between devices: 1.6 us -> 3.65 us  [shifted(): lax.ppermute(x, axis, [(i, i + by) for i in range(n) if 0 <= i + by < n])]
  transfers between devices with their start and end apart: 7 -> 7, of which waited for: 6 -> 6; matrix products, arithmetic and copies ran while one was open for 0% -> 0% of each run, Pallas kernels for 10% -> 9%
where the time goes in v3:
time: 129 us; the launch traced here: 128 us
  starting transfers between devices  39.5 us (31%)
  Pallas kernels  32.2 us (25%)
  waiting for transfers between devices  28.5 us (22%)
  blocking collectives  27.6 us (21%)
    all_to_all x5, starting transfers between devices, exchanged(): return lax.all_to_all(x, axis, 0, 0, tiled=True)  35.1 us
    all_to_all x3, blocking collectives, exchanged(): return lax.all_to_all(x, axis, 0, 0, tiled=True)  27.6 us
    all_to_all x5, waiting for transfers between devices, exchanged(): return lax.all_to_all(x, axis, 0, 0, tiled=True)  24.8 us
    pallas_call x3, Pallas kernels, step(): pl.pallas_call(functools.partial(step_kernel, first), in_specs=[VMEM] * 5...  11.3 us
    pallas_call x3, Pallas kernels, half_of(): pl.pallas_call(half_kernel, in_specs=[VMEM, HBM], out_specs=VMEM, out_sha...  5.66 us
    pallas_call x1, Pallas kernels, start(): pl.pallas_call(start_kernel, in_specs=[SMEM, SMEM] + [HBM] * 5, out_specs...  5.31 us
    ppermute x2, starting transfers between devices, shifted(): lax.ppermute(x, axis, [(i, i + by) for i in range(n) if 0 <= i + by < n])  4.43 us
    pallas_call x1, Pallas kernels, first_half(): pl.pallas_call(first_half_kernel, in_specs=[VMEM] * 3 + [HBM], out_specs=...  3.79 us
  transfers between devices with their start and end apart: 7, of which 6 were waited for; matrix products, arithmetic and copies ran while one was open for 0% of the time, Pallas kernels for 9%

profile of v3, /device:TPU:1, one launch (start us, length us, event | category | flops | bytes accessed | tf_op | source)
XLA Modules:
  0.0 128.1 jit_solution(10995653854948244994)
XLA Ops:
  0.0 5.3 %start.1 = (bf16[1024,512]{1,0:T(8,128)(2,1)S(1)}, bf16[16,1024]{1,0:T(8,128)(2,1)S(1)}, bf16[16,1024]{1,0:T(8,128)(2,1)S(1)}, f32[32,8,128]{2,1,0:T(8,128)}, f3...) custom-call(f32[8]{0:T(128)} %table.1, s32[4,8]{1,0:T(4,128)} %bitcast.1, s32[1024,512]{1,0:T(8,128)} %classes.1, ...), custom_call_target="tpu_custom_call" | custom-call | tf_op jit(solution)/shard_map/start/pallas_call | solution.py:262
  5.3 11.9 %all-to-all-start = ((f32[32,8,128]{2,1,0:T(8,128)}), f32[32,8,128]{2,1,0:T(8,128)S(1)}, u32[]{:S(2)}, u32[]{:S(2)}) async-start(f32[32,8,128]{2,1,0:T(8,128)} %get-tuple-element.37), calls=%async_computation | async-start | bytes 262144 | tf_op jit(solution)/shard_map/all_to_all | solution.py:579
  17.2 3.1 %collective-permute-start = (bf16[16,1024]{1,0:T(8,128)(2,1)S(1)}, bf16[16,1024]{1,0:T(8,128)(2,1)S(1)}, u32[]{:S(2)}, u32[]{:S(2)}) collective-permute-start(bf16[16,1024]{1,0:T(8,128)(2,1)S(1)} %get-tuple-element.35), channel_id=1, source_target_pairs={{0,8},{8,16},{16,24},{24,32},{32,40},{40,48},{48,56},{56,64},{64,7... | collective-permute-start | bytes 98312 | tf_op jit(solution)/shard_map/ppermute | solution.py:575
  21.7 3.6 %collective-permute-done.1.refs_2_.hi = bf16[16,1024]{1,0:T(8,128)(2,1)S(1)} collective-permute-done((bf16[16,1024]{1,0:T(8,128)(2,1)S(1)}, bf16[16,1024]{1,0:T(8,128)(2,1)S(1)}, u32[]{:S(2)}, u32[]{:S(2)}) %collective-permute-start.1) | collective-permute-done | bytes 32800 | tf_op jit(solution)/shard_map/ppermute | solution.py:575
  27.5 6.8 %all-to-all-start.1 = ((f32[8,88,128]{2,1,0:T(8,128)}), f32[8,88,128]{2,1,0:T(8,128)S(1)}, u32[]{:S(2)}, u32[]{:S(2)}) async-start(f32[8,88,128]{2,1,0:T(8,128)} %get-tuple-element.41), calls=%async_computation.1 | async-start | bytes 720896 | tf_op jit(solution)/shard_map/all_to_all | solution.py:579
  34.3 3.8 %first_half.1 = (bf16[1056,640]{1,0:T(8,128)(2,1)}, bf16[1056,640]{1,0:T(8,128)(2,1)}) custom-call(bf16[1024,512]{1,0:T(8,128)(2,1)S(1)} %get-tuple-element.34.refs_0_.tile, bf16[16,1024]{1,0:T(8,128)(2,1)S(1)} %collective-permute-done.refs_1_.lo, bf16[16,1024]{1,0:T(8,128)(2,1)S(1)} %collective-permute-done.1.refs_2_.hi, ...), custom_call_target="tpu_custom_call" | custom-call | flops 1730150400 | bytes 4055040 | tf_op jit(solution)/shard_map/first_half/pallas_call | solution.py:410
  38.1 1.8 %pick.1 = (bf16[608,144]{1,0:T(8,128)(2,1)S(1)}, bf16[128,640]{1,0:T(8,128)(2,1)S(1)}, bf16[128,96]{1,0:T(8,128)(2,1)S(1)}) custom-call(f32[80,128]{1,0:T(8,128)S(1)} %get-tuple-element.42.after.part, f32[3]{0:T(128)} %weights.1, f32[8,304,144]{2,1,0:T(8,128)} %constant.17.clone.matrix_far, bf16[128,640]{1,0:T(8,128)(2,1)} %constant.18.clone.spread_far, ...), custom_call_target="tpu_custom_call" | custom-call | tf_op jit(solution)/shard_map/pick/pallas_call | solution.py:317
  39.9 2.2 %all-to-all-done.1.got = f32[8,88,128]{2,1,0:T(8,128)S(1)} async-done(((f32[8,88,128]{2,1,0:T(8,128)}), f32[8,88,128]{2,1,0:T(8,128)S(1)}, u32[]{:S(2)}, u32[]{:S(2)}) %all-to-all-start.1) | async-done | bytes 360480 | tf_op jit(solution)/shard_map/all_to_all | solution.py:579
  42.0 4.4 %first_step.1 = (bf16[1056,640]{1,0:T(8,128)(2,1)S(1)}, f32[32,8,128]{2,1,0:T(8,128)}, f32[32,128]{1,0:T(8,128)S(1)}) custom-call(f32[8,88,128]{2,1,0:T(8,128)S(1)} %all-to-all-done.1.got, f32[80,128]{1,0:T(8,128)S(1)} %get-tuple-element.42.after.part, bf16[608,144]{1,0:T(8,128)(2,1)S(1)} %get-tuple-element.43.matrix, ...), custom_call_target="tpu_custom_call" | custom-call | tf_op jit(solution)/shard_map/first_step/pallas_call | solution.py:523
  46.5 8.5 %all-to-all-start.2 = ((f32[32,8,128]{2,1,0:T(8,128)}), f32[32,8,128]{2,1,0:T(8,128)S(1)}, u32[]{:S(2)}, u32[]{:S(2)}) async-start(f32[32,8,128]{2,1,0:T(8,128)} %get-tuple-element.49), calls=%async_computation.2 | async-start | bytes 262144 | tf_op jit(solution)/shard_map/all_to_all | solution.py:579
  55.0 2.0 %half.3.refs_0_ = bf16[1056,640]{1,0:T(8,128)(2,1)S(1)} custom-call(bf16[1056,640]{1,0:T(8,128)(2,1)S(1)} %get-tuple-element.48.dose, bf16[512,256]{1,0:T(8,128)(2,1)} %constant.20.clone.cols_far.refs_0_), custom_call_target="tpu_custom_call" | custom-call | flops 1730150400 | bytes 4055040 | tf_op jit(solution)/shard_map/half/pallas_call | solution.py:437
  57.0 7.2 %all-to-all-done.2.refs_1_ = f32[32,8,128]{2,1,0:T(8,128)S(1)} async-done(((f32[32,8,128]{2,1,0:T(8,128)}), f32[32,8,128]{2,1,0:T(8,128)S(1)}, u32[]{:S(2)}, u32[]{:S(2)}) %all-to-all-start.2) | async-done | bytes 131104 | tf_op jit(solution)/shard_map/all_to_all | solution.py:579
  64.5 9.4 %all_to_all.40.got = f32[8,8,128]{2,1,0:T(8,128)S(1)} all-to-all(f32[8,8,128]{2,1,0:T(8,128)S(1)} %get-tuple-element.51), channel_id=1, replica_groups=mesh['gx'=32,'gy'=8] {'gy'}, dimensions={0} | all-to-all | bytes 65536 | tf_op jit(solution)/shard_map/all_to_all | solution.py:579
  73.9 3.4 %step.2 = (bf16[1056,640]{1,0:T(8,128)(2,1)S(1)}, f32[32,8,128]{2,1,0:T(8,128)}, f32[32,128]{1,0:T(8,128)S(1)}) custom-call(f32[8,8,128]{2,1,0:T(8,128)S(1)} %all_to_all.40.got, f32[80,128]{1,0:T(8,128)S(1)} %get-tuple-element.52.part, bf16[608,144]{1,0:T(8,128)(2,1)S(1)} %get-tuple-element.43.matrix, ...), custom_call_target="tpu_custom_call", output_to_operand_aliasing={{0}: (5, {})} | custom-call | tf_op jit(solution)/shard_map/step/pallas_call | solution.py:523
  77.3 4.0 %all-to-all-start.4 = ((f32[32,8,128]{2,1,0:T(8,128)}), f32[32,8,128]{2,1,0:T(8,128)S(1)}, u32[]{:S(2)}, u32[]{:S(2)}) async-start(f32[32,8,128]{2,1,0:T(8,128)} %get-tuple-element.54), calls=%async_computation.4 | async-start | bytes 262144 | tf_op jit(solution)/shard_map/all_to_all | solution.py:579
  81.4 2.0 %half.4.refs_0_ = bf16[1056,640]{1,0:T(8,128)(2,1)S(1)} custom-call(bf16[1056,640]{1,0:T(8,128)(2,1)S(1)} %get-tuple-element.53.dose, bf16[512,256]{1,0:T(8,128)(2,1)} %constant.20.clone.cols_far.refs_0_), custom_call_target="tpu_custom_call" | custom-call | flops 1730150400 | bytes 4055040 | tf_op jit(solution)/shard_map/half/pallas_call | solution.py:437
  83.4 7.0 %all-to-all-done.4.refs_1_ = f32[32,8,128]{2,1,0:T(8,128)S(1)} async-done(((f32[32,8,128]{2,1,0:T(8,128)}), f32[32,8,128]{2,1,0:T(8,128)S(1)}, u32[]{:S(2)}, u32[]{:S(2)}) %all-to-all-start.4) | async-done | bytes 131104 | tf_op jit(solution)/shard_map/all_to_all | solution.py:579
  90.7 9.1 %all_to_all.41.got = f32[8,8,128]{2,1,0:T(8,128)S(1)} all-to-all(f32[8,8,128]{2,1,0:T(8,128)S(1)} %get-tuple-element.56), channel_id=1, replica_groups=mesh['gx'=32,'gy'=8] {'gy'}, dimensions={0} | all-to-all | bytes 65536 | tf_op jit(solution)/shard_map/all_to_all | solution.py:579
  99.9 3.4 %step.3 = (bf16[1056,640]{1,0:T(8,128)(2,1)S(1)}, f32[32,8,128]{2,1,0:T(8,128)}, f32[32,128]{1,0:T(8,128)S(1)}) custom-call(f32[8,8,128]{2,1,0:T(8,128)S(1)} %all_to_all.41.got, f32[80,128]{1,0:T(8,128)S(1)} %get-tuple-element.57.part, bf16[608,144]{1,0:T(8,128)(2,1)S(1)} %get-tuple-element.43.matrix, ...), custom_call_target="tpu_custom_call", output_to_operand_aliasing={{0}: (5, {})} | custom-call | tf_op jit(solution)/shard_map/step/pallas_call | solution.py:523
  103.3 3.9 %all-to-all-start.6 = ((f32[32,8,128]{2,1,0:T(8,128)}), f32[32,8,128]{2,1,0:T(8,128)S(1)}, u32[]{:S(2)}, u32[]{:S(2)}) async-start(f32[32,8,128]{2,1,0:T(8,128)} %get-tuple-element.59), calls=%async_computation.6 | async-start | bytes 262144 | tf_op jit(solution)/shard_map/all_to_all | solution.py:579
  107.1 1.7 %half.5.refs_0_ = bf16[1056,512]{1,0:T(8,128)(2,1)S(1)} custom-call(bf16[1056,640]{1,0:T(8,128)(2,1)S(1)} %get-tuple-element.58.dose, bf16[512,256]{1,0:T(8,128)(2,1)} %constant.20.clone.cols_far.refs_0_), custom_call_target="tpu_custom_call" | custom-call | flops 1730150400 | bytes 4055040 | tf_op jit(solution)/shard_map/half/pallas_call | solution.py:437
  108.8 7.5 %all-to-all-done.6.refs_1_ = f32[32,8,128]{2,1,0:T(8,128)S(1)} async-done(((f32[32,8,128]{2,1,0:T(8,128)}), f32[32,8,128]{2,1,0:T(8,128)S(1)}, u32[]{:S(2)}, u32[]{:S(2)}) %all-to-all-start.6) | async-done | bytes 131104 | tf_op jit(solution)/shard_map/all_to_all | solution.py:579
  116.7 9.1 %all_to_all.42.got = f32[8,8,128]{2,1,0:T(8,128)S(1)} all-to-all(f32[8,8,128]{2,1,0:T(8,128)S(1)} %get-tuple-element.61), channel_id=1, replica_groups=mesh['gx'=32,'gy'=8] {'gy'}, dimensions={0} | all-to-all | bytes 65536 | tf_op jit(solution)/shard_map/all_to_all | solution.py:579
  125.8 2.1 %finish.1 = f32[1024,512]{1,0:T(8,128)} custom-call(f32[8,8,128]{2,1,0:T(8,128)S(1)} %all_to_all.42.got, f32[80,128]{1,0:T(8,128)S(1)} %get-tuple-element.62.part, bf16[608,144]{1,0:T(8,128)(2,1)S(1)} %get-tuple-element.43.matrix, bf16[128,640]{1,0:T(8,128)(2,1)S(1)} %get-tuple-element.44.cols, bf16[1056,640]{1,0:T(8,128)(2,1)S(1)} %get-tuple-element.58.dose, ...), custom_call_target="tpu_custom_call" | custom-call | tf_op jit(solution)/shard_map/finish/pallas_call | solution.py:557
  (7 shorter events, 4.6 us)
Async XLA Ops:
  5.3 21.0 %all-to-all-start = ((f32[32,8,128]{2,1,0:T(8,128)}), f32[32,8,128]{2,1,0:T(8,128)S(1)}, u32[]{:S(2)}, u32[]{:S(2)}) async-start(f32[32,8,128]{2,1,0:T(8,128)} %get-tuple-element.37), calls=%async_computation | async-start | bytes 262144 | tf_op jit(solution)/shard_map/all_to_all | solution.py:579
  17.2 4.4 %collective-permute-start = (bf16[16,1024]{1,0:T(8,128)(2,1)S(1)}, bf16[16,1024]{1,0:T(8,128)(2,1)S(1)}, u32[]{:S(2)}, u32[]{:S(2)}) collective-permute-start(bf16[16,1024]{1,0:T(8,128)(2,1)S(1)} %get-tuple-element.35), channel_id=1, source_target_pairs={{0,8},{8,16},{16,24},{24,32},{32,40},{40,48},{48,56},{56,64},{64,7... | collective-permute-start | bytes 98312 | tf_op jit(solution)/shard_map/ppermute | solution.py:575
  20.3 5.0 %collective-permute-start.1 = (bf16[16,1024]{1,0:T(8,128)(2,1)S(1)}, bf16[16,1024]{1,0:T(8,128)(2,1)S(1)}, u32[]{:S(2)}, u32[]{:S(2)}) collective-permute-start(bf16[16,1024]{1,0:T(8,128)(2,1)S(1)} %get-tuple-element.36), channel_id=1, source_target_pairs={{8,0},{16,8},{24,16},{32,24},{40,32},{48,40},{56,48},{64,56},{72,6... | collective-permute-start | bytes 98312 | tf_op jit(solution)/shard_map/ppermute | solution.py:575
  27.5 14.5 %all-to-all-start.1 = ((f32[8,88,128]{2,1,0:T(8,128)}), f32[8,88,128]{2,1,0:T(8,128)S(1)}, u32[]{:S(2)}, u32[]{:S(2)}) async-start(f32[8,88,128]{2,1,0:T(8,128)} %get-tuple-element.41), calls=%async_computation.1 | async-start | bytes 720896 | tf_op jit(solution)/shard_map/all_to_all | solution.py:579
  46.5 17.7 %all-to-all-start.2 = ((f32[32,8,128]{2,1,0:T(8,128)}), f32[32,8,128]{2,1,0:T(8,128)S(1)}, u32[]{:S(2)}, u32[]{:S(2)}) async-start(f32[32,8,128]{2,1,0:T(8,128)} %get-tuple-element.49), calls=%async_computation.2 | async-start | bytes 262144 | tf_op jit(solution)/shard_map/all_to_all | solution.py:579
  77.3 13.0 %all-to-all-start.4 = ((f32[32,8,128]{2,1,0:T(8,128)}), f32[32,8,128]{2,1,0:T(8,128)S(1)}, u32[]{:S(2)}, u32[]{:S(2)}) async-start(f32[32,8,128]{2,1,0:T(8,128)} %get-tuple-element.54), calls=%async_computation.4 | async-start | bytes 262144 | tf_op jit(solution)/shard_map/all_to_all | solution.py:579
  103.3 13.0 %all-to-all-start.6 = ((f32[32,8,128]{2,1,0:T(8,128)}), f32[32,8,128]{2,1,0:T(8,128)S(1)}, u32[]{:S(2)}, u32[]{:S(2)}) async-start(f32[32,8,128]{2,1,0:T(8,128)} %get-tuple-element.59), calls=%async_computation.6 | async-start | bytes 262144 | tf_op jit(solution)/shard_map/all_to_all | solution.py:579

commit v4 on v3

--- a/solution.py
+++ b/solution.py
@@ -81,27 +81,27 @@
     return got, own
 
 
-def row_matrices(groups, first, step, length):
+QM = QR + 4
+
+
+def row_matrices():
     second, third, fourth = level_operators(NY * 64)
-    m = 16 * groups
-    out = np.zeros((NY, 3 * m + 16, 144), np.float32)
+    out = np.zeros((NY, 3 * QM + 8, 144), np.float32)
     for py in range(NY):
-        for b in range(groups):
-            for k in range(length):
-                row, q = b * 16 + k, first + step * b + k
-                g = min(max(64 * py + q - 2, 0), NY * 64 - 1)
-                for s in np.nonzero(second[g])[0]:
-                    p, j = divmod(int(s), 64)
-                    assert p == py or (j >= 56 if p < py else j < 8)
-                    out[py, row, 64 + j if p == py else p * 8 + j % 8] = second[g, s]
-                for s in np.nonzero(third[g])[0]:
-                    p, j = divmod(int(s), 16)
-                    assert p == py or (j >= 8 if p < py else j < 8)
-                    out[py, m + row, 128 + j if p == py else p * 8 + j % 8] = third[g, s]
-                for s in np.nonzero(fourth[g])[0]:
-                    p, j = divmod(int(s), 4)
-                    out[py, 2 * m + row, p * 8 + j] = fourth[g, s]
-        out[py, 3 * m, 4:64:8] = 1
+        for q in range(QR):
+            g = min(max(64 * py + q - 2, 0), NY * 64 - 1)
+            for s in np.nonzero(second[g])[0]:
+                p, j = divmod(int(s), 64)
+                assert p == py or (j >= 56 if p < py else j < 8)
+                out[py, q, 64 + j if p == py else p * 8 + j % 8] = second[g, s]
+            for s in np.nonzero(third[g])[0]:
+                p, j = divmod(int(s), 16)
+                assert p == py or (j >= 8 if p < py else j < 8)
+                out[py, QM + q, 128 + j if p == py else p * 8 + j % 8] = third[g, s]
+            for s in np.nonzero(fourth[g])[0]:
+                p, j = divmod(int(s), 4)
+                out[py, 2 * QM + q, p * 8 + j] = fourth[g, s]
+        out[py, 3 * QM, 4:64:8] = 1
     return out
 
 
@@ -195,7 +195,7 @@
     cpool[...] = jnp.where((group == lane) & (col < TC), 1.0, 0.0).astype(BF16)
 
 
-def pooled_out(sums, row_pool_ref, px, send_ref, own_ref):
+def pooled_out(sums, row_pool_ref, px, send_ref, own_ref, corners=None):
     a, b, c = pieces(sums)
     rows = row_pool_ref[...]
     pooled = (dot(rows, a) + dot(rows, b) + dot(rows, c)).T
@@ -205,13 +205,25 @@
     left = jnp.where(lane < 64, pooled[0:8], coarse)
     right = jnp.where(lane < 64, pooled[24:32], coarse)
     for p in range(NX):
-        send_ref[p] = jnp.where(p < px, left, right)
-
-
-def start_kernel(table, exps, classes, gain, rpool_far, mgot_far, mown_far, dose, lo, hi, send, own, mgot, mown, *scratch):
-    cbuf, gbuf, cpool, rpool, sums, csem, gsem, tsem = scratch
-    px = lax.axis_index("gx")
+        send_ref[p, :8] = jnp.where(p < px, left, right)
+        if corners is not None:
+            send_ref[p, 8:] = jnp.where(p < px, *corners)
+
+
+def corner(strip):
+    lane = lax.broadcasted_iota(jnp.int32, (8, 128), 1)
+    both = jnp.where(lane < 64, strip[:8, :128].astype(F32), strip[:8, TR - 128 :].astype(F32))
+    more = jnp.where(lane < 64, strip[8:, :128].astype(F32), strip[8:, TR - 128 :].astype(F32))
+    inner = jnp.where(lane < 64, pltpu.roll(more, 16, 1), pltpu.roll(more, 112, 1))
+    return jnp.where((lane < 16) | (lane >= 112), both, inner)
+
+
+def start_kernel(table, exps, weights, classes, gain, *refs):
+    fars, refs = refs[:6], refs[6:]
+    dose, top, bottom, lo, hi, send, own, mgot, mown, matrix, spread_near, rpool_later = refs[:12]
+    cbuf, gbuf, cpool, rpool, sums, csem, gsem, tsem = refs[12:]
     steps = TR // SB
+    px, py = lax.axis_index("gx"), lax.axis_index("gy")
     loads = []
     for i in range(steps):
         rows = pl.ds(i * SB, SB)
@@ -223,13 +235,13 @@
         )
         for copy in loads[-1]:
             copy.start()
-    tables = (
-        pltpu.make_async_copy(rpool_far, rpool, tsem.at[0]),
-        pltpu.make_async_copy(mgot_far.at[px], mgot, tsem.at[1]),
-        pltpu.make_async_copy(mown_far.at[px], mown, tsem.at[2]),
-    )
-    for copy in tables:
-        copy.start()
+    nears = (rpool, mgot, mown, matrix, spread_near, rpool_later)
+    index = (None, px, px, py, None, None)
+    tables = []
+    for i in range(6):
+        source = fars[i] if index[i] is None else fars[i].at[index[i]]
+        tables.append(pltpu.make_async_copy(source, nears[i], tsem.at[i]))
+        tables[-1].start()
     fill_pool(cpool)
     for i in range(steps):
         for copy in loads[i]:
@@ -251,26 +263,37 @@
                 hi[:, rows] = value.astype(F32).T[SB - HALO :].astype(BF16)
         across = dot(dose[rows], cpool[...])
         sums[8 * i : 8 * i + 8] = jnp.sum(across.reshape(8, 16, 128), axis=1)
+    top[...] = dose[:HALO]
+    bottom[...] = dose[TR - HALO :]
     for copy in tables:
         copy.wait()
-    pooled_out(sums[...], rpool, px, send, own)
-
-
-def start(table, exps, classes, gain):
+    for level in range(3):
+        at = slice(QM * level, QM * (level + 1) if level < 2 else matrix.shape[0])
+        matrix[at] = matrix[at] * weights[level]
+    pooled_out(sums[...], rpool, px, send, own, (corner(lo), corner(hi)))
+
+
+def start(table, exps, weights, classes, gain):
     steps = TR // SB
     mgot, mown = column_matrices()
+    rows, cols, rpool = row_matrices(), column_spread(), row_pool(NB, 16, BLK // 16, 1)
     return pl.pallas_call(
         start_kernel,
-        in_specs=[SMEM, SMEM] + [HBM] * 5,
-        out_specs=[VMEM] * 7,
+        in_specs=[SMEM, SMEM, SMEM] + [HBM] * 8,
+        out_specs=[VMEM] * 12,
         out_shape=[
             pltpu.VMEM((TR, TC), BF16),
+            pltpu.VMEM((HALO, TC), BF16),
+            pltpu.VMEM((HALO, TC), BF16),
             pltpu.VMEM((HALO, TR), BF16),
             pltpu.VMEM((HALO, TR), BF16),
-            pltpu.HBM((NX, 8, 128), F32),
+            pltpu.HBM((NX, 16, 128), F32),
             pltpu.VMEM((32, 128), F32),
             pltpu.VMEM(mgot.shape[1:], F32),
             pltpu.VMEM(mown.shape[1:], F32),
+            pltpu.VMEM(rows.shape[1:], F32),
+            pltpu.VMEM(cols.shape, BF16),
+            pltpu.VMEM(rpool.shape, BF16),
         ],
         scratch_shapes=[
             pltpu.VMEM((TR, TC), jnp.int32),
@@ -280,49 +303,14 @@
             pltpu.VMEM((TR // 16, 128), F32),
             DMA((steps,)),
             DMA((steps,)),
-            DMA((3,)),
+            DMA((6,)),
         ],
         compiler_params=params(),
         name="start",
     )(
-        far(table), far(exps.T), far(classes), far(gain), far(jnp.asarray(row_pool(8, 8, 8, 0))),
-        far(jnp.asarray(mgot)), far(jnp.asarray(mown)),
+        far(table), far(exps.T), far(weights), far(classes), far(gain),
+        *[far(jnp.asarray(t)) for t in (row_pool(8, 8, 8, 0), mgot, mown, rows, cols, rpool)],
     )
-
-
-def pick_kernel(after, weights, matrix_far, spread_far, rpool_far, matrix, spread_near, rpool, buf, sems):
-    copies = (
-        pltpu.make_async_copy(matrix_far.at[lax.axis_index("gy")], buf, sems.at[0]),
-        pltpu.make_async_copy(spread_far, spread_near, sems.at[1]),
-        pltpu.make_async_copy(rpool_far, rpool, sems.at[2]),
-    )
-    for copy in copies:
-        copy.start()
-    for copy in copies:
-        copy.wait()
-    m, count = 16 * NB, buf.shape[0]
-    for level in range(3):
-        at = slice(m * level, m * (level + 1) if level < 2 else count)
-        scaled = buf[at] * weights[level]
-        first = scaled.astype(BF16)
-        matrix[at] = first
-        low = slice(count + at.start, count + at.stop)
-        matrix[low] = (scaled - first.astype(F32)).astype(BF16)
-
-
-def pick(after, weights):
-    table = row_matrices(NB, 0, BLK // 16, BLK // 16 + 2)
-    count, width = table.shape[1:]
-    more = [column_spread(), row_pool(NB, 16, BLK // 16, 1)]
-    return pl.pallas_call(
-        pick_kernel,
-        in_specs=[HBM, SMEM] + [HBM] * 3,
-        out_specs=[VMEM] * 3,
-        out_shape=[pltpu.VMEM((2 * count, width), BF16)] + [pltpu.VMEM(t.shape, BF16) for t in more],
-        scratch_shapes=[pltpu.VMEM((count, width), F32), DMA((3,))],
-        compiler_params=params(),
-        name="pick",
-    )(near(after), far(weights), *[far(jnp.asarray(t)) for t in [table, *more]])
 
 
 def side(strip_lo, strip_hi):
@@ -333,10 +321,10 @@
 
 def across_kernel(first, *refs):
     if first:
-        tile, lo, hi, got, own, mgot, mown, send, part = refs
+        got, own, mgot, mown, send, part = refs
     else:
         _, got, own, mgot, mown, send, part = refs
-    received = got[...].reshape(NX * 8, 128)
+    received = got[:, :8].reshape(NX * 8, 128)
     z = dot(mgot[...], received, precision=EXACT)
     mine = dot(mown[...], own[...], precision=EXACT)
     z = jnp.concatenate([z[:40] + mine, z[40:]], axis=0).T
@@ -345,32 +333,29 @@
     coarse = z[80:88]
     up = jnp.where(lane < 40, z[0:8], jnp.where(lane < 80, z[64:72], coarse))
     down = jnp.where(lane < 40, z[56:64], jnp.where(lane < 80, z[72:80], coarse))
-    py = lax.axis_index("gy")
+    px, py = lax.axis_index("gx"), lax.axis_index("gy")
     for p in range(NY):
         send[p, :8] = jnp.where(p < py, up, down)
     if first:
-        for n in range(EC // 128):
-            lanes = slice(128 * n, 128 * n + 128)
-            if n < TC // 128:
-                top, bottom = tile[:HALO, lanes].astype(F32), tile[TR - HALO :, lanes].astype(F32)
-            else:
-                top = side(lo[:, :128], hi[:, :128])[:HALO]
-                bottom = side(lo[:, TR - 128 :], hi[:, TR - 128 :])[128 - HALO :]
-            for p in range(NY):
-                send[p, 8 + HALO * n : 8 + HALO * (n + 1)] = jnp.where(p < py, top, bottom)
+        lo = jnp.where(px > 0, got[jnp.maximum(px - 1, 0), 8:], 0.0)
+        hi = jnp.where(px < NX - 1, got[jnp.minimum(px + 1, NX - 1), 8:], 0.0)
+        ends = []
+        for shift in (112, 16):
+            ends.append(side(*[jnp.concatenate([x, pltpu.roll(x, shift, 1)], axis=0) for x in (lo, hi)]))
+        for p in range(NY):
+            send[p, 8:] = jnp.where(p < py, ends[0][:HALO], ends[1][128 - HALO :])
 
 
 def across(first, extra, got, own, mgot, mown):
-    count = 8 + HALO * (EC // 128) if first else 8
-    specs = [VMEM] * 3 if first else [HBM]
+    count = 8 + HALO if first else 8
     return pl.pallas_call(
         functools.partial(across_kernel, first),
-        in_specs=specs + [VMEM] * 4,
+        in_specs=[VMEM] * 4 if first else [HBM] + [VMEM] * 4,
         out_specs=[VMEM] * 2,
         out_shape=[pltpu.VMEM((NY, count, 128), F32), pltpu.VMEM((80, 128), F32)],
         compiler_params=params(),
         name="across",
-    )(*([near(x) for x in extra] if first else [near(x) for x in extra]), near(got), near(own), near(mgot), near(mown))
+    )(*([] if first else [near(extra)]), near(got), near(own), near(mgot), near(mown))
 
 
 def column_pass(block, cols, half, at):
@@ -446,16 +431,12 @@
     )(near(dose), far(jnp.asarray(fine_columns())))
 
 
-def spread(received, part, matrix, cols, groups):
-    m = 16 * groups
-    count = matrix.shape[0] // 2
-    x, rest, _ = pieces(jnp.concatenate([received, part[...]], axis=0))
-    both = dot(matrix[...], x)
-    y = both[:count] + both[count:] + dot(matrix[:count], rest)
-    lane = lax.broadcasted_iota(jnp.int32, (m, 128), 1)
-    fourth = jnp.where(lane < 120, y[2 * m : 3 * m], jnp.where(lane == 120, y[3 * m : 3 * m + 1], 0.0))
-    a, b, _ = pieces(jnp.where(lane < 40, y[:m], jnp.where(lane < 80, y[m : 2 * m], fourth)))
-    return dot(a, cols) + dot(b, cols)
+def spread(received, part, matrix, cols):
+    y = dot(matrix[...], jnp.concatenate([received, part[...]], axis=0), precision=EXACT)
+    lane = lax.broadcasted_iota(jnp.int32, (QM, 128), 1)
+    fourth = jnp.where(lane < 120, y[2 * QM : 3 * QM], jnp.where(lane == 120, y[3 * QM : 3 * QM + 1], 0.0))
+    a, b, c = pieces(jnp.where(lane < 40, y[:QM], jnp.where(lane < 80, y[QM : 2 * QM], fourth)))
+    return dot(a, cols) + dot(b, cols) + dot(c, cols)
 
 
 def short_range(b, rows, half):
@@ -470,7 +451,8 @@
         row = b * BLK + 16 * n
         if not skip <= row < skip + count:
             continue
-        a, m, c = (grid[16 * b + n + k : 16 * b + n + k + 1] for k in range(3))
+        at = row // 16
+        a, m, c = (grid[at + k : at + k + 1] for k in range(3))
         back = jnp.concatenate([a + (t + 0.5) * (m - a), m + t * (c - m)], axis=0)
         full = 1.0 + (short[16 * n : 16 * n + 16] + back)
         out[row - skip : row - skip + 16] = (old_rows(row).astype(F32) * 2.0 / full).astype(out.dtype)
@@ -478,7 +460,7 @@
 
 def step_kernel(first, got, part, matrix, cols, rpool, dose, half, *refs):
     if first:
-        fcols_far, out, send, own, rows, cpool, grid, sums, hbuf, dbuf, fcols, lsem, fsem = refs
+        above, below, fcols_far, out, send, own, rows, cpool, grid, sums, hbuf, dbuf, fcols, lsem, fsem = refs
         loads = [pltpu.make_async_copy(fcols_far, fcols, fsem)]
         at = pl.ds(HALO, TR)
         loads.append(pltpu.make_async_copy(half.at[at], hbuf.at[at], lsem.at[0]))
@@ -491,13 +473,16 @@
     fill_rows(rows)
     fill_pool(cpool)
     received = got[:, :8].reshape(NY * 8, 128)
-    grid[...] = spread(received, part, matrix, cols[...], NB)
+    grid[...] = spread(received, part, matrix, cols[...])
     if first:
         py = lax.axis_index("gy")
         loads[0].wait()
-        for row, p, real in ((0, jnp.maximum(py - 1, 0), py > 0), (ER - HALO, jnp.minimum(py + 1, NY - 1), py < NY - 1)):
-            tiles = [got[p, 8 + HALO * n : 8 + HALO * (n + 1)] for n in range(EC // 128)]
-            values = jnp.where(real, jnp.concatenate(tiles, axis=1), 0.0).astype(BF16)
+        for row, strip, p, real in (
+            (0, above, jnp.maximum(py - 1, 0), py > 0),
+            (ER - HALO, below, jnp.minimum(py + 1, NY - 1), py < NY - 1),
+        ):
+            beside = jnp.where(real, got[p, 8:], 0.0).astype(BF16)
+            values = jnp.concatenate([strip[...], beside], axis=1)
             dbuf[row : row + HALO] = values
             column_pass(values, fcols, hbuf, slice(row, row + HALO))
         for copy in loads[1:]:
@@ -510,11 +495,12 @@
     pooled_out(sums[...], rpool, lax.axis_index("gx"), send, own)
 
 
-def step(first, got, part, dose, half, ops):
+def step(got, part, dose, half, ops, strips=None):
+    first = strips is not None
     scratch = [
         pltpu.VMEM((3, BLK, BLK + 32), BF16),
         pltpu.VMEM((EC, 128), BF16),
-        pltpu.VMEM((NB * 16, EC), F32),
+        pltpu.VMEM((QM, EC), F32),
         pltpu.VMEM((NB * 16, 128), F32),
     ]
     if first:
@@ -522,7 +508,7 @@
     place = far if first else near
     return pl.pallas_call(
         functools.partial(step_kernel, first),
-        in_specs=[VMEM] * 5 + ([HBM] * 3 if first else [VMEM] * 2),
+        in_specs=[VMEM] * 5 + ([HBM] * 2 + [VMEM] * 2 + [HBM] if first else [VMEM] * 2),
         out_specs=[VMEM] * 3,
         out_shape=[
             pltpu.VMEM((ER, EC), BF16),
@@ -535,13 +521,13 @@
         name="first_step" if first else "step",
     )(
         near(got), near(part), *[near(x) for x in ops], place(dose), place(half),
-        *([far(jnp.asarray(fine_columns()))] if first else []),
+        *([*[near(x) for x in strips], far(jnp.asarray(fine_columns()))] if first else []),
     )
 
 
 def finish_kernel(got, part, matrix, cols, dose, half, out, rows, made, grid, ssem):
     fill_rows(rows)
-    grid[...] = spread(got[...].reshape(NY * 8, 128), part, matrix, cols[:, :TC], NB)
+    grid[...] = spread(got[...].reshape(NY * 8, 128), part, matrix, cols[:, :TC])
     stores = []
     for b in range(NB):
         update(b, lambda row: dose[row : row + 16, :TC], short_range(b, rows, half), grid, made, HALO)
@@ -562,7 +548,7 @@
         scratch_shapes=[
             pltpu.VMEM((3, BLK, BLK + 32), BF16),
             pltpu.VMEM((TR, TC), F32),
-            pltpu.VMEM((NB * 16, TC), F32),
+            pltpu.VMEM((QM, TC), F32),
             DMA((NB,)),
         ],
         compiler_params=params(),
@@ -580,21 +566,23 @@
 
 
 def local(classes, exponents, gain_field, level_table, level_weights):
-    tile, lo, hi, send, own, mgot, mown = start(level_table, exponents, classes, gain_field)
+    tile, top, bottom, lo, hi, send, own, mgot, mown, *ops = start(
+        level_table, exponents, level_weights, classes, gain_field
+    )
     left, right = shifted(hi, "gx", 1), shifted(lo, "gx", -1)
+    above, below = shifted(bottom, "gy", 1), shifted(top, "gy", -1)
     got = exchanged(send, "gx")
-    send, part = across(True, (tile, left, right), got, own, mgot, mown)
+    send, part = across(True, None, got, own, mgot, mown)
     got = exchanged(send, "gy")
-    ops = pick(part, level_weights)
     half, dose = first_half(tile, left, right)
-    dose, send, own = step(True, got, part, dose, half, ops)
+    dose, send, own = step(got, part, dose, half, ops, (above, below))
     for sweep in range(2, ITERS + 1):
         got = exchanged(send, "gx")
         half = half_of(dose, EC if sweep < ITERS else TC)
-        send, part = across(False, (half,), got, own, mgot, mown)
+        send, part = across(False, half, got, own, mgot, mown)
         got = exchanged(send, "gy")
         if sweep < ITERS:
-            dose, send, own = step(False, got, part, dose, half, ops)
+            dose, send, own = step(got, part, dose, half, ops)
     return finish(got, part, dose, half, ops)
 
 

time: 129 us -> 131 us (1.016)
  starting transfers between devices: 39.5 us -> 47.3 us
  waiting for transfers between devices: 28.5 us -> 22.9 us
    ppermute x2 -> x4, starting transfers between devices: 4.43 us -> 11 us  [shifted(): lax.ppermute(x, axis, [(i, i + by) for i in range(n) if 0 <= i + by < n])]
    ppermute x2 -> x4, waiting for transfers between devices: 3.65 us -> 0.01 us  [shifted(): lax.ppermute(x, axis, [(i, i + by) for i in range(n) if 0 <= i + by < n])]
    all_to_all x5, waiting for transfers between devices: 24.8 us -> 22.9 us  [exchanged(): return lax.all_to_all(x, axis, 0, 0, tiled=True)]
    pallas_call x6 -> x5, Pallas kernels: 9.36 us -> 7.59 us  [the longest x1 5.41 us: start(): pl.pallas_call(start_kernel, in_specs=[SMEM, SMEM, SMEM] + [HBM] * 8, out...]
    all_to_all x5, starting transfers between devices: 35.1 us -> 36.4 us  [exchanged(): return lax.all_to_all(x, axis, 0, 0, tiled=True)]
  transfers between devices with their start and end apart: 7 -> 9, of which waited for: 6 -> 4; matrix products, arithmetic and copies ran while one was open for 0% -> 0% of each run, Pallas kernels for 9% -> 8%
where the time goes in v4:
time: 131 us; the launch traced here: 130 us
  starting transfers between devices  47.3 us (36%)
  Pallas kernels  31.3 us (24%)
  blocking collectives  28.2 us (22%)
  waiting for transfers between devices  22.9 us (17%)
    all_to_all x5, starting transfers between devices, exchanged(): return lax.all_to_all(x, axis, 0, 0, tiled=True)  36.4 us
    all_to_all x3, blocking collectives, exchanged(): return lax.all_to_all(x, axis, 0, 0, tiled=True)  28.2 us
    all_to_all x5, waiting for transfers between devices, exchanged(): return lax.all_to_all(x, axis, 0, 0, tiled=True)  22.9 us
    pallas_call x3, Pallas kernels, step(): pl.pallas_call(functools.partial(step_kernel, first), in_specs=[VMEM] * 5...  12 us
    ppermute x4, starting transfers between devices, shifted(): lax.ppermute(x, axis, [(i, i + by) for i in range(n) if 0 <= i + by < n])  11 us
    pallas_call x3, Pallas kernels, half_of(): pl.pallas_call(half_kernel, in_specs=[VMEM, HBM], out_specs=VMEM, out_sha...  5.7 us
    pallas_call x1, Pallas kernels, start(): pl.pallas_call(start_kernel, in_specs=[SMEM, SMEM, SMEM] + [HBM] * 8, out...  5.41 us
    pallas_call x1, Pallas kernels, first_half(): pl.pallas_call(first_half_kernel, in_specs=[VMEM] * 3 + [HBM], out_specs=...  3.79 us
  transfers between devices with their start and end apart: 9, of which 4 were waited for; matrix products, arithmetic and copies ran while one was open for 0% of the time, Pallas kernels for 8%

profile of v4, /device:TPU:1, one launch (start us, length us, event | category | flops | bytes accessed | tf_op | source)
XLA Modules:
  0.0 130.1 jit_solution(10104121975284756446)
XLA Ops:
  0.0 5.4 %start.1 = (bf16[1024,512]{1,0:T(8,128)(2,1)S(1)}, bf16[16,512]{1,0:T(8,128)(2,1)S(1)}, bf16[16,512]{1,0:T(8,128)(2,1)S(1)}, bf16[16,1024]{1,0:T(8,128)(2,1)S(1)...) custom-call(f32[8]{0:T(128)} %table.1, ...), custom_call_target="tpu_custom_call" | custom-call | tf_op jit(solution)/shard_map/start/pallas_call | solution.py:280
  5.4 11.9 %all-to-all-start = ((f32[32,16,128]{2,1,0:T(8,128)}), f32[32,16,128]{2,1,0:T(8,128)S(1)}, u32[]{:S(2)}, u32[]{:S(2)}) async-start(f32[32,16,128]{2,1,0:T(8,128)} %get-tuple-element.36), calls=%async_computation | async-start | bytes 524288 | tf_op jit(solution)/shard_map/all_to_all | solution.py:565
  17.3 3.1 %collective-permute-start = (bf16[16,1024]{1,0:T(8,128)(2,1)S(1)}, bf16[16,1024]{1,0:T(8,128)(2,1)S(1)}, u32[]{:S(2)}, u32[]{:S(2)}) collective-permute-start(bf16[16,1024]{1,0:T(8,128)(2,1)S(1)} %get-tuple-element.46), channel_id=1, source_target_pairs={{0,8},{8,16},{16,24},{24,32},{32,40},{40,48},{48,56},{56,64},{64,7... | collective-permute-start | bytes 98312 | tf_op jit(solution)/shard_map/ppermute | solution.py:561
  20.4 1.3 collective-permute-start.1
  21.7 4.6 %collective-permute-start.2 = (bf16[16,512]{1,0:T(8,128)(2,1)S(1)}, bf16[16,512]{1,0:T(8,128)(2,1)S(1)}, u32[]{:S(2)}, u32[]{:S(2)}) collective-permute-start(bf16[16,512]{1,0:T(8,128)(2,1)S(1)} %get-tuple-element.50), channel_id=1, source_target_pairs={{0,1},{1,2},{2,3},{3,4},{4,5},{5,6},{6,7},{8,9},{9,10},{10,11},{11... | collective-permute-start | bytes 49160 | tf_op jit(solution)/shard_map/ppermute | solution.py:561
  26.4 1.9 %collective-permute-start.3 = (bf16[16,512]{1,0:T(8,128)(2,1)S(1)}, bf16[16,512]{1,0:T(8,128)(2,1)S(1)}, u32[]{:S(2)}, u32[]{:S(2)}) collective-permute-start(bf16[16,512]{1,0:T(8,128)(2,1)S(1)} %get-tuple-element.51), channel_id=1, source_target_pairs={{1,0},{2,1},{3,2},{4,3},{5,4},{6,5},{7,6},{9,8},{10,9},{11,10},{12... | collective-permute-start | bytes 49160 | tf_op jit(solution)/shard_map/ppermute | solution.py:561
  29.4 7.3 %all-to-all-start.1 = ((f32[8,24,128]{2,1,0:T(8,128)}), f32[8,24,128]{2,1,0:T(8,128)S(1)}, u32[]{:S(2)}, u32[]{:S(2)}) async-start(f32[8,24,128]{2,1,0:T(8,128)} %get-tuple-element.40), calls=%async_computation.1 | async-start | bytes 196608 | tf_op jit(solution)/shard_map/all_to_all | solution.py:565
  36.7 3.8 %first_half.1 = (bf16[1056,640]{1,0:T(8,128)(2,1)}, bf16[1056,640]{1,0:T(8,128)(2,1)}) custom-call(bf16[1024,512]{1,0:T(8,128)(2,1)S(1)} %get-tuple-element.45.tile, bf16[16,1024]{1,0:T(8,128)(2,1)S(1)} %collective-permute-done.lo, bf16[16,1024]{1,0:T(8,128)(2,1)S(1)} %collective-permute-done.1.hi, bf16[512,256]{1,0:T(8,128)(2,1)} %constant.20.clone.cols_far.refs_2_), custom_call_target="tpu_custom_call" | custom-call | flops 1730150400 | bytes 4055040 | tf_op jit(solution)/shard_map/first_half/pallas_call | solution.py:395
  41.7 4.8 %first_step.1 = (bf16[1056,640]{1,0:T(8,128)(2,1)S(1)}, f32[32,8,128]{2,1,0:T(8,128)}, f32[32,128]{1,0:T(8,128)S(1)}) custom-call(f32[8,24,128]{2,1,0:T(8,128)S(1)} %all-to-all-done.1.got, f32[80,128]{1,0:T(8,128)S(1)} %get-tuple-element.41.part, f32[224,144]{1,0:T(8,128)S(1)} %get-tuple-element.42.matrix, bf16[128,640]{1,0:T(8,128)(2,1)S(1)} %get-tuple-element.43.cols, ...), custom_call_target="tpu_custom_call" | custom-call | tf_op jit(solution)/shard_map/first_step/pallas_call | solution.py:509
  46.4 9.3 %all-to-all-start.2 = ((f32[32,8,128]{2,1,0:T(8,128)}), f32[32,8,128]{2,1,0:T(8,128)S(1)}, u32[]{:S(2)}, u32[]{:S(2)}) async-start(f32[32,8,128]{2,1,0:T(8,128)} %get-tuple-element.53), calls=%async_computation.2 | async-start | bytes 262144 | tf_op jit(solution)/shard_map/all_to_all | solution.py:565
  55.7 2.0 %half.3.refs_0_ = bf16[1056,640]{1,0:T(8,128)(2,1)S(1)} custom-call(bf16[1056,640]{1,0:T(8,128)(2,1)S(1)} %get-tuple-element.52.dose, bf16[512,256]{1,0:T(8,128)(2,1)} %constant.20.clone.cols_far.refs_2_), custom_call_target="tpu_custom_call" | custom-call | flops 1730150400 | bytes 4055040 | tf_op jit(solution)/shard_map/half/pallas_call | solution.py:422
  57.7 7.2 %all-to-all-done.2.refs_1_ = f32[32,8,128]{2,1,0:T(8,128)S(1)} async-done(((f32[32,8,128]{2,1,0:T(8,128)}), f32[32,8,128]{2,1,0:T(8,128)S(1)}, u32[]{:S(2)}, u32[]{:S(2)}) %all-to-all-start.2) | async-done | bytes 131104 | tf_op jit(solution)/shard_map/all_to_all | solution.py:565
  65.3 9.9 %all_to_all.40.got = f32[8,8,128]{2,1,0:T(8,128)S(1)} all-to-all(f32[8,8,128]{2,1,0:T(8,128)S(1)} %get-tuple-element.55), channel_id=1, replica_groups=mesh['gx'=32,'gy'=8] {'gy'}, dimensions={0} | all-to-all | bytes 65536 | tf_op jit(solution)/shard_map/all_to_all | solution.py:565
  75.2 3.6 %step.2 = (bf16[1056,640]{1,0:T(8,128)(2,1)S(1)}, f32[32,8,128]{2,1,0:T(8,128)}, f32[32,128]{1,0:T(8,128)S(1)}) custom-call(f32[8,8,128]{2,1,0:T(8,128)S(1)} %all_to_all.40.got, f32[80,128]{1,0:T(8,128)S(1)} %get-tuple-element.56.part, f32[224,144]{1,0:T(8,128)S(1)} %get-tuple-element.42.matrix, ...), custom_call_target="tpu_custom_call", output_to_operand_aliasing={{0}: (5, {})} | custom-call | tf_op jit(solution)/shard_map/step/pallas_call | solution.py:509
  78.8 4.0 %all-to-all-start.4 = ((f32[32,8,128]{2,1,0:T(8,128)}), f32[32,8,128]{2,1,0:T(8,128)S(1)}, u32[]{:S(2)}, u32[]{:S(2)}) async-start(f32[32,8,128]{2,1,0:T(8,128)} %get-tuple-element.58), calls=%async_computation.4 | async-start | bytes 262144 | tf_op jit(solution)/shard_map/all_to_all | solution.py:565
  82.9 2.0 %half.4.refs_0_ = bf16[1056,640]{1,0:T(8,128)(2,1)S(1)} custom-call(bf16[1056,640]{1,0:T(8,128)(2,1)S(1)} %get-tuple-element.57.dose, bf16[512,256]{1,0:T(8,128)(2,1)} %constant.20.clone.cols_far.refs_2_), custom_call_target="tpu_custom_call" | custom-call | flops 1730150400 | bytes 4055040 | tf_op jit(solution)/shard_map/half/pallas_call | solution.py:422
  84.9 7.2 %all-to-all-done.4.refs_1_ = f32[32,8,128]{2,1,0:T(8,128)S(1)} async-done(((f32[32,8,128]{2,1,0:T(8,128)}), f32[32,8,128]{2,1,0:T(8,128)S(1)}, u32[]{:S(2)}, u32[]{:S(2)}) %all-to-all-start.4) | async-done | bytes 131104 | tf_op jit(solution)/shard_map/all_to_all | solution.py:565
  92.4 9.1 %all_to_all.41.got = f32[8,8,128]{2,1,0:T(8,128)S(1)} all-to-all(f32[8,8,128]{2,1,0:T(8,128)S(1)} %get-tuple-element.60), channel_id=1, replica_groups=mesh['gx'=32,'gy'=8] {'gy'}, dimensions={0} | all-to-all | bytes 65536 | tf_op jit(solution)/shard_map/all_to_all | solution.py:565
  101.5 3.6 %step.3 = (bf16[1056,640]{1,0:T(8,128)(2,1)S(1)}, f32[32,8,128]{2,1,0:T(8,128)}, f32[32,128]{1,0:T(8,128)S(1)}) custom-call(f32[8,8,128]{2,1,0:T(8,128)S(1)} %all_to_all.41.got, f32[80,128]{1,0:T(8,128)S(1)} %get-tuple-element.61.part, f32[224,144]{1,0:T(8,128)S(1)} %get-tuple-element.42.matrix, ...), custom_call_target="tpu_custom_call", output_to_operand_aliasing={{0}: (5, {})} | custom-call | tf_op jit(solution)/shard_map/step/pallas_call | solution.py:509
  105.1 3.9 %all-to-all-start.6 = ((f32[32,8,128]{2,1,0:T(8,128)}), f32[32,8,128]{2,1,0:T(8,128)S(1)}, u32[]{:S(2)}, u32[]{:S(2)}) async-start(f32[32,8,128]{2,1,0:T(8,128)} %get-tuple-element.63), calls=%async_computation.6 | async-start | bytes 262144 | tf_op jit(solution)/shard_map/all_to_all | solution.py:565
  109.0 1.7 %half.5.refs_0_ = bf16[1056,512]{1,0:T(8,128)(2,1)S(1)} custom-call(bf16[1056,640]{1,0:T(8,128)(2,1)S(1)} %get-tuple-element.62.dose, bf16[512,256]{1,0:T(8,128)(2,1)} %constant.20.clone.cols_far.refs_2_), custom_call_target="tpu_custom_call" | custom-call | flops 1730150400 | bytes 4055040 | tf_op jit(solution)/shard_map/half/pallas_call | solution.py:422
  110.7 7.4 %all-to-all-done.6.refs_1_ = f32[32,8,128]{2,1,0:T(8,128)S(1)} async-done(((f32[32,8,128]{2,1,0:T(8,128)}), f32[32,8,128]{2,1,0:T(8,128)S(1)}, u32[]{:S(2)}, u32[]{:S(2)}) %all-to-all-start.6) | async-done | bytes 131104 | tf_op jit(solution)/shard_map/all_to_all | solution.py:565
  118.6 9.1 %all_to_all.42.got = f32[8,8,128]{2,1,0:T(8,128)S(1)} all-to-all(f32[8,8,128]{2,1,0:T(8,128)S(1)} %get-tuple-element.65), channel_id=1, replica_groups=mesh['gx'=32,'gy'=8] {'gy'}, dimensions={0} | all-to-all | bytes 65536 | tf_op jit(solution)/shard_map/all_to_all | solution.py:565
  127.7 2.2 %finish.1 = f32[1024,512]{1,0:T(8,128)} custom-call(f32[8,8,128]{2,1,0:T(8,128)S(1)} %all_to_all.42.got, f32[80,128]{1,0:T(8,128)S(1)} %get-tuple-element.66.part, f32[224,144]{1,0:T(8,128)S(1)} %get-tuple-element.42.matrix, bf16[128,640]{1,0:T(8,128)(2,1)S(1)} %get-tuple-element.43.cols, bf16[1056,640]{1,0:T(8,128)(2,1)S(1)} %get-tuple-element.62.dose, ...), custom_call_target="tpu_custom_call" | custom-call | tf_op jit(solution)/shard_map/finish/pallas_call | solution.py:543
  (10 shorter events, 3.3 us)
Async XLA Ops:
  5.4 22.9 %all-to-all-start = ((f32[32,16,128]{2,1,0:T(8,128)}), f32[32,16,128]{2,1,0:T(8,128)S(1)}, u32[]{:S(2)}, u32[]{:S(2)}) async-start(f32[32,16,128]{2,1,0:T(8,128)} %get-tuple-element.36), calls=%async_computation | async-start | bytes 524288 | tf_op jit(solution)/shard_map/all_to_all | solution.py:565
  17.3 19.4 %collective-permute-start = (bf16[16,1024]{1,0:T(8,128)(2,1)S(1)}, bf16[16,1024]{1,0:T(8,128)(2,1)S(1)}, u32[]{:S(2)}, u32[]{:S(2)}) collective-permute-start(bf16[16,1024]{1,0:T(8,128)(2,1)S(1)} %get-tuple-element.46), channel_id=1, source_target_pairs={{0,8},{8,16},{16,24},{24,32},{32,40},{40,48},{48,56},{56,64},{64,7... | collective-permute-start | bytes 98312 | tf_op jit(solution)/shard_map/ppermute | solution.py:561
  20.4 16.2 %collective-permute-start.1 = (bf16[16,1024]{1,0:T(8,128)(2,1)S(1)}, bf16[16,1024]{1,0:T(8,128)(2,1)S(1)}, u32[]{:S(2)}, u32[]{:S(2)}) collective-permute-start(bf16[16,1024]{1,0:T(8,128)(2,1)S(1)} %get-tuple-element.47), channel_id=1, source_target_pairs={{8,0},{16,8},{24,16},{32,24},{40,32},{48,40},{56,48},{64,56},{72,6... | collective-permute-start | bytes 98312 | tf_op jit(solution)/shard_map/ppermute | solution.py:561
  21.7 18.7 %collective-permute-start.2 = (bf16[16,512]{1,0:T(8,128)(2,1)S(1)}, bf16[16,512]{1,0:T(8,128)(2,1)S(1)}, u32[]{:S(2)}, u32[]{:S(2)}) collective-permute-start(bf16[16,512]{1,0:T(8,128)(2,1)S(1)} %get-tuple-element.50), channel_id=1, source_target_pairs={{0,1},{1,2},{2,3},{3,4},{4,5},{5,6},{6,7},{8,9},{9,10},{10,11},{11... | collective-permute-start | bytes 49160 | tf_op jit(solution)/shard_map/ppermute | solution.py:561
  26.4 14.1 %collective-permute-start.3 = (bf16[16,512]{1,0:T(8,128)(2,1)S(1)}, bf16[16,512]{1,0:T(8,128)(2,1)S(1)}, u32[]{:S(2)}, u32[]{:S(2)}) collective-permute-start(bf16[16,512]{1,0:T(8,128)(2,1)S(1)} %get-tuple-element.51), channel_id=1, source_target_pairs={{1,0},{2,1},{3,2},{4,3},{5,4},{6,5},{7,6},{9,8},{10,9},{11,10},{12... | collective-permute-start | bytes 49160 | tf_op jit(solution)/shard_map/ppermute | solution.py:561
  29.4 12.3 %all-to-all-start.1 = ((f32[8,24,128]{2,1,0:T(8,128)}), f32[8,24,128]{2,1,0:T(8,128)S(1)}, u32[]{:S(2)}, u32[]{:S(2)}) async-start(f32[8,24,128]{2,1,0:T(8,128)} %get-tuple-element.40), calls=%async_computation.1 | async-start | bytes 196608 | tf_op jit(solution)/shard_map/all_to_all | solution.py:565
  46.4 18.4 %all-to-all-start.2 = ((f32[32,8,128]{2,1,0:T(8,128)}), f32[32,8,128]{2,1,0:T(8,128)S(1)}, u32[]{:S(2)}, u32[]{:S(2)}) async-start(f32[32,8,128]{2,1,0:T(8,128)} %get-tuple-element.53), calls=%async_computation.2 | async-start | bytes 262144 | tf_op jit(solution)/shard_map/all_to_all | solution.py:565
  78.8 13.2 %all-to-all-start.4 = ((f32[32,8,128]{2,1,0:T(8,128)}), f32[32,8,128]{2,1,0:T(8,128)S(1)}, u32[]{:S(2)}, u32[]{:S(2)}) async-start(f32[32,8,128]{2,1,0:T(8,128)} %get-tuple-element.58), calls=%async_computation.4 | async-start | bytes 262144 | tf_op jit(solution)/shard_map/all_to_all | solution.py:565
  105.1 13.0 %all-to-all-start.6 = ((f32[32,8,128]{2,1,0:T(8,128)}), f32[32,8,128]{2,1,0:T(8,128)S(1)}, u32[]{:S(2)}, u32[]{:S(2)}) async-start(f32[32,8,128]{2,1,0:T(8,128)} %get-tuple-element.63), calls=%async_computation.6 | async-start | bytes 262144 | tf_op jit(solution)/shard_map/all_to_all | solution.py:565

commit v5 on v4

--- a/solution.py
+++ b/solution.py
@@ -319,11 +319,7 @@
     return jnp.concatenate([strip_hi.astype(F32).T, empty, strip_lo.astype(F32).T], axis=1)
 
 
-def across_kernel(first, *refs):
-    if first:
-        got, own, mgot, mown, send, part = refs
-    else:
-        _, got, own, mgot, mown, send, part = refs
+def across_kernel(first, got, own, mgot, mown, send, part):
     received = got[:, :8].reshape(NX * 8, 128)
     z = dot(mgot[...], received, precision=EXACT)
     mine = dot(mown[...], own[...], precision=EXACT)
@@ -346,16 +342,16 @@
             send[p, 8:] = jnp.where(p < py, ends[0][:HALO], ends[1][128 - HALO :])
 
 
-def across(first, extra, got, own, mgot, mown):
+def across(first, got, own, mgot, mown):
     count = 8 + HALO if first else 8
     return pl.pallas_call(
         functools.partial(across_kernel, first),
-        in_specs=[VMEM] * 4 if first else [HBM] + [VMEM] * 4,
+        in_specs=[VMEM] * 4,
         out_specs=[VMEM] * 2,
         out_shape=[pltpu.VMEM((NY, count, 128), F32), pltpu.VMEM((80, 128), F32)],
         compiler_params=params(),
         name="across",
-    )(*([] if first else [near(extra)]), near(got), near(own), near(mgot), near(mown))
+    )(near(got), near(own), near(mgot), near(mown))
 
 
 def column_pass(block, cols, half, at):
@@ -367,21 +363,19 @@
         half[at, 512:] = dot(join(3, 4, 0), cols[:384, :128]).astype(BF16)
 
 
-def first_half_kernel(tile, lo, hi, cols_far, half_far, dose_far, half, dose, cols, sems, csem):
+def first_half_kernel(tile, lo, hi, cols_far, half_far, sides, half, cols, sems, csem):
     load = pltpu.make_async_copy(cols_far, cols, csem)
     load.start()
     stores = []
     for n in range(TR // SB):
         rows, begin = slice(n * SB, (n + 1) * SB), HALO + n * SB
-        dose[begin : begin + SB, :TC] = tile[rows]
-        dose[begin : begin + SB, TC:] = side(lo[:, rows], hi[:, rows]).astype(BF16)
+        beside = side(lo[:, rows], hi[:, rows]).astype(BF16)
+        sides[rows] = beside
         if n == 0:
             load.wait()
-        column_pass(dose[begin : begin + SB], cols, half, slice(begin, begin + SB))
+        column_pass(jnp.concatenate([tile[rows], beside], axis=1), cols, half, slice(begin, begin + SB))
         at = pl.ds(begin, SB)
-        stores.append(pltpu.make_async_copy(half.at[at], half_far.at[at], sems.at[0, n]))
-        stores[-1].start()
-        stores.append(pltpu.make_async_copy(dose.at[at], dose_far.at[at], sems.at[1, n]))
+        stores.append(pltpu.make_async_copy(half.at[at], half_far.at[at], sems.at[n]))
         stores[-1].start()
     for copy in stores:
         copy.wait()
@@ -395,15 +389,9 @@
     return pl.pallas_call(
         first_half_kernel,
         in_specs=[VMEM] * 3 + [HBM],
-        out_specs=[HBM, HBM],
-        out_shape=[pltpu.HBM((ER, EC), BF16)] * 2,
-        scratch_shapes=[
-            pltpu.VMEM((ER, EC), BF16),
-            pltpu.VMEM((ER, EC), BF16),
-            pltpu.VMEM((512, 256), BF16),
-            DMA((2, TR // SB)),
-            DMA,
-        ],
+        out_specs=[HBM, VMEM],
+        out_shape=[pltpu.HBM((ER, EC), BF16), pltpu.VMEM((TR, EC - TC), BF16)],
+        scratch_shapes=[pltpu.VMEM((ER, EC), BF16), pltpu.VMEM((512, 256), BF16), DMA((TR // SB,)), DMA],
         compiler_params=params(),
         cost_estimate=half_cost(),
         name="first_half",
@@ -460,16 +448,16 @@
 
 def step_kernel(first, got, part, matrix, cols, rpool, dose, half, *refs):
     if first:
-        above, below, fcols_far, out, send, own, rows, cpool, grid, sums, hbuf, dbuf, fcols, lsem, fsem = refs
+        sides, above, below, fcols_far, out, send, own, rows, cpool, grid, sums, hbuf, fcols, lsem, fsem = refs
         loads = [pltpu.make_async_copy(fcols_far, fcols, fsem)]
         at = pl.ds(HALO, TR)
-        loads.append(pltpu.make_async_copy(half.at[at], hbuf.at[at], lsem.at[0]))
-        loads.append(pltpu.make_async_copy(dose.at[at], dbuf.at[at], lsem.at[1]))
+        loads.append(pltpu.make_async_copy(half.at[at], hbuf.at[at], lsem))
         for copy in loads:
             copy.start()
     else:
         out, send, own, rows, cpool, grid, sums = refs
-        dbuf, hbuf = dose, half
+        hbuf = half
+    edge = {}
     fill_rows(rows)
     fill_pool(cpool)
     received = got[:, :8].reshape(NY * 8, 128)
@@ -483,12 +471,21 @@
         ):
             beside = jnp.where(real, got[p, 8:], 0.0).astype(BF16)
             values = jnp.concatenate([strip[...], beside], axis=1)
-            dbuf[row : row + HALO] = values
+            edge[row] = values
             column_pass(values, fcols, hbuf, slice(row, row + HALO))
         for copy in loads[1:]:
             copy.wait()
+
+    def old_rows(row):
+        if row in edge:
+            return edge[row]
+        if first:
+            at = slice(row - HALO, row - HALO + 16)
+            return jnp.concatenate([dose[at], sides[at]], axis=1)
+        return dose[row : row + 16]
+
     for b in range(NB):
-        update(b, lambda row: dbuf[row : row + 16], short_range(b, rows, hbuf), grid, out, 0)
+        update(b, old_rows, short_range(b, rows, hbuf), grid, out, 0)
         pooled = dot(out[b * BLK : (b + 1) * BLK], cpool[...])
         pooled = jnp.sum(pooled.reshape(BLK // 16, 16, 128), axis=1)
         sums[16 * b : 16 * b + 16] = jnp.concatenate([pooled, jnp.zeros((16 - BLK // 16, 128), F32)], axis=0)
@@ -504,11 +501,10 @@
         pltpu.VMEM((NB * 16, 128), F32),
     ]
     if first:
-        scratch += [pltpu.VMEM((ER, EC), BF16)] * 2 + [pltpu.VMEM((512, 256), BF16), DMA((2,)), DMA]
-    place = far if first else near
+        scratch += [pltpu.VMEM((ER, EC), BF16), pltpu.VMEM((512, 256), BF16), DMA, DMA]
     return pl.pallas_call(
         functools.partial(step_kernel, first),
-        in_specs=[VMEM] * 5 + ([HBM] * 2 + [VMEM] * 2 + [HBM] if first else [VMEM] * 2),
+        in_specs=[VMEM] * 6 + ([HBM] + [VMEM] * 3 + [HBM] if first else [VMEM]),
         out_specs=[VMEM] * 3,
         out_shape=[
             pltpu.VMEM((ER, EC), BF16),
@@ -520,7 +516,7 @@
         compiler_params=params(),
         name="first_step" if first else "step",
     )(
-        near(got), near(part), *[near(x) for x in ops], place(dose), place(half),
+        near(got), near(part), *[near(x) for x in ops], near(dose), far(half) if first else near(half),
         *([*[near(x) for x in strips], far(jnp.asarray(fine_columns()))] if first else []),
     )
 
@@ -572,14 +568,14 @@
     left, right = shifted(hi, "gx", 1), shifted(lo, "gx", -1)
     above, below = shifted(bottom, "gy", 1), shifted(top, "gy", -1)
     got = exchanged(send, "gx")
-    send, part = across(True, None, got, own, mgot, mown)
+    send, part = across(True, got, own, mgot, mown)
     got = exchanged(send, "gy")
-    half, dose = first_half(tile, left, right)
-    dose, send, own = step(got, part, dose, half, ops, (above, below))
+    half, sides = first_half(tile, left, right)
+    dose, send, own = step(got, part, tile, half, ops, (sides, above, below))
     for sweep in range(2, ITERS + 1):
         got = exchanged(send, "gx")
         half = half_of(dose, EC if sweep < ITERS else TC)
-        send, part = across(False, half, got, own, mgot, mown)
+        send, part = across(False, got, own, mgot, mown)
         got = exchanged(send, "gy")
         if sweep < ITERS:
             dose, send, own = step(got, part, dose, half, ops)

time: 131 us -> 134 us (1.023)
  blocking collectives: 28.2 us -> 44.4 us
  waiting for transfers between devices: 22.9 us -> 10.4 us
    all_to_all x3, blocking collectives: 28.2 us -> 44.4 us  [exchanged(): return lax.all_to_all(x, axis, 0, 0, tiled=True)]
    all_to_all x5, waiting for transfers between devices: 22.9 us -> 10.4 us  [exchanged(): return lax.all_to_all(x, axis, 0, 0, tiled=True)]
    pallas_call x4, Pallas kernels: 2.18 us -> 4.06 us  [across(): pl.pallas_call(functools.partial(across_kernel, first), in_specs=[VMEM] *...]
  transfers between devices with their start and end apart: 9 -> 9, of which waited for: 4 -> 4; matrix products, arithmetic and copies ran while one was open for 0% -> 0% of each run, Pallas kernels for 8% -> 7%
where the time goes in v5:
time: 134 us; the launch traced here: 133 us
  starting transfers between devices  46.2 us (34%)
  blocking collectives  44.4 us (33%)
  Pallas kernels  31.7 us (24%)
  waiting for transfers between devices  10.4 us (8%)
    all_to_all x3, blocking collectives, exchanged(): return lax.all_to_all(x, axis, 0, 0, tiled=True)  44.4 us
    all_to_all x5, starting transfers between devices, exchanged(): return lax.all_to_all(x, axis, 0, 0, tiled=True)  35.3 us
    pallas_call x3, Pallas kernels, step(): pl.pallas_call(functools.partial(step_kernel, first), in_specs=[VMEM] * 6...  11.3 us
    ppermute x4, starting transfers between devices, shifted(): lax.ppermute(x, axis, [(i, i + by) for i in range(n) if 0 <= i + by < n])  11 us
    all_to_all x5, waiting for transfers between devices, exchanged(): return lax.all_to_all(x, axis, 0, 0, tiled=True)  10.4 us
    pallas_call x3, Pallas kernels, half_of(): pl.pallas_call(half_kernel, in_specs=[VMEM, HBM], out_specs=VMEM, out_sha...  5.69 us
    pallas_call x1, Pallas kernels, start(): pl.pallas_call(start_kernel, in_specs=[SMEM, SMEM, SMEM] + [HBM] * 8, out...  5.41 us
    pallas_call x4, Pallas kernels, across(): pl.pallas_call(functools.partial(across_kernel, first), in_specs=[VMEM] *...  4.06 us
  transfers between devices with their start and end apart: 9, of which 4 were waited for; matrix products, arithmetic and copies ran while one was open for 0% of the time, Pallas kernels for 7%

profile of v5, /device:TPU:1, one launch (start us, length us, event | category | flops | bytes accessed | tf_op | source)
XLA Modules:
  0.0 133.1 jit_solution(2817425278843067844)
XLA Ops:
  0.0 5.4 %start.1 = (bf16[1024,512]{1,0:T(8,128)(2,1)S(1)}, bf16[16,512]{1,0:T(8,128)(2,1)S(1)}, bf16[16,512]{1,0:T(8,128)(2,1)S(1)}, bf16[16,1024]{1,0:T(8,128)(2,1)S(1)...) custom-call(f32[8]{0:T(128)} %table.1, ...), custom_call_target="tpu_custom_call" | custom-call | tf_op jit(solution)/shard_map/start/pallas_call | solution.py:280
  5.4 11.9 %all-to-all-start = ((f32[32,16,128]{2,1,0:T(8,128)}), f32[32,16,128]{2,1,0:T(8,128)S(1)}, u32[]{:S(2)}, u32[]{:S(2)}) async-start(f32[32,16,128]{2,1,0:T(8,128)} %get-tuple-element.36), calls=%async_computation | async-start | bytes 524288 | tf_op jit(solution)/shard_map/all_to_all | solution.py:561
  17.3 3.1 %collective-permute-start = (bf16[16,1024]{1,0:T(8,128)(2,1)S(1)}, bf16[16,1024]{1,0:T(8,128)(2,1)S(1)}, u32[]{:S(2)}, u32[]{:S(2)}) collective-permute-start(bf16[16,1024]{1,0:T(8,128)(2,1)S(1)} %get-tuple-element.46), channel_id=1, source_target_pairs={{0,8},{8,16},{16,24},{24,32},{32,40},{40,48},{48,56},{56,64},{64,7... | collective-permute-start | bytes 98312 | tf_op jit(solution)/shard_map/ppermute | solution.py:557
  21.7 4.6 %collective-permute-start.2 = (bf16[16,512]{1,0:T(8,128)(2,1)S(1)}, bf16[16,512]{1,0:T(8,128)(2,1)S(1)}, u32[]{:S(2)}, u32[]{:S(2)}) collective-permute-start(bf16[16,512]{1,0:T(8,128)(2,1)S(1)} %get-tuple-element.50), channel_id=1, source_target_pairs={{0,1},{1,2},{2,3},{3,4},{4,5},{5,6},{6,7},{8,9},{9,10},{10,11},{11... | collective-permute-start | bytes 49160 | tf_op jit(solution)/shard_map/ppermute | solution.py:557
  26.4 1.9 %collective-permute-start.3 = (bf16[16,512]{1,0:T(8,128)(2,1)S(1)}, bf16[16,512]{1,0:T(8,128)(2,1)S(1)}, u32[]{:S(2)}, u32[]{:S(2)}) collective-permute-start(bf16[16,512]{1,0:T(8,128)(2,1)S(1)} %get-tuple-element.51), channel_id=1, source_target_pairs={{1,0},{2,1},{3,2},{4,3},{5,4},{6,5},{7,6},{9,8},{10,9},{11,10},{12... | collective-permute-start | bytes 49160 | tf_op jit(solution)/shard_map/ppermute | solution.py:557
  29.4 7.3 %all-to-all-start.1 = ((f32[8,24,128]{2,1,0:T(8,128)}), f32[8,24,128]{2,1,0:T(8,128)S(1)}, u32[]{:S(2)}, u32[]{:S(2)}) async-start(f32[8,24,128]{2,1,0:T(8,128)} %get-tuple-element.40), calls=%async_computation.1 | async-start | bytes 196608 | tf_op jit(solution)/shard_map/all_to_all | solution.py:561
  36.7 3.0 %first_half.1 = (bf16[1056,640]{1,0:T(8,128)(2,1)}, bf16[1024,128]{1,0:T(8,128)(2,1)S(1)}) custom-call(bf16[1024,512]{1,0:T(8,128)(2,1)S(1)} %get-tuple-element.45.tile.dose, bf16[16,1024]{1,0:T(8,128)(2,1)S(1)} %collective-permute-done.lo, bf16[16,1024]{1,0:T(8,128)(2,1)S(1)} %collective-permute-done.1.hi, bf16[512,256]{1,0:T(8,128)(2,1)} %constant.20.clone.cols_far.refs_3_), custom_call_target="tpu_custom_call" | custom-call | flops 1730150400 | bytes 4055040 | tf_op jit(solution)/shard_map/first_half/pallas_call | solution.py:389
  39.7 1.9 %all-to-all-done.1.got = f32[8,24,128]{2,1,0:T(8,128)S(1)} async-done(((f32[8,24,128]{2,1,0:T(8,128)}), f32[8,24,128]{2,1,0:T(8,128)S(1)}, u32[]{:S(2)}, u32[]{:S(2)}) %all-to-all-start.1) | async-done | bytes 98336 | tf_op jit(solution)/shard_map/all_to_all | solution.py:561
  41.7 4.0 %first_step.1 = (bf16[1056,640]{1,0:T(8,128)(2,1)S(1)}, f32[32,8,128]{2,1,0:T(8,128)}, f32[32,128]{1,0:T(8,128)S(1)}) custom-call(f32[8,24,128]{2,1,0:T(8,128)S(1)} %all-to-all-done.1.got, f32[80,128]{1,0:T(8,128)S(1)} %get-tuple-element.41.part, f32[224,144]{1,0:T(8,128)S(1)} %get-tuple-element.42.matrix, bf16[128,640]{1,0:T(8,128)(2,1)S(1)} %get-tuple-element.43.cols, ...), custom_call_target="tpu_custom_call" | custom-call | tf_op jit(solution)/shard_map/first_step/pallas_call | solution.py:505
  45.7 18.4 %all_to_all.40.got = f32[32,8,128]{2,1,0:T(8,128)S(1)} all-to-all(f32[32,8,128]{2,1,0:T(8,128)} %get-tuple-element.52), channel_id=1, replica_groups=mesh['gx'=32,'gy'=8] {'gx'}, dimensions={0} | all-to-all | bytes 262144 | tf_op jit(solution)/shard_map/all_to_all | solution.py:561
  65.1 5.5 %all-to-all-start.3 = ((f32[8,8,128]{2,1,0:T(8,128)}), f32[8,8,128]{2,1,0:T(8,128)S(1)}, u32[]{:S(2)}, u32[]{:S(2)}) async-start(f32[8,8,128]{2,1,0:T(8,128)} %get-tuple-element.54), calls=%async_computation.3 | async-start | bytes 65536 | tf_op jit(solution)/shard_map/all_to_all | solution.py:561
  70.6 2.0 %half.3 = bf16[1056,640]{1,0:T(8,128)(2,1)S(1)} custom-call(bf16[1056,640]{1,0:T(8,128)(2,1)S(1)} %get-tuple-element.56.dose, bf16[512,256]{1,0:T(8,128)(2,1)} %constant.20.clone.cols_far.refs_3_), custom_call_target="tpu_custom_call" | custom-call | flops 1730150400 | bytes 4055040 | tf_op jit(solution)/shard_map/half/pallas_call | solution.py:410
  72.6 2.7 %all-to-all-done.3.got = f32[8,8,128]{2,1,0:T(8,128)S(1)} async-done(((f32[8,8,128]{2,1,0:T(8,128)}), f32[8,8,128]{2,1,0:T(8,128)S(1)}, u32[]{:S(2)}, u32[]{:S(2)}) %all-to-all-start.3) | async-done | bytes 32800 | tf_op jit(solution)/shard_map/all_to_all | solution.py:561
  75.3 3.6 %step.2 = (bf16[1056,640]{1,0:T(8,128)(2,1)S(1)}, f32[32,8,128]{2,1,0:T(8,128)}, f32[32,128]{1,0:T(8,128)S(1)}) custom-call(f32[8,8,128]{2,1,0:T(8,128)S(1)} %all-to-all-done.3.got, f32[80,128]{1,0:T(8,128)S(1)} %get-tuple-element.55.part, f32[224,144]{1,0:T(8,128)S(1)} %get-tuple-element.42.matrix, ...), custom_call_target="tpu_custom_call", output_to_operand_aliasing={{0}: (5, {})} | custom-call | tf_op jit(solution)/shard_map/step/pallas_call | solution.py:505
  79.0 13.0 %all_to_all.41.got = f32[32,8,128]{2,1,0:T(8,128)S(1)} all-to-all(f32[32,8,128]{2,1,0:T(8,128)} %get-tuple-element.57), channel_id=1, replica_groups=mesh['gx'=32,'gy'=8] {'gx'}, dimensions={0} | all-to-all | bytes 262144 | tf_op jit(solution)/shard_map/all_to_all | solution.py:561
  93.0 5.3 %all-to-all-start.5 = ((f32[8,8,128]{2,1,0:T(8,128)}), f32[8,8,128]{2,1,0:T(8,128)S(1)}, u32[]{:S(2)}, u32[]{:S(2)}) async-start(f32[8,8,128]{2,1,0:T(8,128)} %get-tuple-element.59), calls=%async_computation.5 | async-start | bytes 65536 | tf_op jit(solution)/shard_map/all_to_all | solution.py:561
  98.3 2.0 %half.4 = bf16[1056,640]{1,0:T(8,128)(2,1)S(1)} custom-call(bf16[1056,640]{1,0:T(8,128)(2,1)S(1)} %get-tuple-element.61.dose, bf16[512,256]{1,0:T(8,128)(2,1)} %constant.20.clone.cols_far.refs_3_), custom_call_target="tpu_custom_call" | custom-call | flops 1730150400 | bytes 4055040 | tf_op jit(solution)/shard_map/half/pallas_call | solution.py:410
  100.3 2.7 %all-to-all-done.5.got = f32[8,8,128]{2,1,0:T(8,128)S(1)} async-done(((f32[8,8,128]{2,1,0:T(8,128)}), f32[8,8,128]{2,1,0:T(8,128)S(1)}, u32[]{:S(2)}, u32[]{:S(2)}) %all-to-all-start.5) | async-done | bytes 32800 | tf_op jit(solution)/shard_map/all_to_all | solution.py:561
  103.0 3.6 %step.3 = (bf16[1056,640]{1,0:T(8,128)(2,1)S(1)}, f32[32,8,128]{2,1,0:T(8,128)}, f32[32,128]{1,0:T(8,128)S(1)}) custom-call(f32[8,8,128]{2,1,0:T(8,128)S(1)} %all-to-all-done.5.got, f32[80,128]{1,0:T(8,128)S(1)} %get-tuple-element.60.part, f32[224,144]{1,0:T(8,128)S(1)} %get-tuple-element.42.matrix, ...), custom_call_target="tpu_custom_call", output_to_operand_aliasing={{0}: (5, {})} | custom-call | tf_op jit(solution)/shard_map/step/pallas_call | solution.py:505
  106.6 13.0 %all_to_all.42.got = f32[32,8,128]{2,1,0:T(8,128)S(1)} all-to-all(f32[32,8,128]{2,1,0:T(8,128)} %get-tuple-element.62), channel_id=1, replica_groups=mesh['gx'=32,'gy'=8] {'gx'}, dimensions={0} | all-to-all | bytes 262144 | tf_op jit(solution)/shard_map/all_to_all | solution.py:561
  120.6 5.3 %all-to-all-start.7 = ((f32[8,8,128]{2,1,0:T(8,128)}), f32[8,8,128]{2,1,0:T(8,128)S(1)}, u32[]{:S(2)}, u32[]{:S(2)}) async-start(f32[8,8,128]{2,1,0:T(8,128)} %get-tuple-element.64), calls=%async_computation.7 | async-start | bytes 65536 | tf_op jit(solution)/shard_map/all_to_all | solution.py:561
  125.9 1.7 %half.5 = bf16[1056,512]{1,0:T(8,128)(2,1)S(1)} custom-call(bf16[1056,640]{1,0:T(8,128)(2,1)S(1)} %get-tuple-element.66.dose, bf16[512,256]{1,0:T(8,128)(2,1)} %constant.20.clone.cols_far.refs_3_), custom_call_target="tpu_custom_call" | custom-call | flops 1730150400 | bytes 4055040 | tf_op jit(solution)/shard_map/half/pallas_call | solution.py:410
  127.6 3.0 %all-to-all-done.7.got = f32[8,8,128]{2,1,0:T(8,128)S(1)} async-done(((f32[8,8,128]{2,1,0:T(8,128)}), f32[8,8,128]{2,1,0:T(8,128)S(1)}, u32[]{:S(2)}, u32[]{:S(2)}) %all-to-all-start.7) | async-done | bytes 32800 | tf_op jit(solution)/shard_map/all_to_all | solution.py:561
  130.7 2.2 %finish.1 = f32[1024,512]{1,0:T(8,128)} custom-call(f32[8,8,128]{2,1,0:T(8,128)S(1)} %all-to-all-done.7.got, f32[80,128]{1,0:T(8,128)S(1)} %get-tuple-element.65.part, f32[224,144]{1,0:T(8,128)S(1)} %get-tuple-element.42.matrix, bf16[128,640]{1,0:T(8,128)(2,1)S(1)} %get-tuple-element.43.cols, bf16[1056,640]{1,0:T(8,128)(2,1)S(1)} %get-tuple-element.66.dose, ...), custom_call_target="tpu_custom_call" | custom-call | tf_op jit(solution)/shard_map/finish/pallas_call | solution.py:539
  (10 shorter events, 5.4 us)
Async XLA Ops:
  5.4 22.9 %all-to-all-start = ((f32[32,16,128]{2,1,0:T(8,128)}), f32[32,16,128]{2,1,0:T(8,128)S(1)}, u32[]{:S(2)}, u32[]{:S(2)}) async-start(f32[32,16,128]{2,1,0:T(8,128)} %get-tuple-element.36), calls=%async_computation | async-start | bytes 524288 | tf_op jit(solution)/shard_map/all_to_all | solution.py:561
  17.3 19.4 %collective-permute-start = (bf16[16,1024]{1,0:T(8,128)(2,1)S(1)}, bf16[16,1024]{1,0:T(8,128)(2,1)S(1)}, u32[]{:S(2)}, u32[]{:S(2)}) collective-permute-start(bf16[16,1024]{1,0:T(8,128)(2,1)S(1)} %get-tuple-element.46), channel_id=1, source_target_pairs={{0,8},{8,16},{16,24},{24,32},{32,40},{40,48},{48,56},{56,64},{64,7... | collective-permute-start | bytes 98312 | tf_op jit(solution)/shard_map/ppermute | solution.py:557
  20.4 16.2 %collective-permute-start.1 = (bf16[16,1024]{1,0:T(8,128)(2,1)S(1)}, bf16[16,1024]{1,0:T(8,128)(2,1)S(1)}, u32[]{:S(2)}, u32[]{:S(2)}) collective-permute-start(bf16[16,1024]{1,0:T(8,128)(2,1)S(1)} %get-tuple-element.47), channel_id=1, source_target_pairs={{8,0},{16,8},{24,16},{32,24},{40,32},{48,40},{56,48},{64,56},{72,6... | collective-permute-start | bytes 98312 | tf_op jit(solution)/shard_map/ppermute | solution.py:557
  21.7 18.0 %collective-permute-start.2 = (bf16[16,512]{1,0:T(8,128)(2,1)S(1)}, bf16[16,512]{1,0:T(8,128)(2,1)S(1)}, u32[]{:S(2)}, u32[]{:S(2)}) collective-permute-start(bf16[16,512]{1,0:T(8,128)(2,1)S(1)} %get-tuple-element.50), channel_id=1, source_target_pairs={{0,1},{1,2},{2,3},{3,4},{4,5},{5,6},{6,7},{8,9},{9,10},{10,11},{11... | collective-permute-start | bytes 49160 | tf_op jit(solution)/shard_map/ppermute | solution.py:557
  26.4 13.4 %collective-permute-start.3 = (bf16[16,512]{1,0:T(8,128)(2,1)S(1)}, bf16[16,512]{1,0:T(8,128)(2,1)S(1)}, u32[]{:S(2)}, u32[]{:S(2)}) collective-permute-start(bf16[16,512]{1,0:T(8,128)(2,1)S(1)} %get-tuple-element.51), channel_id=1, source_target_pairs={{1,0},{2,1},{3,2},{4,3},{5,4},{6,5},{7,6},{9,8},{10,9},{11,10},{12... | collective-permute-start | bytes 49160 | tf_op jit(solution)/shard_map/ppermute | solution.py:557
  29.4 12.3 %all-to-all-start.1 = ((f32[8,24,128]{2,1,0:T(8,128)}), f32[8,24,128]{2,1,0:T(8,128)S(1)}, u32[]{:S(2)}, u32[]{:S(2)}) async-start(f32[8,24,128]{2,1,0:T(8,128)} %get-tuple-element.40), calls=%async_computation.1 | async-start | bytes 196608 | tf_op jit(solution)/shard_map/all_to_all | solution.py:561
  65.1 10.2 %all-to-all-start.3 = ((f32[8,8,128]{2,1,0:T(8,128)}), f32[8,8,128]{2,1,0:T(8,128)S(1)}, u32[]{:S(2)}, u32[]{:S(2)}) async-start(f32[8,8,128]{2,1,0:T(8,128)} %get-tuple-element.54), calls=%async_computation.3 | async-start | bytes 65536 | tf_op jit(solution)/shard_map/all_to_all | solution.py:561
  93.0 10.0 %all-to-all-start.5 = ((f32[8,8,128]{2,1,0:T(8,128)}), f32[8,8,128]{2,1,0:T(8,128)S(1)}, u32[]{:S(2)}, u32[]{:S(2)}) async-start(f32[8,8,128]{2,1,0:T(8,128)} %get-tuple-element.59), calls=%async_computation.5 | async-start | bytes 65536 | tf_op jit(solution)/shard_map/all_to_all | solution.py:561
  120.6 10.0 %all-to-all-start.7 = ((f32[8,8,128]{2,1,0:T(8,128)}), f32[8,8,128]{2,1,0:T(8,128)S(1)}, u32[]{:S(2)}, u32[]{:S(2)}) async-start(f32[8,8,128]{2,1,0:T(8,128)} %get-tuple-element.64), calls=%async_computation.7 | async-start | bytes 65536 | tf_op jit(solution)/shard_map/all_to_all | solution.py:561

commit v6 on v5

--- a/solution.py
+++ b/solution.py
@@ -195,7 +195,7 @@
     cpool[...] = jnp.where((group == lane) & (col < TC), 1.0, 0.0).astype(BF16)
 
 
-def pooled_out(sums, row_pool_ref, px, send_ref, own_ref, corners=None):
+def pooled_out(sums, row_pool_ref, px, send_ref, own_ref):
     a, b, c = pieces(sums)
     rows = row_pool_ref[...]
     pooled = (dot(rows, a) + dot(rows, b) + dot(rows, c)).T
@@ -205,17 +205,7 @@
     left = jnp.where(lane < 64, pooled[0:8], coarse)
     right = jnp.where(lane < 64, pooled[24:32], coarse)
     for p in range(NX):
-        send_ref[p, :8] = jnp.where(p < px, left, right)
-        if corners is not None:
-            send_ref[p, 8:] = jnp.where(p < px, *corners)
-
-
-def corner(strip):
-    lane = lax.broadcasted_iota(jnp.int32, (8, 128), 1)
-    both = jnp.where(lane < 64, strip[:8, :128].astype(F32), strip[:8, TR - 128 :].astype(F32))
-    more = jnp.where(lane < 64, strip[8:, :128].astype(F32), strip[8:, TR - 128 :].astype(F32))
-    inner = jnp.where(lane < 64, pltpu.roll(more, 16, 1), pltpu.roll(more, 112, 1))
-    return jnp.where((lane < 16) | (lane >= 112), both, inner)
+        send_ref[p] = jnp.where(p < px, left, right)
 
 
 def start_kernel(table, exps, weights, classes, gain, *refs):
@@ -270,7 +260,7 @@
     for level in range(3):
         at = slice(QM * level, QM * (level + 1) if level < 2 else matrix.shape[0])
         matrix[at] = matrix[at] * weights[level]
-    pooled_out(sums[...], rpool, px, send, own, (corner(lo), corner(hi)))
+    pooled_out(sums[...], rpool, px, send, own)
 
 
 def start(table, exps, weights, classes, gain):
@@ -287,7 +277,7 @@
             pltpu.VMEM((HALO, TC), BF16),
             pltpu.VMEM((HALO, TR), BF16),
             pltpu.VMEM((HALO, TR), BF16),
-            pltpu.HBM((NX, 16, 128), F32),
+            pltpu.HBM((NX, 8, 128), F32),
             pltpu.VMEM((32, 128), F32),
             pltpu.VMEM(mgot.shape[1:], F32),
             pltpu.VMEM(mown.shape[1:], F32),
@@ -319,8 +309,12 @@
     return jnp.concatenate([strip_hi.astype(F32).T, empty, strip_lo.astype(F32).T], axis=1)
 
 
-def across_kernel(first, got, own, mgot, mown, send, part):
-    received = got[:, :8].reshape(NX * 8, 128)
+def across_kernel(first, *refs):
+    if first:
+        top, bottom, lo, hi, got, own, mgot, mown, send, part = refs
+    else:
+        _, got, own, mgot, mown, send, part = refs
+    received = got[...].reshape(NX * 8, 128)
     z = dot(mgot[...], received, precision=EXACT)
     mine = dot(mown[...], own[...], precision=EXACT)
     z = jnp.concatenate([z[:40] + mine, z[40:]], axis=0).T
@@ -329,29 +323,39 @@
     coarse = z[80:88]
     up = jnp.where(lane < 40, z[0:8], jnp.where(lane < 80, z[64:72], coarse))
     down = jnp.where(lane < 40, z[56:64], jnp.where(lane < 80, z[72:80], coarse))
-    px, py = lax.axis_index("gx"), lax.axis_index("gy")
+    py = lax.axis_index("gy")
+    if not first:
+        for p in range(NY):
+            send[p] = jnp.where(p < py, up, down)
+        return
+    above = side(lo[:, :128], hi[:, :128])[:HALO]
+    below = side(lo[:, TR - 128 :], hi[:, TR - 128 :])[128 - HALO :]
+    blocks = []
+    for strip, coarse_part, beside in ((top, up, above), (bottom, down, below)):
+        parts = [x.astype(F32) for x in pieces(coarse_part)] + [jnp.zeros((8, 128), F32)]
+        parts += [strip[:, 128 * n : 128 * n + 128].astype(F32) for n in range(TC // 128)] + [beside]
+        blocks.append(jnp.concatenate(parts, axis=0).astype(BF16))
     for p in range(NY):
-        send[p, :8] = jnp.where(p < py, up, down)
-    if first:
-        lo = jnp.where(px > 0, got[jnp.maximum(px - 1, 0), 8:], 0.0)
-        hi = jnp.where(px < NX - 1, got[jnp.minimum(px + 1, NX - 1), 8:], 0.0)
-        ends = []
-        for shift in (112, 16):
-            ends.append(side(*[jnp.concatenate([x, pltpu.roll(x, shift, 1)], axis=0) for x in (lo, hi)]))
-        for p in range(NY):
-            send[p, 8:] = jnp.where(p < py, ends[0][:HALO], ends[1][128 - HALO :])
-
-
-def across(first, got, own, mgot, mown):
-    count = 8 + HALO if first else 8
+
+        @pl.when(p < py)
+        def _():
+            send[p] = blocks[0]
+
+        @pl.when(p >= py)
+        def _():
+            send[p] = blocks[1]
+
+
+def across(first, extra, got, own, mgot, mown):
+    rows, kind = (32 + HALO * (EC // 128), BF16) if first else (8, F32)
     return pl.pallas_call(
         functools.partial(across_kernel, first),
-        in_specs=[VMEM] * 4,
+        in_specs=([VMEM] * 4 if first else [HBM]) + [VMEM] * 4,
         out_specs=[VMEM] * 2,
-        out_shape=[pltpu.VMEM((NY, count, 128), F32), pltpu.VMEM((80, 128), F32)],
+        out_shape=[pltpu.VMEM((NY, rows, 128), kind), pltpu.VMEM((80, 128), F32)],
         compiler_params=params(),
         name="across",
-    )(near(got), near(own), near(mgot), near(mown))
+    )(*[near(x) for x in extra], near(got), near(own), near(mgot), near(mown))
 
 
 def column_pass(block, cols, half, at):
@@ -390,7 +394,7 @@
         first_half_kernel,
         in_specs=[VMEM] * 3 + [HBM],
         out_specs=[HBM, VMEM],
-        out_shape=[pltpu.HBM((ER, EC), BF16), pltpu.VMEM((TR, EC - TC), BF16)],
+        out_shape=[pltpu.HBM((ER, EC), BF16), pltpu.HBM((TR, EC - TC), BF16)],
         scratch_shapes=[pltpu.VMEM((ER, EC), BF16), pltpu.VMEM((512, 256), BF16), DMA((TR // SB,)), DMA],
         compiler_params=params(),
         cost_estimate=half_cost(),
@@ -448,10 +452,11 @@
 
 def step_kernel(first, got, part, matrix, cols, rpool, dose, half, *refs):
     if first:
-        sides, above, below, fcols_far, out, send, own, rows, cpool, grid, sums, hbuf, fcols, lsem, fsem = refs
+        sides_far, fcols_far, out, send, own, rows, cpool, grid, sums, hbuf, sides, fcols, lsem, ssem, fsem = refs
         loads = [pltpu.make_async_copy(fcols_far, fcols, fsem)]
         at = pl.ds(HALO, TR)
         loads.append(pltpu.make_async_copy(half.at[at], hbuf.at[at], lsem))
+        loads.append(pltpu.make_async_copy(sides_far, sides, ssem))
         for copy in loads:
             copy.start()
     else:
@@ -460,17 +465,22 @@
     edge = {}
     fill_rows(rows)
     fill_pool(cpool)
-    received = got[:, :8].reshape(NY * 8, 128)
+    if first:
+        parts = got[:, :32].astype(F32)
+        received = parts[:, :8] + (parts[:, 8:16] + parts[:, 16:24])
+    else:
+        received = got[...]
+    received = received.reshape(NY * 8, 128)
     grid[...] = spread(received, part, matrix, cols[...])
     if first:
         py = lax.axis_index("gy")
         loads[0].wait()
-        for row, strip, p, real in (
-            (0, above, jnp.maximum(py - 1, 0), py > 0),
-            (ER - HALO, below, jnp.minimum(py + 1, NY - 1), py < NY - 1),
+        for row, p, real in (
+            (0, jnp.maximum(py - 1, 0), py > 0),
+            (ER - HALO, jnp.minimum(py + 1, NY - 1), py < NY - 1),
         ):
-            beside = jnp.where(real, got[p, 8:], 0.0).astype(BF16)
-            values = jnp.concatenate([strip[...], beside], axis=1)
+            tiles = [got[p, 32 + HALO * n : 32 + HALO * (n + 1)].astype(F32) for n in range(EC // 128)]
+            values = jnp.where(real, jnp.concatenate(tiles, axis=1), 0.0).astype(BF16)
             edge[row] = values
             column_pass(values, fcols, hbuf, slice(row, row + HALO))
         for copy in loads[1:]:
@@ -492,8 +502,8 @@
     pooled_out(sums[...], rpool, lax.axis_index("gx"), send, own)
 
 
-def step(got, part, dose, half, ops, strips=None):
-    first = strips is not None
+def step(got, part, dose, half, ops, sides=None):
+    first = sides is not None
     scratch = [
         pltpu.VMEM((3, BLK, BLK + 32), BF16),
         pltpu.VMEM((EC, 128), BF16),
@@ -501,10 +511,11 @@
         pltpu.VMEM((NB * 16, 128), F32),
     ]
     if first:
-        scratch += [pltpu.VMEM((ER, EC), BF16), pltpu.VMEM((512, 256), BF16), DMA, DMA]
+        scratch += [pltpu.VMEM((ER, EC), BF16), pltpu.VMEM((TR, EC - TC), BF16), pltpu.VMEM((512, 256), BF16)]
+        scratch += [DMA] * 3
     return pl.pallas_call(
         functools.partial(step_kernel, first),
-        in_specs=[VMEM] * 6 + ([HBM] + [VMEM] * 3 + [HBM] if first else [VMEM]),
+        in_specs=[VMEM] * 6 + ([HBM] * 3 if first else [VMEM]),
         out_specs=[VMEM] * 3,
         out_shape=[
             pltpu.VMEM((ER, EC), BF16),
@@ -517,7 +528,7 @@
         name="first_step" if first else "step",
     )(
         near(got), near(part), *[near(x) for x in ops], near(dose), far(half) if first else near(half),
-        *([*[near(x) for x in strips], far(jnp.asarray(fine_columns()))] if first else []),
+        *([far(sides), far(jnp.asarray(fine_columns()))] if first else []),
     )
 
 
@@ -566,16 +577,15 @@
         level_table, exponents, level_weights, classes, gain_field
     )
     left, right = shifted(hi, "gx", 1), shifted(lo, "gx", -1)
-    above, below = shifted(bottom, "gy", 1), shifted(top, "gy", -1)
     got = exchanged(send, "gx")
-    send, part = across(True, got, own, mgot, mown)
+    send, part = across(True, (top, bottom, left, right), got, own, mgot, mown)
     got = exchanged(send, "gy")
     half, sides = first_half(tile, left, right)
-    dose, send, own = step(got, part, tile, half, ops, (sides, above, below))
+    dose, send, own = step(got, part, tile, half, ops, sides)
     for sweep in range(2, ITERS + 1):
         got = exchanged(send, "gx")
         half = half_of(dose, EC if sweep < ITERS else TC)
-        send, part = across(False, got, own, mgot, mown)
+        send, part = across(False, (half,), got, own, mgot, mown)
         got = exchanged(send, "gy")
         if sweep < ITERS:
             dose, send, own = step(got, part, dose, half, ops)

time: 134 us -> 128 us (0.955)
  waiting for transfers between devices: 10.4 us -> 28.8 us
  blocking collectives: 44.4 us -> 27.8 us
  starting transfers between devices: 46.2 us -> 39.5 us
    all_to_all x3, blocking collectives: 44.4 us -> 27.8 us  [exchanged(): return lax.all_to_all(x, axis, 0, 0, tiled=True)]
    all_to_all x5, waiting for transfers between devices: 10.4 us -> 25.1 us  [exchanged(): return lax.all_to_all(x, axis, 0, 0, tiled=True)]
    ppermute x4 -> x2, starting transfers between devices: 11 us -> 4.43 us  [shifted(): lax.ppermute(x, axis, [(i, i + by) for i in range(n) if 0 <= i + by < n])]
    ppermute x4 -> x2, waiting for transfers between devices: 0.01 us -> 3.65 us  [shifted(): lax.ppermute(x, axis, [(i, i + by) for i in range(n) if 0 <= i + by < n])]
    pallas_call x4, Pallas kernels: 4.06 us -> 2.27 us  [across(): pl.pallas_call(functools.partial(across_kernel, first), in_specs=([VMEM]...]
  transfers between devices with their start and end apart: 9 -> 7, of which waited for: 4 -> 6; matrix products, arithmetic and copies ran while one was open for 0% -> 0% of each run, Pallas kernels for 7% -> 7%
where the time goes in v6:
time: 128 us; the launch traced here: 127 us
  starting transfers between devices  39.5 us (31%)
  Pallas kernels  30.5 us (24%)
  waiting for transfers between devices  28.8 us (22%)
  blocking collectives  27.8 us (22%)
    all_to_all x5, starting transfers between devices, exchanged(): return lax.all_to_all(x, axis, 0, 0, tiled=True)  35.1 us
    all_to_all x3, blocking collectives, exchanged(): return lax.all_to_all(x, axis, 0, 0, tiled=True)  27.8 us
    all_to_all x5, waiting for transfers between devices, exchanged(): return lax.all_to_all(x, axis, 0, 0, tiled=True)  25.1 us
    pallas_call x3, Pallas kernels, step(): pl.pallas_call(functools.partial(step_kernel, first), in_specs=[VMEM] * 6...  11.2 us
    pallas_call x3, Pallas kernels, half_of(): pl.pallas_call(half_kernel, in_specs=[VMEM, HBM], out_specs=VMEM, out_sha...  5.66 us
    pallas_call x1, Pallas kernels, start(): pl.pallas_call(start_kernel, in_specs=[SMEM, SMEM, SMEM] + [HBM] * 8, out...  5.35 us
    ppermute x2, starting transfers between devices, shifted(): lax.ppermute(x, axis, [(i, i + by) for i in range(n) if 0 <= i + by < n])  4.43 us
    pallas_call x1, Pallas kernels, first_half(): pl.pallas_call(first_half_kernel, in_specs=[VMEM] * 3 + [HBM], out_specs=...  3.73 us
  transfers between devices with their start and end apart: 7, of which 6 were waited for; matrix products, arithmetic and copies ran while one was open for 0% of the time, Pallas kernels for 7%

profile of v6, /device:TPU:1, one launch (start us, length us, event | category | flops | bytes accessed | tf_op | source)
XLA Modules:
  0.0 126.9 jit_solution(5203777596354486302)
XLA Ops:
  0.0 5.4 %start.1 = (bf16[1024,512]{1,0:T(8,128)(2,1)S(1)}, bf16[16,512]{1,0:T(8,128)(2,1)S(1)}, bf16[16,512]{1,0:T(8,128)(2,1)S(1)}, bf16[16,1024]{1,0:T(8,128)(2,1)S(1)...) custom-call(f32[8]{0:T(128)} %table.1, ...), custom_call_target="tpu_custom_call" | custom-call | tf_op jit(solution)/shard_map/start/pallas_call | solution.py:270
  5.4 11.9 %all-to-all-start = ((f32[32,8,128]{2,1,0:T(8,128)}), f32[32,8,128]{2,1,0:T(8,128)S(1)}, u32[]{:S(2)}, u32[]{:S(2)}) async-start(f32[32,8,128]{2,1,0:T(8,128)} %get-tuple-element.40), calls=%async_computation | async-start | bytes 262144 | tf_op jit(solution)/shard_map/all_to_all | solution.py:572
  17.2 3.1 %collective-permute-start = (bf16[16,1024]{1,0:T(8,128)(2,1)S(1)}, bf16[16,1024]{1,0:T(8,128)(2,1)S(1)}, u32[]{:S(2)}, u32[]{:S(2)}) collective-permute-start(bf16[16,1024]{1,0:T(8,128)(2,1)S(1)} %get-tuple-element.38), channel_id=1, source_target_pairs={{0,8},{8,16},{16,24},{24,32},{32,40},{40,48},{48,56},{56,64},{64,7... | collective-permute-start | bytes 98312 | tf_op jit(solution)/shard_map/ppermute | solution.py:568
  20.4 1.3 %collective-permute-start.1 = (bf16[16,1024]{1,0:T(8,128)(2,1)S(1)}, bf16[16,1024]{1,0:T(8,128)(2,1)S(1)}, u32[]{:S(2)}, u32[]{:S(2)}) collective-permute-start(bf16[16,1024]{1,0:T(8,128)(2,1)S(1)} %get-tuple-element.39), channel_id=1, source_target_pairs={{8,0},{16,8},{24,16},{32,24},{40,32},{48,40},{56,48},{64,56},{72,6... | collective-permute-start | bytes 98312 | tf_op jit(solution)/shard_map/ppermute | solution.py:568
  21.7 3.6 %collective-permute-done.1.refs_3_.hi = bf16[16,1024]{1,0:T(8,128)(2,1)S(1)} collective-permute-done((bf16[16,1024]{1,0:T(8,128)(2,1)S(1)}, bf16[16,1024]{1,0:T(8,128)(2,1)S(1)}, u32[]{:S(2)}, u32[]{:S(2)}) %collective-permute-start.1) | collective-permute-done | bytes 32800 | tf_op jit(solution)/shard_map/ppermute | solution.py:568
  27.6 6.8 %all-to-all-start.1 = ((bf16[8,112,128]{2,1,0:T(8,128)(2,1)}), bf16[8,112,128]{2,1,0:T(8,128)(2,1)S(1)}, u32[]{:S(2)}, u32[]{:S(2)}) async-start(bf16[8,112,128]{2,1,0:T(8,128)(2,1)} %get-tuple-element.44), calls=%async_computation.1 | async-start | bytes 458752 | tf_op jit(solution)/shard_map/all_to_all | solution.py:572
  34.3 3.7 %first_half.1 = (bf16[1056,640]{1,0:T(8,128)(2,1)}, bf16[1024,128]{1,0:T(8,128)(2,1)}) custom-call(bf16[1024,512]{1,0:T(8,128)(2,1)S(1)} %get-tuple-element.49.tile.dose, bf16[16,1024]{1,0:T(8,128)(2,1)S(1)} %collective-permute-done.refs_2_.lo, bf16[16,1024]{1,0:T(8,128)(2,1)S(1)} %collective-permute-done.1.refs_3_.hi, ...), custom_call_target="tpu_custom_call" | custom-call | flops 1730150400 | bytes 4055040 | tf_op jit(solution)/shard_map/first_half/pallas_call | solution.py:393
  38.1 2.5 %all-to-all-done.1.got = bf16[8,112,128]{2,1,0:T(8,128)(2,1)S(1)} async-done(((bf16[8,112,128]{2,1,0:T(8,128)(2,1)}), bf16[8,112,128]{2,1,0:T(8,128)(2,1)S(1)}, u32[]{:S(2)}, u32[]{:S(2)}) %all-to-all-start.1) | async-done | bytes 229408 | tf_op jit(solution)/shard_map/all_to_all | solution.py:572
  40.5 4.0 %first_step.1 = (bf16[1056,640]{1,0:T(8,128)(2,1)S(1)}, f32[32,8,128]{2,1,0:T(8,128)}, f32[32,128]{1,0:T(8,128)S(1)}) custom-call(bf16[8,112,128]{2,1,0:T(8,128)(2,1)S(1)} %all-to-all-done.1.got, f32[80,128]{1,0:T(8,128)S(1)} %get-tuple-element.45.part, f32[224,144]{1,0:T(8,128)S(1)} %get-tuple-element.46.matrix, ...), custom_call_target="tpu_custom_call" | custom-call | tf_op jit(solution)/shard_map/first_step/pallas_call | solution.py:516
  44.6 8.5 %all-to-all-start.2 = ((f32[32,8,128]{2,1,0:T(8,128)}), f32[32,8,128]{2,1,0:T(8,128)S(1)}, u32[]{:S(2)}, u32[]{:S(2)}) async-start(f32[32,8,128]{2,1,0:T(8,128)} %get-tuple-element.53), calls=%async_computation.2 | async-start | bytes 262144 | tf_op jit(solution)/shard_map/all_to_all | solution.py:572
  53.1 2.0 %half.3.refs_0_ = bf16[1056,640]{1,0:T(8,128)(2,1)S(1)} custom-call(bf16[1056,640]{1,0:T(8,128)(2,1)S(1)} %get-tuple-element.52.dose, bf16[512,256]{1,0:T(8,128)(2,1)} %constant.20.clone.cols_far.refs_1_), custom_call_target="tpu_custom_call" | custom-call | flops 1730150400 | bytes 4055040 | tf_op jit(solution)/shard_map/half/pallas_call | solution.py:414
  55.1 7.2 %all-to-all-done.2.refs_1_ = f32[32,8,128]{2,1,0:T(8,128)S(1)} async-done(((f32[32,8,128]{2,1,0:T(8,128)}), f32[32,8,128]{2,1,0:T(8,128)S(1)}, u32[]{:S(2)}, u32[]{:S(2)}) %all-to-all-start.2) | async-done | bytes 131104 | tf_op jit(solution)/shard_map/all_to_all | solution.py:572
  62.6 9.6 %all_to_all.40.got = f32[8,8,128]{2,1,0:T(8,128)S(1)} all-to-all(f32[8,8,128]{2,1,0:T(8,128)S(1)} %get-tuple-element.55), channel_id=1, replica_groups=mesh['gx'=32,'gy'=8] {'gy'}, dimensions={0} | all-to-all | bytes 65536 | tf_op jit(solution)/shard_map/all_to_all | solution.py:572
  72.2 3.6 %step.2 = (bf16[1056,640]{1,0:T(8,128)(2,1)S(1)}, f32[32,8,128]{2,1,0:T(8,128)}, f32[32,128]{1,0:T(8,128)S(1)}) custom-call(f32[8,8,128]{2,1,0:T(8,128)S(1)} %all_to_all.40.got, f32[80,128]{1,0:T(8,128)S(1)} %get-tuple-element.56.part, f32[224,144]{1,0:T(8,128)S(1)} %get-tuple-element.46.matrix, ...), custom_call_target="tpu_custom_call", output_to_operand_aliasing={{0}: (5, {})} | custom-call | tf_op jit(solution)/shard_map/step/pallas_call | solution.py:516
  75.8 4.0 %all-to-all-start.4 = ((f32[32,8,128]{2,1,0:T(8,128)}), f32[32,8,128]{2,1,0:T(8,128)S(1)}, u32[]{:S(2)}, u32[]{:S(2)}) async-start(f32[32,8,128]{2,1,0:T(8,128)} %get-tuple-element.58), calls=%async_computation.4 | async-start | bytes 262144 | tf_op jit(solution)/shard_map/all_to_all | solution.py:572
  79.8 2.0 %half.4.refs_0_ = bf16[1056,640]{1,0:T(8,128)(2,1)S(1)} custom-call(bf16[1056,640]{1,0:T(8,128)(2,1)S(1)} %get-tuple-element.57.dose, bf16[512,256]{1,0:T(8,128)(2,1)} %constant.20.clone.cols_far.refs_1_), custom_call_target="tpu_custom_call" | custom-call | flops 1730150400 | bytes 4055040 | tf_op jit(solution)/shard_map/half/pallas_call | solution.py:414
  81.8 7.0 %all-to-all-done.4.refs_1_ = f32[32,8,128]{2,1,0:T(8,128)S(1)} async-done(((f32[32,8,128]{2,1,0:T(8,128)}), f32[32,8,128]{2,1,0:T(8,128)S(1)}, u32[]{:S(2)}, u32[]{:S(2)}) %all-to-all-start.4) | async-done | bytes 131104 | tf_op jit(solution)/shard_map/all_to_all | solution.py:572
  89.2 9.1 %all_to_all.41.got = f32[8,8,128]{2,1,0:T(8,128)S(1)} all-to-all(f32[8,8,128]{2,1,0:T(8,128)S(1)} %get-tuple-element.60), channel_id=1, replica_groups=mesh['gx'=32,'gy'=8] {'gy'}, dimensions={0} | all-to-all | bytes 65536 | tf_op jit(solution)/shard_map/all_to_all | solution.py:572
  98.3 3.6 %step.3 = (bf16[1056,640]{1,0:T(8,128)(2,1)S(1)}, f32[32,8,128]{2,1,0:T(8,128)}, f32[32,128]{1,0:T(8,128)S(1)}) custom-call(f32[8,8,128]{2,1,0:T(8,128)S(1)} %all_to_all.41.got, f32[80,128]{1,0:T(8,128)S(1)} %get-tuple-element.61.part, f32[224,144]{1,0:T(8,128)S(1)} %get-tuple-element.46.matrix, ...), custom_call_target="tpu_custom_call", output_to_operand_aliasing={{0}: (5, {})} | custom-call | tf_op jit(solution)/shard_map/step/pallas_call | solution.py:516
  101.9 3.9 %all-to-all-start.6 = ((f32[32,8,128]{2,1,0:T(8,128)}), f32[32,8,128]{2,1,0:T(8,128)S(1)}, u32[]{:S(2)}, u32[]{:S(2)}) async-start(f32[32,8,128]{2,1,0:T(8,128)} %get-tuple-element.63), calls=%async_computation.6 | async-start | bytes 262144 | tf_op jit(solution)/shard_map/all_to_all | solution.py:572
  105.8 1.7 %half.5.refs_0_ = bf16[1056,512]{1,0:T(8,128)(2,1)S(1)} custom-call(bf16[1056,640]{1,0:T(8,128)(2,1)S(1)} %get-tuple-element.62.dose, bf16[512,256]{1,0:T(8,128)(2,1)} %constant.20.clone.cols_far.refs_1_), custom_call_target="tpu_custom_call" | custom-call | flops 1730150400 | bytes 4055040 | tf_op jit(solution)/shard_map/half/pallas_call | solution.py:414
  107.5 7.5 %all-to-all-done.6.refs_1_ = f32[32,8,128]{2,1,0:T(8,128)S(1)} async-done(((f32[32,8,128]{2,1,0:T(8,128)}), f32[32,8,128]{2,1,0:T(8,128)S(1)}, u32[]{:S(2)}, u32[]{:S(2)}) %all-to-all-start.6) | async-done | bytes 131104 | tf_op jit(solution)/shard_map/all_to_all | solution.py:572
  115.3 9.1 %all_to_all.42.got = f32[8,8,128]{2,1,0:T(8,128)S(1)} all-to-all(f32[8,8,128]{2,1,0:T(8,128)S(1)} %get-tuple-element.65), channel_id=1, replica_groups=mesh['gx'=32,'gy'=8] {'gy'}, dimensions={0} | all-to-all | bytes 65536 | tf_op jit(solution)/shard_map/all_to_all | solution.py:572
  124.5 2.2 %finish.1 = f32[1024,512]{1,0:T(8,128)} custom-call(f32[8,8,128]{2,1,0:T(8,128)S(1)} %all_to_all.42.got, f32[80,128]{1,0:T(8,128)S(1)} %get-tuple-element.66.part, f32[224,144]{1,0:T(8,128)S(1)} %get-tuple-element.46.matrix, bf16[128,640]{1,0:T(8,128)(2,1)S(1)} %get-tuple-element.47.cols, bf16[1056,640]{1,0:T(8,128)(2,1)S(1)} %get-tuple-element.62.dose, ...), custom_call_target="tpu_custom_call" | custom-call | tf_op jit(solution)/shard_map/finish/pallas_call | solution.py:550
  (6 shorter events, 3.3 us)
Async XLA Ops:
  5.4 21.0 %all-to-all-start = ((f32[32,8,128]{2,1,0:T(8,128)}), f32[32,8,128]{2,1,0:T(8,128)S(1)}, u32[]{:S(2)}, u32[]{:S(2)}) async-start(f32[32,8,128]{2,1,0:T(8,128)} %get-tuple-element.40), calls=%async_computation | async-start | bytes 262144 | tf_op jit(solution)/shard_map/all_to_all | solution.py:572
  17.2 4.4 %collective-permute-start = (bf16[16,1024]{1,0:T(8,128)(2,1)S(1)}, bf16[16,1024]{1,0:T(8,128)(2,1)S(1)}, u32[]{:S(2)}, u32[]{:S(2)}) collective-permute-start(bf16[16,1024]{1,0:T(8,128)(2,1)S(1)} %get-tuple-element.38), channel_id=1, source_target_pairs={{0,8},{8,16},{16,24},{24,32},{32,40},{40,48},{48,56},{56,64},{64,7... | collective-permute-start | bytes 98312 | tf_op jit(solution)/shard_map/ppermute | solution.py:568
  20.4 5.0 %collective-permute-start.1 = (bf16[16,1024]{1,0:T(8,128)(2,1)S(1)}, bf16[16,1024]{1,0:T(8,128)(2,1)S(1)}, u32[]{:S(2)}, u32[]{:S(2)}) collective-permute-start(bf16[16,1024]{1,0:T(8,128)(2,1)S(1)} %get-tuple-element.39), channel_id=1, source_target_pairs={{8,0},{16,8},{24,16},{32,24},{40,32},{48,40},{56,48},{64,56},{72,6... | collective-permute-start | bytes 98312 | tf_op jit(solution)/shard_map/ppermute | solution.py:568
  27.6 13.0 %all-to-all-start.1 = ((bf16[8,112,128]{2,1,0:T(8,128)(2,1)}), bf16[8,112,128]{2,1,0:T(8,128)(2,1)S(1)}, u32[]{:S(2)}, u32[]{:S(2)}) async-start(bf16[8,112,128]{2,1,0:T(8,128)(2,1)} %get-tuple-element.44), calls=%async_computation.1 | async-start | bytes 458752 | tf_op jit(solution)/shard_map/all_to_all | solution.py:572
  44.6 17.7 %all-to-all-start.2 = ((f32[32,8,128]{2,1,0:T(8,128)}), f32[32,8,128]{2,1,0:T(8,128)S(1)}, u32[]{:S(2)}, u32[]{:S(2)}) async-start(f32[32,8,128]{2,1,0:T(8,128)} %get-tuple-element.53), calls=%async_computation.2 | async-start | bytes 262144 | tf_op jit(solution)/shard_map/all_to_all | solution.py:572
  75.8 13.0 %all-to-all-start.4 = ((f32[32,8,128]{2,1,0:T(8,128)}), f32[32,8,128]{2,1,0:T(8,128)S(1)}, u32[]{:S(2)}, u32[]{:S(2)}) async-start(f32[32,8,128]{2,1,0:T(8,128)} %get-tuple-element.58), calls=%async_computation.4 | async-start | bytes 262144 | tf_op jit(solution)/shard_map/all_to_all | solution.py:572
  101.9 13.0 %all-to-all-start.6 = ((f32[32,8,128]{2,1,0:T(8,128)}), f32[32,8,128]{2,1,0:T(8,128)S(1)}, u32[]{:S(2)}, u32[]{:S(2)}) async-start(f32[32,8,128]{2,1,0:T(8,128)} %get-tuple-element.63), calls=%async_computation.6 | async-start | bytes 262144 | tf_op jit(solution)/shard_map/all_to_all | solution.py:572

commit v7 on v6

--- a/solution.py
+++ b/solution.py
@@ -18,6 +18,7 @@
 HALO = HW * ITERS
 ER = TR + 2 * HALO
 EC = TC + 128
+PAD = 16
 BLK = 176
 NB = ER // BLK
 QC, QR = 36, 68
@@ -179,13 +180,16 @@
 
 
 def fill_rows(rows):
-    shape = (BLK, BLK + 32)
-    shift = lax.broadcasted_iota(jnp.int32, shape, 1) - lax.broadcasted_iota(jnp.int32, shape, 0)
-    for which in range(3):
-        band = jnp.zeros(shape, F32)
-        for k in range(-HW, HW + 1):
-            band = jnp.where(shift == 16 * which + k, float(fine_taps()[k + HW]), band)
-        rows[which] = band.astype(BF16)
+    shift = lax.broadcasted_iota(jnp.int32, rows.shape, 1) - lax.broadcasted_iota(jnp.int32, rows.shape, 0)
+    band = jnp.zeros(rows.shape, F32)
+    for k in range(-HW, HW + 1):
+        band = jnp.where(shift == PAD + k, float(fine_taps()[k + HW]), band)
+    rows[...] = band.astype(BF16)
+
+
+def fill_pads(half):
+    for at in (slice(0, PAD), slice(PAD + ER, PAD + ER + PAD)):
+        half[at] = jnp.zeros((PAD, half.shape[1]), BF16)
 
 
 def fill_pool(cpool):
@@ -208,12 +212,18 @@
         send_ref[p] = jnp.where(p < px, left, right)
 
 
-def start_kernel(table, exps, weights, classes, gain, *refs):
+def start_kernel(table_far, exps_far, weights_far, classes, gain, *refs):
     fars, refs = refs[:6], refs[6:]
     dose, top, bottom, lo, hi, send, own, mgot, mown, matrix, spread_near, rpool_later = refs[:12]
-    cbuf, gbuf, cpool, rpool, sums, csem, gsem, tsem = refs[12:]
+    cbuf, gbuf, cpool, rpool, sums, table, exps, weights, csem, gsem, tsem, ssem = refs[12:]
     steps = TR // SB
     px, py = lax.axis_index("gx"), lax.axis_index("gy")
+    scalars = [
+        pltpu.make_async_copy(source, to, ssem.at[i])
+        for i, (source, to) in enumerate(((table_far, table), (exps_far, exps), (weights_far, weights)))
+    ]
+    for copy in scalars:
+        copy.start()
     loads = []
     for i in range(steps):
         rows = pl.ds(i * SB, SB)
@@ -233,6 +243,8 @@
         tables.append(pltpu.make_async_copy(source, nears[i], tsem.at[i]))
         tables[-1].start()
     fill_pool(cpool)
+    for copy in scalars:
+        copy.wait()
     for i in range(steps):
         for copy in loads[i]:
             copy.wait()
@@ -269,7 +281,7 @@
     rows, cols, rpool = row_matrices(), column_spread(), row_pool(NB, 16, BLK // 16, 1)
     return pl.pallas_call(
         start_kernel,
-        in_specs=[SMEM, SMEM, SMEM] + [HBM] * 8,
+        in_specs=[HBM] * 11,
         out_specs=[VMEM] * 12,
         out_shape=[
             pltpu.VMEM((TR, TC), BF16),
@@ -291,9 +303,13 @@
             pltpu.VMEM((TC, 128), BF16),
             pltpu.VMEM((128, TR // 16), BF16),
             pltpu.VMEM((TR // 16, 128), F32),
+            pltpu.SMEM((CLASSES,), F32),
+            pltpu.SMEM((TC // SB, TR // SB), jnp.int32),
+            pltpu.SMEM((3,), F32),
             DMA((steps,)),
             DMA((steps,)),
             DMA((6,)),
+            DMA((3,)),
         ],
         compiler_params=params(),
         name="start",
@@ -377,8 +393,8 @@
         sides[rows] = beside
         if n == 0:
             load.wait()
-        column_pass(jnp.concatenate([tile[rows], beside], axis=1), cols, half, slice(begin, begin + SB))
-        at = pl.ds(begin, SB)
+        column_pass(jnp.concatenate([tile[rows], beside], axis=1), cols, half, slice(PAD + begin, PAD + begin + SB))
+        at = pl.ds(PAD + begin, SB)
         stores.append(pltpu.make_async_copy(half.at[at], half_far.at[at], sems.at[n]))
         stores[-1].start()
     for copy in stores:
@@ -394,8 +410,8 @@
         first_half_kernel,
         in_specs=[VMEM] * 3 + [HBM],
         out_specs=[HBM, VMEM],
-        out_shape=[pltpu.HBM((ER, EC), BF16), pltpu.HBM((TR, EC - TC), BF16)],
-        scratch_shapes=[pltpu.VMEM((ER, EC), BF16), pltpu.VMEM((512, 256), BF16), DMA((TR // SB,)), DMA],
+        out_shape=[pltpu.HBM((ER + 2 * PAD, EC), BF16), pltpu.HBM((TR, EC - TC), BF16)],
+        scratch_shapes=[pltpu.VMEM((ER + 2 * PAD, EC), BF16), pltpu.VMEM((512, 256), BF16), DMA((TR // SB,)), DMA],
         compiler_params=params(),
         cost_estimate=half_cost(),
         name="first_half",
@@ -405,9 +421,10 @@
 def half_kernel(dose, cols_far, half, cols, csem):
     load = pltpu.make_async_copy(cols_far, cols, csem)
     load.start()
+    fill_pads(half)
     load.wait()
     for b in range(NB):
-        column_pass(dose[b * BLK : (b + 1) * BLK], cols, half, slice(b * BLK, (b + 1) * BLK))
+        column_pass(dose[b * BLK : (b + 1) * BLK], cols, half, slice(PAD + b * BLK, PAD + (b + 1) * BLK))
 
 
 def half_of(dose, lanes):
@@ -415,7 +432,7 @@
         half_kernel,
         in_specs=[VMEM, HBM],
         out_specs=VMEM,
-        out_shape=pltpu.VMEM((ER, lanes), BF16),
+        out_shape=pltpu.VMEM((ER + 2 * PAD, lanes), BF16),
         scratch_shapes=[pltpu.VMEM((512, 256), BF16), DMA],
         compiler_params=params(),
         cost_estimate=half_cost(),
@@ -432,8 +449,7 @@
 
 
 def short_range(b, rows, half):
-    begin = min(max(b * BLK - 16, 0), ER - BLK - 32)
-    return dot(rows[(b * BLK - begin) // 16], half[begin : begin + BLK + 32])
+    return dot(rows[...], half[b * BLK : (b + 1) * BLK + 2 * PAD])
 
 
 def update(b, old_rows, short, grid, out, skip):
@@ -454,7 +470,7 @@
     if first:
         sides_far, fcols_far, out, send, own, rows, cpool, grid, sums, hbuf, sides, fcols, lsem, ssem, fsem = refs
         loads = [pltpu.make_async_copy(fcols_far, fcols, fsem)]
-        at = pl.ds(HALO, TR)
+        at = pl.ds(PAD + HALO, TR)
         loads.append(pltpu.make_async_copy(half.at[at], hbuf.at[at], lsem))
         loads.append(pltpu.make_async_copy(sides_far, sides, ssem))
         for copy in loads:
@@ -474,6 +490,7 @@
     grid[...] = spread(received, part, matrix, cols[...])
     if first:
         py = lax.axis_index("gy")
+        fill_pads(hbuf)
         loads[0].wait()
         for row, p, real in (
             (0, jnp.maximum(py - 1, 0), py > 0),
@@ -482,7 +499,7 @@
             tiles = [got[p, 32 + HALO * n : 32 + HALO * (n + 1)].astype(F32) for n in range(EC // 128)]
             values = jnp.where(real, jnp.concatenate(tiles, axis=1), 0.0).astype(BF16)
             edge[row] = values
-            column_pass(values, fcols, hbuf, slice(row, row + HALO))
+            column_pass(values, fcols, hbuf, slice(PAD + row, PAD + row + HALO))
         for copy in loads[1:]:
             copy.wait()
 
@@ -496,7 +513,7 @@
 
     for b in range(NB):
         update(b, old_rows, short_range(b, rows, hbuf), grid, out, 0)
-        pooled = dot(out[b * BLK : (b + 1) * BLK], cpool[...])
+        pooled = dot(out[b * BLK : (b + 1) * BLK, :TC], cpool[...])
         pooled = jnp.sum(pooled.reshape(BLK // 16, 16, 128), axis=1)
         sums[16 * b : 16 * b + 16] = jnp.concatenate([pooled, jnp.zeros((16 - BLK // 16, 128), F32)], axis=0)
     pooled_out(sums[...], rpool, lax.axis_index("gx"), send, own)
@@ -505,13 +522,13 @@
 def step(got, part, dose, half, ops, sides=None):
     first = sides is not None
     scratch = [
-        pltpu.VMEM((3, BLK, BLK + 32), BF16),
-        pltpu.VMEM((EC, 128), BF16),
+        pltpu.VMEM((BLK, BLK + 2 * PAD), BF16),
+        pltpu.VMEM((TC, 128), BF16),
         pltpu.VMEM((QM, EC), F32),
         pltpu.VMEM((NB * 16, 128), F32),
     ]
     if first:
-        scratch += [pltpu.VMEM((ER, EC), BF16), pltpu.VMEM((TR, EC - TC), BF16), pltpu.VMEM((512, 256), BF16)]
+        scratch += [pltpu.VMEM((ER + 2 * PAD, EC), BF16), pltpu.VMEM((TR, EC - TC), BF16), pltpu.VMEM((512, 256), BF16)]
         scratch += [DMA] * 3
     return pl.pallas_call(
         functools.partial(step_kernel, first),
@@ -553,7 +570,7 @@
         out_specs=HBM,
         out_shape=pltpu.HBM((TR, TC), F32),
         scratch_shapes=[
-            pltpu.VMEM((3, BLK, BLK + 32), BF16),
+            pltpu.VMEM((BLK, BLK + 2 * PAD), BF16),
             pltpu.VMEM((TR, TC), F32),
             pltpu.VMEM((QM, TC), F32),
             DMA((NB,)),

time: 128 us -> 127 us (level)
  no operation moved by 1% of the time
where the time goes in v7:
time: 127 us; the launch traced here: 126 us
  starting transfers between devices  39.5 us (31%)
  Pallas kernels  29.6 us (23%)
  waiting for transfers between devices  28.8 us (23%)
  blocking collectives  27.8 us (22%)
    all_to_all x5, starting transfers between devices, exchanged(): return lax.all_to_all(x, axis, 0, 0, tiled=True)  35.1 us
    all_to_all x3, blocking collectives, exchanged(): return lax.all_to_all(x, axis, 0, 0, tiled=True)  27.8 us
    all_to_all x5, waiting for transfers between devices, exchanged(): return lax.all_to_all(x, axis, 0, 0, tiled=True)  25.1 us
    pallas_call x3, Pallas kernels, step(): pl.pallas_call(functools.partial(step_kernel, first), in_specs=[VMEM] * 6...  11 us
    pallas_call x3, Pallas kernels, half_of(): pl.pallas_call(half_kernel, in_specs=[VMEM, HBM], out_specs=VMEM, out_sha...  5.66 us
    pallas_call x1, Pallas kernels, start(): pl.pallas_call(start_kernel, in_specs=[HBM] * 11, out_specs=[VMEM] * 12,...  4.68 us
    ppermute x2, starting transfers between devices, shifted(): lax.ppermute(x, axis, [(i, i + by) for i in range(n) if 0 <= i + by < n])  4.43 us
    pallas_call x1, Pallas kernels, first_half(): pl.pallas_call(first_half_kernel, in_specs=[VMEM] * 3 + [HBM], out_specs=...  3.73 us
  transfers between devices with their start and end apart: 7, of which 6 were waited for; matrix products, arithmetic and copies ran while one was open for 0% of the time, Pallas kernels for 7%

profile of v7, /device:TPU:1, one launch (start us, length us, event | category | flops | bytes accessed | tf_op | source)
XLA Modules:
  0.0 126.0 jit_solution(3218504827274390136)
XLA Ops:
  0.0 4.7 %start.1 = (bf16[1024,512]{1,0:T(8,128)(2,1)S(1)}, bf16[16,512]{1,0:T(8,128)(2,1)S(1)}, bf16[16,512]{1,0:T(8,128)(2,1)S(1)}, bf16[16,1024]{1,0:T(8,128)(2,1)S(1)...) custom-call(f32[8]{0:T(128)} %table_far.1, ...), custom_call_target="tpu_custom_call" | custom-call | tf_op jit(solution)/shard_map/start/pallas_call | solution.py:282
  4.7 11.9 %all-to-all-start = ((f32[32,8,128]{2,1,0:T(8,128)}), f32[32,8,128]{2,1,0:T(8,128)S(1)}, u32[]{:S(2)}, u32[]{:S(2)}) async-start(f32[32,8,128]{2,1,0:T(8,128)} %get-tuple-element.40), calls=%async_computation | async-start | bytes 262144 | tf_op jit(solution)/shard_map/all_to_all | solution.py:589
  16.6 3.1 %collective-permute-start = (bf16[16,1024]{1,0:T(8,128)(2,1)S(1)}, bf16[16,1024]{1,0:T(8,128)(2,1)S(1)}, u32[]{:S(2)}, u32[]{:S(2)}) collective-permute-start(bf16[16,1024]{1,0:T(8,128)(2,1)S(1)} %get-tuple-element.38), channel_id=1, source_target_pairs={{0,8},{8,16},{16,24},{24,32},{32,40},{40,48},{48,56},{56,64},{64,7... | collective-permute-start | bytes 98312 | tf_op jit(solution)/shard_map/ppermute | solution.py:585
  19.7 1.3 %collective-permute-start.1 = (bf16[16,1024]{1,0:T(8,128)(2,1)S(1)}, bf16[16,1024]{1,0:T(8,128)(2,1)S(1)}, u32[]{:S(2)}, u32[]{:S(2)}) collective-permute-start(bf16[16,1024]{1,0:T(8,128)(2,1)S(1)} %get-tuple-element.39), channel_id=1, source_target_pairs={{8,0},{16,8},{24,16},{32,24},{40,32},{48,40},{56,48},{64,56},{72,6... | collective-permute-start | bytes 98312 | tf_op jit(solution)/shard_map/ppermute | solution.py:585
  21.0 3.6 %collective-permute-done.1.refs_3_.hi = bf16[16,1024]{1,0:T(8,128)(2,1)S(1)} collective-permute-done((bf16[16,1024]{1,0:T(8,128)(2,1)S(1)}, bf16[16,1024]{1,0:T(8,128)(2,1)S(1)}, u32[]{:S(2)}, u32[]{:S(2)}) %collective-permute-start.1) | collective-permute-done | bytes 32800 | tf_op jit(solution)/shard_map/ppermute | solution.py:585
  26.9 6.8 %all-to-all-start.1 = ((bf16[8,112,128]{2,1,0:T(8,128)(2,1)}), bf16[8,112,128]{2,1,0:T(8,128)(2,1)S(1)}, u32[]{:S(2)}, u32[]{:S(2)}) async-start(bf16[8,112,128]{2,1,0:T(8,128)(2,1)} %get-tuple-element.44), calls=%async_computation.1 | async-start | bytes 458752 | tf_op jit(solution)/shard_map/all_to_all | solution.py:589
  33.7 3.7 %first_half.1 = (bf16[1088,640]{1,0:T(8,128)(2,1)}, bf16[1024,128]{1,0:T(8,128)(2,1)}) custom-call(bf16[1024,512]{1,0:T(8,128)(2,1)S(1)} %get-tuple-element.49.tile.dose, bf16[16,1024]{1,0:T(8,128)(2,1)S(1)} %collective-permute-done.refs_2_.lo, bf16[16,1024]{1,0:T(8,128)(2,1)S(1)} %collective-permute-done.1.refs_3_.hi, ...), custom_call_target="tpu_custom_call" | custom-call | flops 1730150400 | bytes 4055040 | tf_op jit(solution)/shard_map/first_half/pallas_call | solution.py:409
  37.4 2.5 %all-to-all-done.1.got = bf16[8,112,128]{2,1,0:T(8,128)(2,1)S(1)} async-done(((bf16[8,112,128]{2,1,0:T(8,128)(2,1)}), bf16[8,112,128]{2,1,0:T(8,128)(2,1)S(1)}, u32[]{:S(2)}, u32[]{:S(2)}) %all-to-all-start.1) | async-done | bytes 229408 | tf_op jit(solution)/shard_map/all_to_all | solution.py:589
  39.9 4.2 %first_step.1 = (bf16[1056,640]{1,0:T(8,128)(2,1)S(1)}, f32[32,8,128]{2,1,0:T(8,128)}, f32[32,128]{1,0:T(8,128)S(1)}) custom-call(bf16[8,112,128]{2,1,0:T(8,128)(2,1)S(1)} %all-to-all-done.1.got, f32[80,128]{1,0:T(8,128)S(1)} %get-tuple-element.45.part, f32[224,144]{1,0:T(8,128)S(1)} %get-tuple-element.46.matrix, ...), custom_call_target="tpu_custom_call" | custom-call | tf_op jit(solution)/shard_map/first_step/pallas_call | solution.py:533
  44.1 8.5 %all-to-all-start.2 = ((f32[32,8,128]{2,1,0:T(8,128)}), f32[32,8,128]{2,1,0:T(8,128)S(1)}, u32[]{:S(2)}, u32[]{:S(2)}) async-start(f32[32,8,128]{2,1,0:T(8,128)} %get-tuple-element.53), calls=%async_computation.2 | async-start | bytes 262144 | tf_op jit(solution)/shard_map/all_to_all | solution.py:589
  52.6 2.0 %half.3.refs_0_ = bf16[1088,640]{1,0:T(8,128)(2,1)S(1)} custom-call(bf16[1056,640]{1,0:T(8,128)(2,1)S(1)} %get-tuple-element.52.dose, bf16[512,256]{1,0:T(8,128)(2,1)} %constant.20.clone.cols_far.refs_1_), custom_call_target="tpu_custom_call" | custom-call | flops 1730150400 | bytes 4055040 | tf_op jit(solution)/shard_map/half/pallas_call | solution.py:431
  54.6 7.2 %all-to-all-done.2.refs_1_ = f32[32,8,128]{2,1,0:T(8,128)S(1)} async-done(((f32[32,8,128]{2,1,0:T(8,128)}), f32[32,8,128]{2,1,0:T(8,128)S(1)}, u32[]{:S(2)}, u32[]{:S(2)}) %all-to-all-start.2) | async-done | bytes 131104 | tf_op jit(solution)/shard_map/all_to_all | solution.py:589
  62.2 9.6 %all_to_all.40.got = f32[8,8,128]{2,1,0:T(8,128)S(1)} all-to-all(f32[8,8,128]{2,1,0:T(8,128)S(1)} %get-tuple-element.55), channel_id=1, replica_groups=mesh['gx'=32,'gy'=8] {'gy'}, dimensions={0} | all-to-all | bytes 65536 | tf_op jit(solution)/shard_map/all_to_all | solution.py:589
  71.7 3.4 %step.2 = (bf16[1056,640]{1,0:T(8,128)(2,1)S(1)}, f32[32,8,128]{2,1,0:T(8,128)}, f32[32,128]{1,0:T(8,128)S(1)}) custom-call(f32[8,8,128]{2,1,0:T(8,128)S(1)} %all_to_all.40.got, f32[80,128]{1,0:T(8,128)S(1)} %get-tuple-element.56.part, f32[224,144]{1,0:T(8,128)S(1)} %get-tuple-element.46.matrix, ...), custom_call_target="tpu_custom_call", output_to_operand_aliasing={{0}: (5, {})} | custom-call | tf_op jit(solution)/shard_map/step/pallas_call | solution.py:533
  75.1 4.0 %all-to-all-start.4 = ((f32[32,8,128]{2,1,0:T(8,128)}), f32[32,8,128]{2,1,0:T(8,128)S(1)}, u32[]{:S(2)}, u32[]{:S(2)}) async-start(f32[32,8,128]{2,1,0:T(8,128)} %get-tuple-element.58), calls=%async_computation.4 | async-start | bytes 262144 | tf_op jit(solution)/shard_map/all_to_all | solution.py:589
  79.2 2.0 %half.4.refs_0_ = bf16[1088,640]{1,0:T(8,128)(2,1)S(1)} custom-call(bf16[1056,640]{1,0:T(8,128)(2,1)S(1)} %get-tuple-element.57.dose, bf16[512,256]{1,0:T(8,128)(2,1)} %constant.20.clone.cols_far.refs_1_), custom_call_target="tpu_custom_call" | custom-call | flops 1730150400 | bytes 4055040 | tf_op jit(solution)/shard_map/half/pallas_call | solution.py:431
  81.2 7.0 %all-to-all-done.4.refs_1_ = f32[32,8,128]{2,1,0:T(8,128)S(1)} async-done(((f32[32,8,128]{2,1,0:T(8,128)}), f32[32,8,128]{2,1,0:T(8,128)S(1)}, u32[]{:S(2)}, u32[]{:S(2)}) %all-to-all-start.4) | async-done | bytes 131104 | tf_op jit(solution)/shard_map/all_to_all | solution.py:589
  88.5 9.1 %all_to_all.41.got = f32[8,8,128]{2,1,0:T(8,128)S(1)} all-to-all(f32[8,8,128]{2,1,0:T(8,128)S(1)} %get-tuple-element.60), channel_id=1, replica_groups=mesh['gx'=32,'gy'=8] {'gy'}, dimensions={0} | all-to-all | bytes 65536 | tf_op jit(solution)/shard_map/all_to_all | solution.py:589
  97.7 3.4 %step.3 = (bf16[1056,640]{1,0:T(8,128)(2,1)S(1)}, f32[32,8,128]{2,1,0:T(8,128)}, f32[32,128]{1,0:T(8,128)S(1)}) custom-call(f32[8,8,128]{2,1,0:T(8,128)S(1)} %all_to_all.41.got, f32[80,128]{1,0:T(8,128)S(1)} %get-tuple-element.61.part, f32[224,144]{1,0:T(8,128)S(1)} %get-tuple-element.46.matrix, ...), custom_call_target="tpu_custom_call", output_to_operand_aliasing={{0}: (5, {})} | custom-call | tf_op jit(solution)/shard_map/step/pallas_call | solution.py:533
  101.1 3.9 %all-to-all-start.6 = ((f32[32,8,128]{2,1,0:T(8,128)}), f32[32,8,128]{2,1,0:T(8,128)S(1)}, u32[]{:S(2)}, u32[]{:S(2)}) async-start(f32[32,8,128]{2,1,0:T(8,128)} %get-tuple-element.63), calls=%async_computation.6 | async-start | bytes 262144 | tf_op jit(solution)/shard_map/all_to_all | solution.py:589
  104.9 1.7 %half.5.refs_0_ = bf16[1088,512]{1,0:T(8,128)(2,1)S(1)} custom-call(bf16[1056,640]{1,0:T(8,128)(2,1)S(1)} %get-tuple-element.62.dose, bf16[512,256]{1,0:T(8,128)(2,1)} %constant.20.clone.cols_far.refs_1_), custom_call_target="tpu_custom_call" | custom-call | flops 1730150400 | bytes 4055040 | tf_op jit(solution)/shard_map/half/pallas_call | solution.py:431
  106.7 7.5 %all-to-all-done.6.refs_1_ = f32[32,8,128]{2,1,0:T(8,128)S(1)} async-done(((f32[32,8,128]{2,1,0:T(8,128)}), f32[32,8,128]{2,1,0:T(8,128)S(1)}, u32[]{:S(2)}, u32[]{:S(2)}) %all-to-all-start.6) | async-done | bytes 131104 | tf_op jit(solution)/shard_map/all_to_all | solution.py:589
  114.5 9.1 %all_to_all.42.got = f32[8,8,128]{2,1,0:T(8,128)S(1)} all-to-all(f32[8,8,128]{2,1,0:T(8,128)S(1)} %get-tuple-element.65), channel_id=1, replica_groups=mesh['gx'=32,'gy'=8] {'gy'}, dimensions={0} | all-to-all | bytes 65536 | tf_op jit(solution)/shard_map/all_to_all | solution.py:589
  123.6 2.2 %finish.1 = f32[1024,512]{1,0:T(8,128)} custom-call(f32[8,8,128]{2,1,0:T(8,128)S(1)} %all_to_all.42.got, f32[80,128]{1,0:T(8,128)S(1)} %get-tuple-element.66.part, f32[224,144]{1,0:T(8,128)S(1)} %get-tuple-element.46.matrix, bf16[128,640]{1,0:T(8,128)(2,1)S(1)} %get-tuple-element.47.cols, bf16[1056,640]{1,0:T(8,128)(2,1)S(1)} %get-tuple-element.62.dose, ...), custom_call_target="tpu_custom_call" | custom-call | tf_op jit(solution)/shard_map/finish/pallas_call | solution.py:567
  (6 shorter events, 3.3 us)
Async XLA Ops:
  4.7 21.0 %all-to-all-start = ((f32[32,8,128]{2,1,0:T(8,128)}), f32[32,8,128]{2,1,0:T(8,128)S(1)}, u32[]{:S(2)}, u32[]{:S(2)}) async-start(f32[32,8,128]{2,1,0:T(8,128)} %get-tuple-element.40), calls=%async_computation | async-start | bytes 262144 | tf_op jit(solution)/shard_map/all_to_all | solution.py:589
  16.6 4.4 %collective-permute-start = (bf16[16,1024]{1,0:T(8,128)(2,1)S(1)}, bf16[16,1024]{1,0:T(8,128)(2,1)S(1)}, u32[]{:S(2)}, u32[]{:S(2)}) collective-permute-start(bf16[16,1024]{1,0:T(8,128)(2,1)S(1)} %get-tuple-element.38), channel_id=1, source_target_pairs={{0,8},{8,16},{16,24},{24,32},{32,40},{40,48},{48,56},{56,64},{64,7... | collective-permute-start | bytes 98312 | tf_op jit(solution)/shard_map/ppermute | solution.py:585
  19.7 5.0 %collective-permute-start.1 = (bf16[16,1024]{1,0:T(8,128)(2,1)S(1)}, bf16[16,1024]{1,0:T(8,128)(2,1)S(1)}, u32[]{:S(2)}, u32[]{:S(2)}) collective-permute-start(bf16[16,1024]{1,0:T(8,128)(2,1)S(1)} %get-tuple-element.39), channel_id=1, source_target_pairs={{8,0},{16,8},{24,16},{32,24},{40,32},{48,40},{56,48},{64,56},{72,6... | collective-permute-start | bytes 98312 | tf_op jit(solution)/shard_map/ppermute | solution.py:585
  26.9 13.0 %all-to-all-start.1 = ((bf16[8,112,128]{2,1,0:T(8,128)(2,1)}), bf16[8,112,128]{2,1,0:T(8,128)(2,1)S(1)}, u32[]{:S(2)}, u32[]{:S(2)}) async-start(bf16[8,112,128]{2,1,0:T(8,128)(2,1)} %get-tuple-element.44), calls=%async_computation.1 | async-start | bytes 458752 | tf_op jit(solution)/shard_map/all_to_all | solution.py:589
  44.1 17.7 %all-to-all-start.2 = ((f32[32,8,128]{2,1,0:T(8,128)}), f32[32,8,128]{2,1,0:T(8,128)S(1)}, u32[]{:S(2)}, u32[]{:S(2)}) async-start(f32[32,8,128]{2,1,0:T(8,128)} %get-tuple-element.53), calls=%async_computation.2 | async-start | bytes 262144 | tf_op jit(solution)/shard_map/all_to_all | solution.py:589
  75.1 13.0 %all-to-all-start.4 = ((f32[32,8,128]{2,1,0:T(8,128)}), f32[32,8,128]{2,1,0:T(8,128)S(1)}, u32[]{:S(2)}, u32[]{:S(2)}) async-start(f32[32,8,128]{2,1,0:T(8,128)} %get-tuple-element.58), calls=%async_computation.4 | async-start | bytes 262144 | tf_op jit(solution)/shard_map/all_to_all | solution.py:589
  101.1 13.0 %all-to-all-start.6 = ((f32[32,8,128]{2,1,0:T(8,128)}), f32[32,8,128]{2,1,0:T(8,128)S(1)}, u32[]{:S(2)}, u32[]{:S(2)}) async-start(f32[32,8,128]{2,1,0:T(8,128)} %get-tuple-element.63), calls=%async_computation.6 | async-start | bytes 262144 | tf_op jit(solution)/shard_map/all_to_all | solution.py:589

commit v8 on v7

--- a/solution.py
+++ b/solution.py
@@ -245,6 +245,11 @@
     fill_pool(cpool)
     for copy in scalars:
         copy.wait()
+
+    def pool(i):
+        across = dot(dose[i * SB : (i + 1) * SB], cpool[...])
+        sums[8 * i : 8 * i + 8] = jnp.sum(across.reshape(8, 16, 128), axis=1)
+
     for i in range(steps):
         for copy in loads[i]:
             copy.wait()
@@ -263,8 +268,9 @@
                 lo[:, rows] = value.astype(F32).T[:HALO].astype(BF16)
             if k == TC // SB - 1:
                 hi[:, rows] = value.astype(F32).T[SB - HALO :].astype(BF16)
-        across = dot(dose[rows], cpool[...])
-        sums[8 * i : 8 * i + 8] = jnp.sum(across.reshape(8, 16, 128), axis=1)
+        if i > 0:
+            pool(i - 1)
+    pool(steps - 1)
     top[...] = dose[:HALO]
     bottom[...] = dose[TR - HALO :]
     for copy in tables:

time: 127 us -> 126 us (level)
  no operation moved by 1% of the time
where the time goes in v8:
time: 126 us; the launch traced here: 125 us
  starting transfers between devices  39.5 us (31%)
  Pallas kernels  29 us (23%)
  waiting for transfers between devices  28.8 us (23%)
  blocking collectives  27.8 us (22%)
    all_to_all x5, starting transfers between devices, exchanged(): return lax.all_to_all(x, axis, 0, 0, tiled=True)  35.1 us
    all_to_all x3, blocking collectives, exchanged(): return lax.all_to_all(x, axis, 0, 0, tiled=True)  27.8 us
    all_to_all x5, waiting for transfers between devices, exchanged(): return lax.all_to_all(x, axis, 0, 0, tiled=True)  25.1 us
    pallas_call x3, Pallas kernels, step(): pl.pallas_call(functools.partial(step_kernel, first), in_specs=[VMEM] * 6...  11 us
    pallas_call x3, Pallas kernels, half_of(): pl.pallas_call(half_kernel, in_specs=[VMEM, HBM], out_specs=VMEM, out_sha...  5.66 us
    ppermute x2, starting transfers between devices, shifted(): lax.ppermute(x, axis, [(i, i + by) for i in range(n) if 0 <= i + by < n])  4.43 us
    pallas_call x1, Pallas kernels, start(): pl.pallas_call(start_kernel, in_specs=[HBM] * 11, out_specs=[VMEM] * 12,...  4.08 us
    pallas_call x1, Pallas kernels, first_half(): pl.pallas_call(first_half_kernel, in_specs=[VMEM] * 3 + [HBM], out_specs=...  3.74 us
  transfers between devices with their start and end apart: 7, of which 6 were waited for; matrix products, arithmetic and copies ran while one was open for 0% of the time, Pallas kernels for 7%

profile of v8, /device:TPU:1, one launch (start us, length us, event | category | flops | bytes accessed | tf_op | source)
XLA Modules:
  0.0 125.4 jit_solution(13686381768836593054)
XLA Ops:
  0.0 4.1 %start.1 = (bf16[1024,512]{1,0:T(8,128)(2,1)S(1)}, bf16[16,512]{1,0:T(8,128)(2,1)S(1)}, bf16[16,512]{1,0:T(8,128)(2,1)S(1)}, bf16[16,1024]{1,0:T(8,128)(2,1)S(1)...) custom-call(f32[8]{0:T(128)} %table_far.1, ...), custom_call_target="tpu_custom_call" | custom-call | tf_op jit(solution)/shard_map/start/pallas_call | solution.py:288
  4.1 11.9 %all-to-all-start = ((f32[32,8,128]{2,1,0:T(8,128)}), f32[32,8,128]{2,1,0:T(8,128)S(1)}, u32[]{:S(2)}, u32[]{:S(2)}) async-start(f32[32,8,128]{2,1,0:T(8,128)} %get-tuple-element.40), calls=%async_computation | async-start | bytes 262144 | tf_op jit(solution)/shard_map/all_to_all | solution.py:595
  16.0 3.1 %collective-permute-start = (bf16[16,1024]{1,0:T(8,128)(2,1)S(1)}, bf16[16,1024]{1,0:T(8,128)(2,1)S(1)}, u32[]{:S(2)}, u32[]{:S(2)}) collective-permute-start(bf16[16,1024]{1,0:T(8,128)(2,1)S(1)} %get-tuple-element.38), channel_id=1, source_target_pairs={{0,8},{8,16},{16,24},{24,32},{32,40},{40,48},{48,56},{56,64},{64,7... | collective-permute-start | bytes 98312 | tf_op jit(solution)/shard_map/ppermute | solution.py:591
  19.1 1.3 %collective-permute-start.1 = (bf16[16,1024]{1,0:T(8,128)(2,1)S(1)}, bf16[16,1024]{1,0:T(8,128)(2,1)S(1)}, u32[]{:S(2)}, u32[]{:S(2)}) collective-permute-start(bf16[16,1024]{1,0:T(8,128)(2,1)S(1)} %get-tuple-element.39), channel_id=1, source_target_pairs={{8,0},{16,8},{24,16},{32,24},{40,32},{48,40},{56,48},{64,56},{72,6... | collective-permute-start | bytes 98312 | tf_op jit(solution)/shard_map/ppermute | solution.py:591
  20.4 3.6 %collective-permute-done.1.refs_3_.hi = bf16[16,1024]{1,0:T(8,128)(2,1)S(1)} collective-permute-done((bf16[16,1024]{1,0:T(8,128)(2,1)S(1)}, bf16[16,1024]{1,0:T(8,128)(2,1)S(1)}, u32[]{:S(2)}, u32[]{:S(2)}) %collective-permute-start.1) | collective-permute-done | bytes 32800 | tf_op jit(solution)/shard_map/ppermute | solution.py:591
  26.3 6.8 %all-to-all-start.1 = ((bf16[8,112,128]{2,1,0:T(8,128)(2,1)}), bf16[8,112,128]{2,1,0:T(8,128)(2,1)S(1)}, u32[]{:S(2)}, u32[]{:S(2)}) async-start(bf16[8,112,128]{2,1,0:T(8,128)(2,1)} %get-tuple-element.44), calls=%async_computation.1 | async-start | bytes 458752 | tf_op jit(solution)/shard_map/all_to_all | solution.py:595
  33.1 3.7 %first_half.1 = (bf16[1088,640]{1,0:T(8,128)(2,1)}, bf16[1024,128]{1,0:T(8,128)(2,1)}) custom-call(bf16[1024,512]{1,0:T(8,128)(2,1)S(1)} %get-tuple-element.49.tile.dose, bf16[16,1024]{1,0:T(8,128)(2,1)S(1)} %collective-permute-done.refs_2_.lo, bf16[16,1024]{1,0:T(8,128)(2,1)S(1)} %collective-permute-done.1.refs_3_.hi, ...), custom_call_target="tpu_custom_call" | custom-call | flops 1730150400 | bytes 4055040 | tf_op jit(solution)/shard_map/first_half/pallas_call | solution.py:415
  36.8 2.4 %all-to-all-done.1.got = bf16[8,112,128]{2,1,0:T(8,128)(2,1)S(1)} async-done(((bf16[8,112,128]{2,1,0:T(8,128)(2,1)}), bf16[8,112,128]{2,1,0:T(8,128)(2,1)S(1)}, u32[]{:S(2)}, u32[]{:S(2)}) %all-to-all-start.1) | async-done | bytes 229408 | tf_op jit(solution)/shard_map/all_to_all | solution.py:595
  39.3 4.2 %first_step.1 = (bf16[1056,640]{1,0:T(8,128)(2,1)S(1)}, f32[32,8,128]{2,1,0:T(8,128)}, f32[32,128]{1,0:T(8,128)S(1)}) custom-call(bf16[8,112,128]{2,1,0:T(8,128)(2,1)S(1)} %all-to-all-done.1.got, f32[80,128]{1,0:T(8,128)S(1)} %get-tuple-element.45.part, f32[224,144]{1,0:T(8,128)S(1)} %get-tuple-element.46.matrix, ...), custom_call_target="tpu_custom_call" | custom-call | tf_op jit(solution)/shard_map/first_step/pallas_call | solution.py:539
  43.5 8.5 %all-to-all-start.2 = ((f32[32,8,128]{2,1,0:T(8,128)}), f32[32,8,128]{2,1,0:T(8,128)S(1)}, u32[]{:S(2)}, u32[]{:S(2)}) async-start(f32[32,8,128]{2,1,0:T(8,128)} %get-tuple-element.53), calls=%async_computation.2 | async-start | bytes 262144 | tf_op jit(solution)/shard_map/all_to_all | solution.py:595
  52.0 2.0 %half.3.refs_0_ = bf16[1088,640]{1,0:T(8,128)(2,1)S(1)} custom-call(bf16[1056,640]{1,0:T(8,128)(2,1)S(1)} %get-tuple-element.52.dose, bf16[512,256]{1,0:T(8,128)(2,1)} %constant.20.clone.cols_far.refs_1_), custom_call_target="tpu_custom_call" | custom-call | flops 1730150400 | bytes 4055040 | tf_op jit(solution)/shard_map/half/pallas_call | solution.py:437
  54.0 7.2 %all-to-all-done.2.refs_1_ = f32[32,8,128]{2,1,0:T(8,128)S(1)} async-done(((f32[32,8,128]{2,1,0:T(8,128)}), f32[32,8,128]{2,1,0:T(8,128)S(1)}, u32[]{:S(2)}, u32[]{:S(2)}) %all-to-all-start.2) | async-done | bytes 131104 | tf_op jit(solution)/shard_map/all_to_all | solution.py:595
  61.6 9.5 %all_to_all.40.got = f32[8,8,128]{2,1,0:T(8,128)S(1)} all-to-all(f32[8,8,128]{2,1,0:T(8,128)S(1)} %get-tuple-element.55), channel_id=1, replica_groups=mesh['gx'=32,'gy'=8] {'gy'}, dimensions={0} | all-to-all | bytes 65536 | tf_op jit(solution)/shard_map/all_to_all | solution.py:595
  71.1 3.4 %step.2 = (bf16[1056,640]{1,0:T(8,128)(2,1)S(1)}, f32[32,8,128]{2,1,0:T(8,128)}, f32[32,128]{1,0:T(8,128)S(1)}) custom-call(f32[8,8,128]{2,1,0:T(8,128)S(1)} %all_to_all.40.got, f32[80,128]{1,0:T(8,128)S(1)} %get-tuple-element.56.part, f32[224,144]{1,0:T(8,128)S(1)} %get-tuple-element.46.matrix, ...), custom_call_target="tpu_custom_call", output_to_operand_aliasing={{0}: (5, {})} | custom-call | tf_op jit(solution)/shard_map/step/pallas_call | solution.py:539
  74.5 4.0 %all-to-all-start.4 = ((f32[32,8,128]{2,1,0:T(8,128)}), f32[32,8,128]{2,1,0:T(8,128)S(1)}, u32[]{:S(2)}, u32[]{:S(2)}) async-start(f32[32,8,128]{2,1,0:T(8,128)} %get-tuple-element.58), calls=%async_computation.4 | async-start | bytes 262144 | tf_op jit(solution)/shard_map/all_to_all | solution.py:595
  78.6 2.0 %half.4.refs_0_ = bf16[1088,640]{1,0:T(8,128)(2,1)S(1)} custom-call(bf16[1056,640]{1,0:T(8,128)(2,1)S(1)} %get-tuple-element.57.dose, bf16[512,256]{1,0:T(8,128)(2,1)} %constant.20.clone.cols_far.refs_1_), custom_call_target="tpu_custom_call" | custom-call | flops 1730150400 | bytes 4055040 | tf_op jit(solution)/shard_map/half/pallas_call | solution.py:437
  80.6 7.0 %all-to-all-done.4.refs_1_ = f32[32,8,128]{2,1,0:T(8,128)S(1)} async-done(((f32[32,8,128]{2,1,0:T(8,128)}), f32[32,8,128]{2,1,0:T(8,128)S(1)}, u32[]{:S(2)}, u32[]{:S(2)}) %all-to-all-start.4) | async-done | bytes 131104 | tf_op jit(solution)/shard_map/all_to_all | solution.py:595
  87.9 9.1 %all_to_all.41.got = f32[8,8,128]{2,1,0:T(8,128)S(1)} all-to-all(f32[8,8,128]{2,1,0:T(8,128)S(1)} %get-tuple-element.60), channel_id=1, replica_groups=mesh['gx'=32,'gy'=8] {'gy'}, dimensions={0} | all-to-all | bytes 65536 | tf_op jit(solution)/shard_map/all_to_all | solution.py:595
  97.1 3.4 %step.3 = (bf16[1056,640]{1,0:T(8,128)(2,1)S(1)}, f32[32,8,128]{2,1,0:T(8,128)}, f32[32,128]{1,0:T(8,128)S(1)}) custom-call(f32[8,8,128]{2,1,0:T(8,128)S(1)} %all_to_all.41.got, f32[80,128]{1,0:T(8,128)S(1)} %get-tuple-element.61.part, f32[224,144]{1,0:T(8,128)S(1)} %get-tuple-element.46.matrix, ...), custom_call_target="tpu_custom_call", output_to_operand_aliasing={{0}: (5, {})} | custom-call | tf_op jit(solution)/shard_map/step/pallas_call | solution.py:539
  100.5 3.9 %all-to-all-start.6 = ((f32[32,8,128]{2,1,0:T(8,128)}), f32[32,8,128]{2,1,0:T(8,128)S(1)}, u32[]{:S(2)}, u32[]{:S(2)}) async-start(f32[32,8,128]{2,1,0:T(8,128)} %get-tuple-element.63), calls=%async_computation.6 | async-start | bytes 262144 | tf_op jit(solution)/shard_map/all_to_all | solution.py:595
  104.3 1.7 %half.5.refs_0_ = bf16[1088,512]{1,0:T(8,128)(2,1)S(1)} custom-call(bf16[1056,640]{1,0:T(8,128)(2,1)S(1)} %get-tuple-element.62.dose, bf16[512,256]{1,0:T(8,128)(2,1)} %constant.20.clone.cols_far.refs_1_), custom_call_target="tpu_custom_call" | custom-call | flops 1730150400 | bytes 4055040 | tf_op jit(solution)/shard_map/half/pallas_call | solution.py:437
  106.0 7.5 %all-to-all-done.6.refs_1_ = f32[32,8,128]{2,1,0:T(8,128)S(1)} async-done(((f32[32,8,128]{2,1,0:T(8,128)}), f32[32,8,128]{2,1,0:T(8,128)S(1)}, u32[]{:S(2)}, u32[]{:S(2)}) %all-to-all-start.6) | async-done | bytes 131104 | tf_op jit(solution)/shard_map/all_to_all | solution.py:595
  113.9 9.1 %all_to_all.42.got = f32[8,8,128]{2,1,0:T(8,128)S(1)} all-to-all(f32[8,8,128]{2,1,0:T(8,128)S(1)} %get-tuple-element.65), channel_id=1, replica_groups=mesh['gx'=32,'gy'=8] {'gy'}, dimensions={0} | all-to-all | bytes 65536 | tf_op jit(solution)/shard_map/all_to_all | solution.py:595
  123.0 2.2 %finish.1 = f32[1024,512]{1,0:T(8,128)} custom-call(f32[8,8,128]{2,1,0:T(8,128)S(1)} %all_to_all.42.got, f32[80,128]{1,0:T(8,128)S(1)} %get-tuple-element.66.part, f32[224,144]{1,0:T(8,128)S(1)} %get-tuple-element.46.matrix, bf16[128,640]{1,0:T(8,128)(2,1)S(1)} %get-tuple-element.47.cols, bf16[1056,640]{1,0:T(8,128)(2,1)S(1)} %get-tuple-element.62.dose, ...), custom_call_target="tpu_custom_call" | custom-call | tf_op jit(solution)/shard_map/finish/pallas_call | solution.py:573
  (6 shorter events, 3.3 us)
Async XLA Ops:
  4.1 21.0 %all-to-all-start = ((f32[32,8,128]{2,1,0:T(8,128)}), f32[32,8,128]{2,1,0:T(8,128)S(1)}, u32[]{:S(2)}, u32[]{:S(2)}) async-start(f32[32,8,128]{2,1,0:T(8,128)} %get-tuple-element.40), calls=%async_computation | async-start | bytes 262144 | tf_op jit(solution)/shard_map/all_to_all | solution.py:595
  16.0 4.4 %collective-permute-start = (bf16[16,1024]{1,0:T(8,128)(2,1)S(1)}, bf16[16,1024]{1,0:T(8,128)(2,1)S(1)}, u32[]{:S(2)}, u32[]{:S(2)}) collective-permute-start(bf16[16,1024]{1,0:T(8,128)(2,1)S(1)} %get-tuple-element.38), channel_id=1, source_target_pairs={{0,8},{8,16},{16,24},{24,32},{32,40},{40,48},{48,56},{56,64},{64,7... | collective-permute-start | bytes 98312 | tf_op jit(solution)/shard_map/ppermute | solution.py:591
  19.1 5.0 %collective-permute-start.1 = (bf16[16,1024]{1,0:T(8,128)(2,1)S(1)}, bf16[16,1024]{1,0:T(8,128)(2,1)S(1)}, u32[]{:S(2)}, u32[]{:S(2)}) collective-permute-start(bf16[16,1024]{1,0:T(8,128)(2,1)S(1)} %get-tuple-element.39), channel_id=1, source_target_pairs={{8,0},{16,8},{24,16},{32,24},{40,32},{48,40},{56,48},{64,56},{72,6... | collective-permute-start | bytes 98312 | tf_op jit(solution)/shard_map/ppermute | solution.py:591
  26.3 13.0 %all-to-all-start.1 = ((bf16[8,112,128]{2,1,0:T(8,128)(2,1)}), bf16[8,112,128]{2,1,0:T(8,128)(2,1)S(1)}, u32[]{:S(2)}, u32[]{:S(2)}) async-start(bf16[8,112,128]{2,1,0:T(8,128)(2,1)} %get-tuple-element.44), calls=%async_computation.1 | async-start | bytes 458752 | tf_op jit(solution)/shard_map/all_to_all | solution.py:595
  43.5 17.7 %all-to-all-start.2 = ((f32[32,8,128]{2,1,0:T(8,128)}), f32[32,8,128]{2,1,0:T(8,128)S(1)}, u32[]{:S(2)}, u32[]{:S(2)}) async-start(f32[32,8,128]{2,1,0:T(8,128)} %get-tuple-element.53), calls=%async_computation.2 | async-start | bytes 262144 | tf_op jit(solution)/shard_map/all_to_all | solution.py:595
  74.5 13.0 %all-to-all-start.4 = ((f32[32,8,128]{2,1,0:T(8,128)}), f32[32,8,128]{2,1,0:T(8,128)S(1)}, u32[]{:S(2)}, u32[]{:S(2)}) async-start(f32[32,8,128]{2,1,0:T(8,128)} %get-tuple-element.58), calls=%async_computation.4 | async-start | bytes 262144 | tf_op jit(solution)/shard_map/all_to_all | solution.py:595
  100.5 13.0 %all-to-all-start.6 = ((f32[32,8,128]{2,1,0:T(8,128)}), f32[32,8,128]{2,1,0:T(8,128)S(1)}, u32[]{:S(2)}, u32[]{:S(2)}) async-start(f32[32,8,128]{2,1,0:T(8,128)} %get-tuple-element.63), calls=%async_computation.6 | async-start | bytes 262144 | tf_op jit(solution)/shard_map/all_to_all | solution.py:595
